TPU v7x, 256 devices: a whole 4x4x8 slice. The times are simulated.
256 devices in a mesh: grp: 8 (over z), seq: 32 (over x, y, core).
Axes of the slice: x: 4, y: 4, z: 8, core: 2. Of those that a mesh axis runs over, the one named last changes fastest.
Arguments:
- q_proj: bfloat16 [4096, 32768], P(None, ('grp', 'seq')), may hold values from -8 to 8
- k_proj: bfloat16 [4096, 32768], P(None, ('grp', 'seq')), may hold values from -8 to 8
- v_proj: bfloat16 [4096, 32768], P(None, ('grp', 'seq')), may hold values from -6 to 6
- block_start: int32 [256], replicated, may hold values from 0 to 128, as said below
- kv_select: int32 [256, 3], P(('grp', 'seq')), may hold values from 0 to 1, as said below
- pre_gate: bfloat16 [4096, 32768], P(None, ('grp', 'seq')), may hold values from -6 to 6
- post_gate: bfloat16 [4096, 32768], P(None, ('grp', 'seq')), may hold values from -6 to 6
- long_filter: bfloat16 [4096, 32768], P(('grp', 'seq')), may hold values from -1.5 to 1.5
Outputs:
- attn_out: bfloat16 [4096, 32768], P(None, ('grp', 'seq'))
- mixed: bfloat16 [4096, 32768], P(None, ('grp', 'seq'))
Inputs may be any that keep to these rules, and one draw needn't show every extreme that they name: `block_start`: A record begins at that offset of the block; 128 means that none begins in it. At most one record begins in a block. `kv_select`: column j is 1 where the block reads the keys and values of the block j + 1 places before it. Only blocks at or after the start of the record of the block's first token are read, none before the first block, and the block itself begins no record at offset 0 where any flag is set. Some block reads all 3.
All inputs are finite; a program needn't handle non-finite values.
Results may differ from a plain program's by a relative error of at most 0.0065.
Values may be sent and summed in bfloat16 or wider, within the bound.
No kernel may reach another device: no remote copies, remote signals or barrier semaphores. Data moves between devices by JAX's collectives and lax.ppermute only.
A program may use at most 128 MiB of HBM per device.

v0:
```python
import math

import jax
import jax.numpy as jnp
import ml_dtypes
import numpy as np
from jax import lax
from jax.experimental import pallas as pl
from jax.experimental.pallas import tpu as pltpu
from jax.sharding import Mesh
from jax.sharding import PartitionSpec as P

HD = 128
ALL = ("z", "x", "y", "c")
MASKED = -1e30
VMEM_LIMIT = 48 * 1024 * 1024


def hi_lo(table):
    high = table.astype(ml_dtypes.bfloat16)
    low = (table - high.astype(np.float64)).astype(ml_dtypes.bfloat16)
    return (high, low)


def make_tables(rows, width):
    length = rows * width
    k1 = np.arange(rows)[:, None]
    n1 = np.arange(rows)[None, :]
    theta = 2.0 * np.pi * (((4 * k1 + 1) * n1) % (4 * rows)) / (4 * rows)
    n2 = np.arange(width)[None, :]
    turn = 2.0 * np.pi * (((4 * k1 + 1) * n2) % (4 * length)) / (4 * length)
    k2 = np.arange(width)[:, None]
    phi = 2.0 * np.pi * ((k2 * n2) % width) / width
    first = hi_lo(np.concatenate([np.cos(theta), -np.sin(theta)], axis=0))
    second = hi_lo(np.block([[np.cos(phi), -np.sin(phi)], [np.sin(phi), np.cos(phi)]]))
    second_back = hi_lo(np.block([[np.cos(phi), np.sin(phi)], [-np.sin(phi), np.cos(phi)]]))
    first_back = hi_lo(np.concatenate([np.cos(theta).T, -np.sin(theta).T], axis=1) / length)
    twist = (np.cos(turn).astype(np.float32), -np.sin(turn).astype(np.float32))
    return first, twist, second, second_back, first_back


def dot(left, right):
    return jnp.dot(left, right, preferred_element_type=jnp.float32)


def split(value):
    high = value.astype(jnp.bfloat16)
    low = (value - high.astype(jnp.float32)).astype(jnp.bfloat16)
    return high, low


def forward(signal, first_h, first_l, cosine, sine, second_h, second_l):
    rows = signal.shape[0]
    width = signal.shape[1] // 2
    part = dot(first_h, signal) + dot(first_l, signal)
    turned = []
    for channel in range(2):
        lanes = slice(channel * width, (channel + 1) * width)
        real, imag = part[:rows, lanes], part[rows:, lanes]
        turned.append(
            jnp.concatenate([real * cosine - imag * sine, real * sine + imag * cosine], axis=1)
        )
    high, low = split(jnp.concatenate(turned, axis=0))
    return dot(high, second_h) + (dot(low, second_h) + dot(high, second_l))


def filter_kernel(filter_ref, first_h, first_l, cosine, sine, second_h, second_l, out_ref):
    out_ref[...] = forward(
        filter_ref[...], first_h[...], first_l[...], cosine[...], sine[...], second_h[...], second_l[...]
    )


def conv_kernel(
    signal_ref,
    spectrum_ref,
    first_h,
    first_l,
    cosine_ref,
    sine_ref,
    second_h,
    second_l,
    second_back_h,
    second_back_l,
    first_back_h,
    first_back_l,
    out_ref,
):
    rows = signal_ref.shape[0]
    width = signal_ref.shape[1] // 2
    cosine, sine = cosine_ref[...], sine_ref[...]
    spectrum = forward(
        signal_ref[...], first_h[...], first_l[...], cosine, sine, second_h[...], second_l[...]
    )
    other = spectrum_ref[...]
    real, imag = spectrum[:, :width], spectrum[:, width:]
    other_real, other_imag = other[:, :width], other[:, width:]
    product = jnp.concatenate(
        [real * other_real - imag * other_imag, real * other_imag + imag * other_real], axis=1
    )
    high, low = split(product)
    table = second_back_h[...]
    part = dot(high, table) + (dot(low, table) + dot(high, second_back_l[...]))
    reals, imags = [], []
    for channel in range(2):
        block = part[channel * rows : (channel + 1) * rows]
        real, imag = block[:, :width], block[:, width:]
        reals.append(real * cosine + imag * sine)
        imags.append(imag * cosine - real * sine)
    turned = jnp.concatenate(
        [jnp.concatenate(reals, axis=1), jnp.concatenate(imags, axis=1)], axis=0
    )
    high, low = split(turned)
    table = first_back_h[...]
    result = dot(table, high) + (dot(table, low) + dot(first_back_l[...], high))
    out_ref[...] = result.astype(jnp.bfloat16)


def whole(array):
    return pl.BlockSpec(array.shape, lambda step: (0,) * array.ndim)


def transform_filter(taps, tables):
    first, twist, second, _, _ = tables
    rows, lanes = taps.shape
    width = twist[0].shape[1]
    pairs = lanes // (2 * width)
    constants = [jnp.asarray(entry) for entry in (*first, *twist, *second)]
    return pl.pallas_call(
        filter_kernel,
        grid=(pairs,),
        in_specs=[pl.BlockSpec((rows, 2 * width), lambda step: (0, step))]
        + [whole(entry) for entry in constants],
        out_specs=pl.BlockSpec((2 * rows, 2 * width), lambda step: (step, 0)),
        out_shape=jax.ShapeDtypeStruct((2 * pairs * rows, 2 * width), jnp.float32),
        compiler_params=pltpu.CompilerParams(vmem_limit_bytes=VMEM_LIMIT),
        cost_estimate=pl.CostEstimate(
            flops=2 * pairs * 170_000_000, bytes_accessed=6 * 1024 * 1024, transcendentals=0
        ),
        name="filter_spectrum",
    )(taps, *constants)


def convolve(signal, spectrum, tables):
    first, twist, second, second_back, first_back = tables
    rows, lanes = signal.shape
    width = twist[0].shape[1]
    pairs = lanes // (2 * width)
    constants = [
        jnp.asarray(entry) for entry in (*first, *twist, *second, *second_back, *first_back)
    ]
    return pl.pallas_call(
        conv_kernel,
        grid=(pairs,),
        in_specs=[
            pl.BlockSpec((rows, 2 * width), lambda step: (0, step)),
            pl.BlockSpec((2 * rows, 2 * width), lambda step: (step, 0)),
        ]
        + [whole(entry) for entry in constants],
        out_specs=pl.BlockSpec((rows, 2 * width), lambda step: (0, step)),
        out_shape=jax.ShapeDtypeStruct(signal.shape, jnp.bfloat16),
        compiler_params=pltpu.CompilerParams(vmem_limit_bytes=VMEM_LIMIT),
        cost_estimate=pl.CostEstimate(
            flops=2 * pairs * 370_000_000, bytes_accessed=8 * 1024 * 1024, transcendentals=0
        ),
        name="convolve",
    )(signal, spectrum, *constants)


def attend_kernel(bias_ref, q_ref, k_own, v_own, k_near, v_near, k_far, v_far, out_ref):
    heads = q_ref.shape[1] // HD
    for head in range(heads):
        rows = slice(head * HD, (head + 1) * HD)
        queries = jnp.concatenate([q_ref[0, rows], q_ref[1, rows]], axis=1)
        keys = jnp.concatenate(
            [k_far[rows], k_near[0, rows], k_near[1, rows], k_own[0, rows], k_own[1, rows]], axis=1
        )
        scores = lax.dot_general(
            keys, queries, (((0,), (0,)), ((), ())), preferred_element_type=jnp.float32
        )
        masked = scores * (1.0 / math.sqrt(HD)) + bias_ref[...]
        weights = jnp.exp(masked - jnp.max(masked, axis=0, keepdims=True))
        total = jnp.sum(weights, axis=0, keepdims=True)
        values = jnp.concatenate(
            [v_far[rows], v_near[0, rows], v_near[1, rows], v_own[0, rows], v_own[1, rows]], axis=1
        )
        mixed = (dot(values, weights.astype(jnp.bfloat16)) / total).astype(jnp.bfloat16)
        tokens = q_ref.shape[2]
        out_ref[0, rows] = mixed[:, :tokens]
        out_ref[1, rows] = mixed[:, tokens:]


def attend(bias, q_own, k_own, v_own, k_near, v_near, k_far, v_far, step_heads=4):
    channels, tokens = q_own.shape[1:]
    step_rows = step_heads * HD
    pair = pl.BlockSpec((2, step_rows, tokens), lambda step: (0, step, 0))
    single = pl.BlockSpec((step_rows, tokens), lambda step: (step, 0))
    return pl.pallas_call(
        attend_kernel,
        grid=(channels // step_rows,),
        in_specs=[whole(bias), pair, pair, pair, pair, pair, single, single],
        out_specs=pair,
        out_shape=jax.ShapeDtypeStruct(q_own.shape, jnp.bfloat16),
        compiler_params=pltpu.CompilerParams(vmem_limit_bytes=VMEM_LIMIT),
        cost_estimate=pl.CostEstimate(
            flops=(channels // HD) * 4 * HD * 640 * 256,
            bytes_accessed=6 * 1024 * 1024,
            transcendentals=(channels // HD) * 640 * 256,
        ),
        name="attend",
    )(bias, q_own, k_own, v_own, k_near, v_near, k_far, v_far)


def chip_bias(block_start, flags, chip, reach, tokens):
    first = 2 * chip
    key_ids = first - reach + jnp.arange(reach + 2, dtype=jnp.int32)
    opened = (block_start < tokens).astype(jnp.int32)
    all_ids = jnp.arange(block_start.shape[0], dtype=jnp.int32)
    base = jnp.sum(jnp.where(all_ids[None, :] < key_ids[:, None], opened[None, :], 0), axis=1)
    start = jnp.sum(jnp.where(all_ids[None, :] == key_ids[:, None], block_start[None, :], 0), axis=1)
    lanes = jnp.arange(tokens, dtype=jnp.int32)
    record = base[:, None] + (lanes[None, :] >= start[:, None]).astype(jnp.int32)
    same = record[:, :, None, None] == record[None, None, reach:, :]
    causal = lanes[None, :, None, None] <= lanes[None, None, None, :]
    distance = (reach + jnp.arange(2))[None, :] - jnp.arange(reach + 2)[:, None]
    picked = jnp.zeros((reach + 2, 2), jnp.int32)
    for step in range(1, reach + 1):
        picked = jnp.where(distance == step, flags[None, :, step - 1], picked)
    earlier = ((picked == 1) & (key_ids[:, None] >= 0))[:, None, :, None]
    own = (distance == 0)[:, None, :, None]
    visible = same & (earlier | (own & causal))
    bias = jnp.where(visible, 0.0, MASKED).astype(jnp.float32)
    return bias.reshape((reach + 2) * tokens, 2 * tokens)


def over_cores(value):
    return lax.all_to_all(value, "c", split_axis=0, concat_axis=0, tiled=True)


def next_chip(value):
    count = math.prod(lax.axis_size(name) for name in ALL)
    return lax.ppermute(value, ALL, [(source, (source + 2) % count) for source in range(count)])


def body(q_proj, k_proj, v_proj, block_start, kv_select, pre_gate, post_gate, long_filter):
    channels, tokens = q_proj.shape
    devices = math.prod(lax.axis_size(name) for name in ALL)
    reach = kv_select.shape[1]
    own = channels // devices
    half = channels // 2
    tables = make_tables(devices, tokens)

    k_own = over_cores(k_proj.reshape(2, half, tokens))
    k_near = next_chip(k_own)
    v_own = over_cores(v_proj.reshape(2, half, tokens))
    v_near = next_chip(v_own)
    k_far = next_chip(k_near[1])
    v_far = next_chip(v_near[1])
    q_own = over_cores(q_proj.reshape(2, half, tokens))

    flags = lax.all_gather(kv_select.astype(jnp.float32), "c", axis=0, tiled=True).astype(jnp.int32)
    chip = lax.axis_index(("z", "x", "y"))
    bias = chip_bias(block_start, flags, chip, reach, tokens)

    taps = long_filter.reshape(own, devices, tokens).transpose(1, 0, 2).reshape(devices, own * tokens)
    spectrum = transform_filter(taps, tables)

    halves = attend(bias, q_own, k_own, v_own, k_near, v_near, k_far, v_far)
    attn_out = over_cores(halves).reshape(channels, tokens)
    mixed_in = (attn_out.astype(jnp.float32) * pre_gate.astype(jnp.float32)).astype(jnp.bfloat16)

    gathered = lax.all_to_all(
        mixed_in.reshape(devices, own, tokens), ALL, split_axis=0, concat_axis=0, tiled=True
    )
    conv_out = convolve(gathered.reshape(devices, own * tokens), spectrum, tables)
    returned = lax.all_to_all(
        conv_out.reshape(devices, own, tokens), ALL, split_axis=0, concat_axis=0, tiled=True
    ).reshape(channels, tokens)
    mixed = (post_gate.astype(jnp.float32) * returned.astype(jnp.float32)).astype(jnp.bfloat16)
    return (attn_out, mixed)


def solution(mesh):
    chips = Mesh(mesh.devices.reshape(8, 4, 4, 2), ALL)
    return jax.shard_map(
        body,
        mesh=chips,
        in_specs=(
            P(None, ALL),
            P(None, ALL),
            P(None, ALL),
            P(),
            P(ALL, None),
            P(None, ALL),
            P(None, ALL),
            P(ALL, None),
        ),
        out_specs=(P(None, ALL), P(None, ALL)),
        check_vma=False,
    )
```

profile of v0, /device:TPU:1, one launch (start us, length us, event | category | flops | bytes accessed | tf_op | source)
XLA Modules:
  0.0 204.3 jit_solution(3643615383423812324)
XLA Ops:
  0.6 8.7 %all_to_all.30.k_own = bf16[2,2048,128]{2,1,0:T(8,128)(2,1)S(1)} all-to-all(bf16[2,2048,128]{2,1,0:T(8,128)(2,1)} %bitcast.48), channel_id=1, replica_groups=mesh['z'=8,'x'=4,'y'=4,'c'=2] {'c'}, dimensions={0} | all-to-all | bytes 2097152 | tf_op jit(solution)/shard_map/all_to_all | solution.py:236
  9.3 4.1 %all-to-all-start.2 = ((bf16[2,2048,128]{2,1,0:T(8,128)(2,1)}), bf16[2,2048,128]{2,1,0:T(8,128)(2,1)S(1)}, u32[]{:S(2)}, u32[]{:S(2)}) async-start(bf16[2,2048,128]{2,1,0:T(8,128)(2,1)} %bitcast.49), calls=%async_computation.2 | async-start | bytes 2097152 | tf_op jit(solution)/shard_map/all_to_all | solution.py:236
  13.4 1.7 all-to-all-done.2.v_own
  15.2 4.8 %all-to-all-start = ((bf16[2,2048,128]{2,1,0:T(8,128)(2,1)}), bf16[2,2048,128]{2,1,0:T(8,128)(2,1)}, u32[]{:S(2)}, u32[]{:S(2)}) async-start(bf16[2,2048,128]{2,1,0:T(8,128)(2,1)} %bitcast.50), calls=%async_computation | async-start | bytes 2097152 | tf_op jit(solution)/shard_map/all_to_all | solution.py:236
  20.0 1.8 all-gather
  22.5 22.9 %collective-permute-done.k_near = bf16[2,2048,128]{2,1,0:T(8,128)(2,1)} collective-permute-done((bf16[2,2048,128]{2,1,0:T(8,128)(2,1)S(1)}, bf16[2,2048,128]{2,1,0:T(8,128)(2,1)}, u32[]{:S(2)}, u32[]{:S(2)}) %collective-permute-start) | collective-permute-done | bytes 1048608 | tf_op jit(solution)/shard_map/ppermute | solution.py:241
  45.4 1.9 slice_bitcast_fusion.1
  47.3 20.6 %collective-permute-done.1.v_near = bf16[2,2048,128]{2,1,0:T(8,128)(2,1)} collective-permute-done((bf16[2,2048,128]{2,1,0:T(8,128)(2,1)S(1)}, bf16[2,2048,128]{2,1,0:T(8,128)(2,1)}, u32[]{:S(2)}, u32[]{:S(2)}) %collective-permute-start.1) | collective-permute-done | bytes 1048608 | tf_op jit(solution)/shard_map/ppermute | solution.py:241
  67.9 1.9 slice_bitcast_fusion
  71.3 7.8 %collective-permute-done.2.k_far = bf16[2048,128]{1,0:T(8,128)(2,1)} collective-permute-done((bf16[2048,128]{1,0:T(8,128)(2,1)}, bf16[2048,128]{1,0:T(8,128)(2,1)}, u32[]{:S(2)}, u32[]{:S(2)}) %collective-permute-start.2) | collective-permute-done | bytes 524320 | tf_op jit(solution)/shard_map/ppermute | solution.py:241
  79.2 11.2 %collective-permute-done.3.v_far = bf16[2048,128]{1,0:T(8,128)(2,1)} collective-permute-done((bf16[2048,128]{1,0:T(8,128)(2,1)}, bf16[2048,128]{1,0:T(8,128)(2,1)}, u32[]{:S(2)}, u32[]{:S(2)}) %collective-permute-start.3) | collective-permute-done | bytes 524320 | tf_op jit(solution)/shard_map/ppermute | solution.py:241
  90.4 1.1 copy-done.1
  91.5 9.8 %attend.1 = bf16[2,2048,128]{2,1,0:T(8,128)(2,1)S(1)} custom-call(f32[640,256]{1,0:T(8,128)S(1)} %copy-done.1, bf16[2,2048,128]{2,1,0:T(8,128)(2,1)} %all-to-all-done.q_ref, bf16[2,2048,128]{2,1,0:T(8,128)(2,1)S(1)} %all_to_all.30.k_own, bf16[2,2048,128]{2,1,0:T(8,128)(2,1)S(1)} %all-to-all-done.2.v_own, bf16[2,2048,128]{2,1,0:T(8,128)(2,1)} %collective-permute-done.k_near, ...), custom_call_target="tpu_custom_call" | custom-call | flops 1342177280 | bytes 6291456 | tf_op jit(solution)/shard_map/attend/pallas_call | solution.py:197
  101.3 5.0 %all_to_all.31 = bf16[2,2048,128]{2,1,0:T(8,128)(2,1)S(1)} all-to-all(bf16[2,2048,128]{2,1,0:T(8,128)(2,1)S(1)} %attend.1), channel_id=1, replica_groups=mesh['z'=8,'x'=4,'y'=4,'c'=2] {'c'}, dimensions={0} | all-to-all | bytes 2097152 | tf_op jit(solution)/shard_map/all_to_all | solution.py:236
  107.3 1.3 multiply_convert_fusion
  108.6 7.1 %all-to-all-start.4 = ((bf16[256,16,128]{2,1,0:T(8,128)(2,1)}), bf16[256,16,128]{2,1,0:T(8,128)(2,1)}, u32[]{:S(2)}, u32[]{:S(2)}) async-start(bf16[256,16,128]{2,1,0:T(8,128)(2,1)} %bitcast.10), calls=%async_computation.4 | async-start | bytes 2097152 | tf_op jit(solution)/shard_map/all_to_all | solution.py:271
  116.9 7.8 %filter_spectrum.1.spectrum_ref = f32[4096,256]{1,0:T(8,128)} custom-call(bf16[256,2048]{1,0:T(8,128)(2,1)S(1)} %bitcast.45, bf16[512,256]{1,0:T(8,128)(2,1)S(1)} %copy-done.2, bf16[512,256]{1,0:T(8,128)(2,1)S(1)} %copy-done.3, f32[256,128]{1,0:T(8,128)S(1)} %copy-done.6, f32[256,128]{1,0:T(8,128)S(1)} %copy-done.7, bf16[256,256]{1,0:T(8,128)(2,1)S(1)} %copy-done.8, ...), custom_call_target="tpu_custom_call" | custom-call | flops 2720000000 | bytes 6291456 | tf_op jit(solution)/shard_map/filter_spectrum/pallas_call | solution.py:128
  124.8 20.7 %all-to-all-done.4 = bf16[256,16,128]{2,1,0:T(8,128)(2,1)} async-done(((bf16[256,16,128]{2,1,0:T(8,128)(2,1)}), bf16[256,16,128]{2,1,0:T(8,128)(2,1)}, u32[]{:S(2)}, u32[]{:S(2)}) %all-to-all-start.4) | async-done | bytes 1048608 | tf_op jit(solution)/shard_map/all_to_all | solution.py:271
  145.4 1.5 copy.37
  147.0 15.6 %convolve.1 = bf16[256,2048]{1,0:T(8,128)(2,1)S(1)} custom-call(bf16[256,2048]{1,0:T(8,128)(2,1)S(1)} %bitcast.43, f32[4096,256]{1,0:T(8,128)} %filter_spectrum.1.spectrum_ref, bf16[512,256]{1,0:T(8,128)(2,1)S(1)} %copy-done.2, bf16[512,256]{1,0:T(8,128)(2,1)S(1)} %copy-done.3, f32[256,128]{1,0:T(8,128)S(1)} %copy-done.6, f32[256,128]{1,0:T(8,128)S(1)} %copy-done.7, ...), custom_call_target="tpu_custom_call" | custom-call | flops 5920000000 | bytes 8388608 | tf_op jit(solution)/shard_map/convolve/pallas_call | solution.py:151
  162.6 1.2 copy.31
  163.8 6.5 %all-to-all-start.5 = ((bf16[256,16,128]{2,1,0:T(8,128)(2,1)}), bf16[256,16,128]{2,1,0:T(8,128)(2,1)S(1)}, u32[]{:S(2)}, u32[]{:S(2)}) async-start(bf16[256,16,128]{2,1,0:T(8,128)(2,1)} %bitcast.26), calls=%async_computation.5 | async-start | bytes 2097152 | tf_op jit(solution)/shard_map/all_to_all | solution.py:275
  170.2 30.6 %all-to-all-done.5 = bf16[256,16,128]{2,1,0:T(8,128)(2,1)S(1)} async-done(((bf16[256,16,128]{2,1,0:T(8,128)(2,1)}), bf16[256,16,128]{2,1,0:T(8,128)(2,1)S(1)}, u32[]{:S(2)}, u32[]{:S(2)}) %all-to-all-start.5) | async-done | bytes 1048608 | tf_op jit(solution)/shard_map/all_to_all | solution.py:275
  200.9 2.5 %fusion = bf16[4096,128]{1,0:T(8,128)(2,1)} fusion(bf16[4096,128]{1,0:T(8,128)(2,1)} %param.24, bf16[256,16,128]{2,1,0:T(8,128)(2,1)S(1)} %all-to-all-done.5), kind=kLoop, calls=%fused_computation.1 | loop fusion | flops 2097152 | bytes 3145728 | tf_op jit(solution)/shard_map/convert_element_type | solution.py:278
  (57 shorter events, 5.4 us)
Async XLA Ops:
  0.6 115.1 %copy-start = (bf16[16,32768]{1,0:T(8,128)(2,1)S(1)}, bf16[16,32768]{1,0:T(8,128)(2,1)}, u32[]{:S(2)}) copy-start(bf16[16,32768]{1,0:T(8,128)(2,1)} %param.25) | copy-start | bytes 3145732
  9.3 10.6 %copy-start.16 = (s32[1,3]{1,0:T(1,128)S(1)}, s32[1,3]{1,0:T(1,128)}, u32[]{:S(2)}) copy-start(s32[1,3]{1,0:T(1,128)} %param.22) | copy-start | bytes 40
  9.3 12.7 %copy-start.15 = (s32[256]{0:T(256)S(1)}, s32[256]{0:T(256)}, u32[]{:S(2)}) copy-start(s32[256]{0:T(256)} %param.21) | copy-start | bytes 3076
  9.3 5.8 %all-to-all-start.2 = ((bf16[2,2048,128]{2,1,0:T(8,128)(2,1)}), bf16[2,2048,128]{2,1,0:T(8,128)(2,1)S(1)}, u32[]{:S(2)}, u32[]{:S(2)}) async-start(bf16[2,2048,128]{2,1,0:T(8,128)(2,1)} %bitcast.49), calls=%async_computation.2 | async-start | bytes 2097152 | tf_op jit(solution)/shard_map/all_to_all | solution.py:236
  13.4 32.0 %collective-permute-start = (bf16[2,2048,128]{2,1,0:T(8,128)(2,1)S(1)}, bf16[2,2048,128]{2,1,0:T(8,128)(2,1)}, u32[]{:S(2)}, u32[]{:S(2)}) collective-permute-start(bf16[2,2048,128]{2,1,0:T(8,128)(2,1)S(1)} %all_to_all.30.k_own), channel_id=1, source_target_pairs={{0,2},{1,3},{2,4},{3,5},{4,6},{5,7},{6,8},{7,9},{8,10},{9,11},{10,... | collective-permute-start | bytes 3145736 | tf_op jit(solution)/shard_map/ppermute | solution.py:241
  15.2 56.1 %all-to-all-start = ((bf16[2,2048,128]{2,1,0:T(8,128)(2,1)}), bf16[2,2048,128]{2,1,0:T(8,128)(2,1)}, u32[]{:S(2)}, u32[]{:S(2)}) async-start(bf16[2,2048,128]{2,1,0:T(8,128)(2,1)} %bitcast.50), calls=%async_computation | async-start | bytes 2097152 | tf_op jit(solution)/shard_map/all_to_all | solution.py:236
  20.0 48.0 %collective-permute-start.1 = (bf16[2,2048,128]{2,1,0:T(8,128)(2,1)S(1)}, bf16[2,2048,128]{2,1,0:T(8,128)(2,1)}, u32[]{:S(2)}, u32[]{:S(2)}) collective-permute-start(bf16[2,2048,128]{2,1,0:T(8,128)(2,1)S(1)} %all-to-all-done.2.v_own), channel_id=1, source_target_pairs={{0,2},{1,3},{2,4},{3,5},{4,6},{5,7},{6,8},{7,9},{8,10},{9,11},{10,... | collective-permute-start | bytes 3145736 | tf_op jit(solution)/shard_map/ppermute | solution.py:241
  47.3 31.8 %collective-permute-start.2 = (bf16[2048,128]{1,0:T(8,128)(2,1)}, bf16[2048,128]{1,0:T(8,128)(2,1)}, u32[]{:S(2)}, u32[]{:S(2)}) collective-permute-start(bf16[2048,128]{1,0:T(8,128)(2,1)} %slice_bitcast_fusion.1), channel_id=1, source_target_pairs={{0,2},{1,3},{2,4},{3,5},{4,6},{5,7},{6,8},{7,9},{8,10},{9,11},{10,... | collective-permute-start | bytes 1572872 | tf_op jit(solution)/shard_map/ppermute | solution.py:241
  69.8 20.6 %collective-permute-start.3 = (bf16[2048,128]{1,0:T(8,128)(2,1)}, bf16[2048,128]{1,0:T(8,128)(2,1)}, u32[]{:S(2)}, u32[]{:S(2)}) collective-permute-start(bf16[2048,128]{1,0:T(8,128)(2,1)} %slice_bitcast_fusion), channel_id=1, source_target_pairs={{0,2},{1,3},{2,4},{3,5},{4,6},{5,7},{6,8},{7,9},{8,10},{9,11},{10,... | collective-permute-start | bytes 1572872 | tf_op jit(solution)/shard_map/ppermute | solution.py:241
  90.4 1.1 copy-start.1
  101.3 6.0 %copy-start.14 = (bf16[4096,128]{1,0:T(8,128)(2,1)S(1)}, bf16[4096,128]{1,0:T(8,128)(2,1)}, u32[]{:S(2)}) copy-start(bf16[4096,128]{1,0:T(8,128)(2,1)} %param.23) | copy-start | bytes 3145732
  106.3 1.0 copy-start.12
  108.6 36.8 %all-to-all-start.4 = ((bf16[256,16,128]{2,1,0:T(8,128)(2,1)}), bf16[256,16,128]{2,1,0:T(8,128)(2,1)}, u32[]{:S(2)}, u32[]{:S(2)}) async-start(bf16[256,16,128]{2,1,0:T(8,128)(2,1)} %bitcast.10), calls=%async_computation.4 | async-start | bytes 2097152 | tf_op jit(solution)/shard_map/all_to_all | solution.py:271
  115.8 1.0 copy-start.3
  115.8 1.0 copy-start.6
  115.8 1.1 copy-start.7
  115.8 1.1 copy-start.8
  115.8 1.1 copy-start.9
  124.8 22.2 %copy-start.4 = (bf16[256,512]{1,0:T(8,128)(2,1)S(1)}, bf16[256,512]{1,0:T(8,128)(2,1)}, u32[]{:S(2)}) copy-start(bf16[256,512]{1,0:T(8,128)(2,1)} %constant.67.clone.first_back_h) | copy-start | bytes 786436
  124.8 22.2 %copy-start.5 = (bf16[256,512]{1,0:T(8,128)(2,1)S(1)}, bf16[256,512]{1,0:T(8,128)(2,1)}, u32[]{:S(2)}) copy-start(bf16[256,512]{1,0:T(8,128)(2,1)} %constant.68.clone.first_back_l) | copy-start | bytes 786436
  124.8 22.2 %copy-start.10 = (bf16[256,256]{1,0:T(8,128)(2,1)S(1)}, bf16[256,256]{1,0:T(8,128)(2,1)}, u32[]{:S(2)}) copy-start(bf16[256,256]{1,0:T(8,128)(2,1)} %constant.65.clone.second_back_h) | copy-start | bytes 393220
  124.8 22.2 %copy-start.11 = (bf16[256,256]{1,0:T(8,128)(2,1)S(1)}, bf16[256,256]{1,0:T(8,128)(2,1)}, u32[]{:S(2)}) copy-start(bf16[256,256]{1,0:T(8,128)(2,1)} %constant.66.clone.second_back_l) | copy-start | bytes 393220
  163.8 37.1 %all-to-all-start.5 = ((bf16[256,16,128]{2,1,0:T(8,128)(2,1)}), bf16[256,16,128]{2,1,0:T(8,128)(2,1)S(1)}, u32[]{:S(2)}, u32[]{:S(2)}) async-start(bf16[256,16,128]{2,1,0:T(8,128)(2,1)} %bitcast.26), calls=%async_computation.5 | async-start | bytes 2097152 | tf_op jit(solution)/shard_map/all_to_all | solution.py:275
  170.2 33.1 %copy-start.13 = (bf16[2,2048,128]{2,1,0:T(8,128)(2,1)S(1)}, bf16[2,2048,128]{2,1,0:T(8,128)(2,1)}, u32[]{:S(2)}) copy-start(bf16[2,2048,128]{2,1,0:T(8,128)(2,1)} %copy-done.12) | copy-start | bytes 3145732
  (1 other events, 1.0 us)
where the time goes:
time: 205 us; the launch traced here: 204 us
  waiting for transfers between devices  116 us (57%)
  Pallas kernels  33.2 us (16%)
  starting transfers between devices  22.4 us (11%)
  blocking collectives  15.5 us (8%)
  local copies, waits for them, and re-layouts  11.3 us (6%)
  other arithmetic  5.41 us (3%)
    ppermute x4, waiting for transfers between devices, next_chip(): lax.ppermute(value, ALL, [(source, (source + 2) % count) for source in ra...  62.6 us
    all_to_all x1, waiting for transfers between devices, body(): lax.all_to_all(conv_out.reshape(devices, own, tokens), ALL, split_axis=0,...  30.6 us
    all_to_all x1, waiting for transfers between devices, body(): lax.all_to_all(mixed_in.reshape(devices, own, tokens), ALL, split_axis=0,...  20.7 us
    pallas_call x1, Pallas kernels, convolve(): pl.pallas_call(conv_kernel, grid=(pairs,), in_specs=[pl.BlockSpec((rows,...  15.6 us
    all_to_all x2, blocking collectives, over_cores(): return lax.all_to_all(value, 'c', split_axis=0, concat_axis=0, tiled=True)  13.7 us
    pallas_call x1, Pallas kernels, attend(): pl.pallas_call(attend_kernel, grid=(channels // step_rows,), in_specs=[wh...  9.82 us
    all_to_all x2, starting transfers between devices, over_cores(): return lax.all_to_all(value, 'c', split_axis=0, concat_axis=0, tiled=True)  8.86 us
    pallas_call x1, Pallas kernels, transform_filter(): pl.pallas_call(filter_kernel, grid=(pairs,), in_specs=[pl.BlockSpec((rows...  7.81 us
  transfers between devices with their start and end apart: 8, of which 7 were waited for; matrix products, arithmetic and copies ran while one was open for 3% of the time, Pallas kernels for 4%

commit v1 on v0

v1 whole, which is shorter than its diff:
```python
import math

import jax
import jax.numpy as jnp
import ml_dtypes
import numpy as np
from jax import lax
from jax.experimental import pallas as pl
from jax.experimental.pallas import tpu as pltpu
from jax.sharding import Mesh
from jax.sharding import PartitionSpec as P

HD = 128
ALL = ("za", "zb", "zc", "x", "y", "c")
CHIPS = ("za", "zb", "x", "y", "zc")
OWNERS = ("za", "zb", "c", "x", "y", "zc")
STEPS = 4
MASKED = -1e30
VMEM_LIMIT = 48 * 1024 * 1024
HBM_ONLY = 60 * 1024 * 1024


def hi_lo(table):
    high = table.astype(ml_dtypes.bfloat16)
    low = (table - high.astype(np.float64)).astype(ml_dtypes.bfloat16)
    return (high, low)


def make_tables(rows, width):
    length = rows * width
    k1 = np.arange(rows)[:, None]
    n1 = np.arange(rows)[None, :]
    theta = 2.0 * np.pi * (((4 * k1 + 1) * n1) % (4 * rows)) / (4 * rows)
    n2 = np.arange(width)[None, :]
    turn = 2.0 * np.pi * (((4 * k1 + 1) * n2) % (4 * length)) / (4 * length)
    k2 = np.arange(width)[:, None]
    phi = 2.0 * np.pi * ((k2 * n2) % width) / width
    first = hi_lo(np.concatenate([np.cos(theta), -np.sin(theta)], axis=0))
    second = hi_lo(np.block([[np.cos(phi), -np.sin(phi)], [np.sin(phi), np.cos(phi)]]))
    second_back = hi_lo(np.block([[np.cos(phi), np.sin(phi)], [-np.sin(phi), np.cos(phi)]]))
    first_back = hi_lo(np.concatenate([np.cos(theta).T, -np.sin(theta).T], axis=1) / length)
    twist = (np.cos(turn).astype(np.float32), -np.sin(turn).astype(np.float32))
    blocks = np.arange(rows).reshape(4, 2, -1, 2)
    arriving = blocks.transpose(0, 2, 1, 3).reshape(-1)
    leaving = blocks.transpose(0, 3, 2, 1).reshape(-1)
    first_moved = np.concatenate([table[:, arriving] for table in first], axis=1)
    first = np.concatenate(first, axis=1)
    second = np.concatenate([second[0], second[0], second[1]], axis=0)
    second_back = np.concatenate([second_back[0], second_back[0], second_back[1]], axis=0)
    high, low = (table[leaving] for table in first_back)
    first_back = np.concatenate([high, high, low], axis=1)
    return first, first_moved, twist, second, second_back, first_back


def dot(left, right):
    return jnp.dot(left, right, preferred_element_type=jnp.float32)


def split(value):
    high = value.astype(jnp.bfloat16)
    low = (value - high.astype(jnp.float32)).astype(jnp.bfloat16)
    return high, low


def turned_by(real, imag, cosine, sine):
    return real * cosine - imag * sine, real * sine + imag * cosine


def forward(signals, first, cosine, sine, second):
    rows, width = signals[0].shape
    signal = jnp.concatenate(signals, axis=1)
    part = dot(first, jnp.concatenate([signal, signal], axis=0))
    turned = []
    for channel in range(2):
        lanes = slice(channel * width, (channel + 1) * width)
        turned.append(
            jnp.concatenate(turned_by(part[:rows, lanes], part[rows:, lanes], cosine, sine), axis=1)
        )
    high, low = split(jnp.concatenate(turned, axis=0))
    return dot(jnp.concatenate([high, low, high], axis=1), second)


def filter_kernel(filter_ref, first, cosine, sine, second, out_ref):
    for pair in range(filter_ref.shape[0] // 2):
        signals = [filter_ref[2 * pair], filter_ref[2 * pair + 1]]
        rows = signals[0].shape[0]
        out_ref[2 * rows * pair : 2 * rows * (pair + 1)] = forward(
            signals, first[...], cosine[...], sine[...], second[...]
        )


def conv_kernel(
    signal_ref, spectrum_ref, first, cosine_ref, sine_ref, second, second_back, first_back, out_ref
):
    rows, width = signal_ref.shape[1:]
    cosine, sine = cosine_ref[...], sine_ref[...]
    for pair in range(signal_ref.shape[0] // 2):
        signals = [signal_ref[2 * pair], signal_ref[2 * pair + 1]]
        spectrum = forward(signals, first[...], cosine, sine, second[...])
        other = spectrum_ref[2 * rows * pair : 2 * rows * (pair + 1)]
        product = jnp.concatenate(
            turned_by(spectrum[:, :width], spectrum[:, width:], other[:, :width], other[:, width:]),
            axis=1,
        )
        high, low = split(product)
        part = dot(jnp.concatenate([high, low, high], axis=1), second_back[...])
        reals, imags = [], []
        for channel in range(2):
            block = part[channel * rows : (channel + 1) * rows]
            real, imag = turned_by(block[:, :width], block[:, width:], cosine, -sine)
            reals.append(real)
            imags.append(imag)
        turned = jnp.concatenate(
            [jnp.concatenate(reals, axis=1), jnp.concatenate(imags, axis=1)], axis=0
        )
        high, low = split(turned)
        result = dot(first_back[...], jnp.concatenate([high, low, high], axis=0))
        result = result.astype(jnp.bfloat16)
        out_ref[2 * pair] = result[:, :width]
        out_ref[2 * pair + 1] = result[:, width:]


def whole(array):
    return pl.BlockSpec(array.shape, lambda step: (0,) * array.ndim)


def transform_filter(taps, tables, step_channels=4):
    first, _, twist, second, _, _ = tables
    channels, rows, width = taps.shape
    constants = [jnp.asarray(entry) for entry in (first, *twist, second)]
    return pl.pallas_call(
        filter_kernel,
        grid=(channels // step_channels,),
        in_specs=[pl.BlockSpec((step_channels, rows, width), lambda step: (step, 0, 0))]
        + [whole(entry) for entry in constants],
        out_specs=pl.BlockSpec((step_channels * rows, 2 * width), lambda step: (step, 0)),
        out_shape=jax.ShapeDtypeStruct((channels * rows, 2 * width), jnp.float32),
        compiler_params=pltpu.CompilerParams(vmem_limit_bytes=VMEM_LIMIT),
        cost_estimate=pl.CostEstimate(
            flops=channels * 170_000_000, bytes_accessed=6 * 1024 * 1024, transcendentals=0
        ),
        name="filter_spectrum",
    )(taps, *constants)


def convolve(signal, spectrum, tables, step_channels=4):
    _, first, twist, second, second_back, first_back = tables
    channels, rows, width = signal.shape
    constants = [jnp.asarray(entry) for entry in (first, *twist, second, second_back, first_back)]
    block = pl.BlockSpec((step_channels, rows, width), lambda step: (step, 0, 0))
    return pl.pallas_call(
        conv_kernel,
        grid=(channels // step_channels,),
        in_specs=[
            block,
            pl.BlockSpec((step_channels * rows, 2 * width), lambda step: (step, 0)),
        ]
        + [whole(entry) for entry in constants],
        out_specs=block,
        out_shape=jax.ShapeDtypeStruct(signal.shape, jnp.bfloat16),
        compiler_params=pltpu.CompilerParams(vmem_limit_bytes=VMEM_LIMIT),
        cost_estimate=pl.CostEstimate(
            flops=channels * 370_000_000, bytes_accessed=8 * 1024 * 1024, transcendentals=0
        ),
        name="convolve",
    )(signal, spectrum, *constants)


def pick_heads(which, first, second):
    tokens = first.shape[1]
    pairs = [value.reshape(STEPS, 2, -1, tokens) for value in (first, second)]
    return jnp.stack(
        [
            lax.dynamic_index_in_dim(pair, which, 1, keepdims=False).reshape(-1, tokens)
            for pair in pairs
        ]
    )


def attend_kernel(
    core_ref,
    bias_ref,
    q_mine,
    gate_mine,
    q_other,
    gate_other,
    far,
    near,
    crossed,
    own,
    sibling,
    out_mine,
    out_other,
    gated,
):
    heads, tokens = q_mine.shape[0] // HD, q_mine.shape[1]
    group = gated.shape[2]
    core = core_ref[0]
    pairs = (far, near, crossed, own, sibling)
    for head in range(heads):
        rows = slice(head * HD, (head + 1) * HD)
        queries = jnp.concatenate([q_mine[rows], q_other[rows]], axis=1)
        keys = jnp.concatenate([pair[0, rows] for pair in pairs], axis=1)
        scores = lax.dot_general(
            keys, queries, (((0,), (0,)), ((), ())), preferred_element_type=jnp.float32
        )
        masked = scores * (math.log2(math.e) / math.sqrt(HD)) + bias_ref[...]
        weights = jnp.exp2(masked - jnp.max(masked, axis=0, keepdims=True))
        total = jnp.sum(weights, axis=0, keepdims=True)
        values = jnp.concatenate([pair[1, rows] for pair in pairs], axis=1)
        mixed = (dot(values, weights.astype(jnp.bfloat16)) / total).astype(jnp.bfloat16)
        gates = ((out_mine, gate_mine, core), (out_other, gate_other, 1 - core))
        for place, (out, gate, block) in enumerate(gates):
            part = mixed[:, place * tokens : (place + 1) * tokens]
            out[rows] = part
            product = (part.astype(jnp.float32) * gate[rows].astype(jnp.float32)).astype(jnp.bfloat16)
            owners = slice(head * HD // group, (head + 1) * HD // group)
            gated[owners, block] = product.reshape(HD // group, group, tokens)


def attend(core, bias, q_proj, gate, exchanged, blocks, group):
    channels, tokens = q_proj.shape[0] // 2, q_proj.shape[1]
    step_rows = channels // STEPS
    half = pl.BlockSpec((step_rows, tokens), lambda step, core: (2 * step + core[0], 0))
    single = pl.BlockSpec((step_rows, tokens), lambda step, core: (step, 0))
    pair = pl.BlockSpec((2, step_rows, tokens), lambda step, core: (0, step, 0))
    pieces = [
        pl.BlockSpec((None, step_rows, tokens), lambda step, core, which=which: (which, step, 0))
        for which in range(2)
    ]
    return pl.pallas_call(
        attend_kernel,
        grid_spec=pltpu.PrefetchScalarGridSpec(
            num_scalar_prefetch=1,
            grid=(STEPS,),
            in_specs=[pl.BlockSpec(bias.shape, lambda step, core: (0, 0)), half, half, *pieces]
            + [pair] * 5,
            out_specs=[
                single,
                single,
                pl.BlockSpec((step_rows // group, 2, group, tokens), lambda step, core: (step, 0, 0, 0)),
            ],
        ),
        out_shape=[
            jax.ShapeDtypeStruct((channels, tokens), jnp.bfloat16),
            jax.ShapeDtypeStruct((channels, tokens), jnp.bfloat16),
            jax.ShapeDtypeStruct((channels // group, 2, group, tokens), jnp.bfloat16),
        ],
        compiler_params=pltpu.CompilerParams(vmem_limit_bytes=HBM_ONLY),
        cost_estimate=pl.CostEstimate(
            flops=(channels // HD) * 4 * HD * bias.size,
            bytes_accessed=18 * 2 * channels * tokens + 4 * bias.size,
            transcendentals=(channels // HD) * bias.size,
        ),
        name="attend",
    )(core.reshape(1), bias, q_proj, gate, exchanged, exchanged, *blocks)


def chip_bias(block_start, flags, key_ids, query_ids, tokens):
    opened = (block_start < tokens).astype(jnp.int32)
    all_ids = jnp.arange(block_start.shape[0], dtype=jnp.int32)
    lanes = jnp.arange(tokens, dtype=jnp.int32)

    def records(ids):
        base = jnp.sum(jnp.where(all_ids[None, :] < ids[:, None], opened[None, :], 0), axis=1)
        start = jnp.sum(
            jnp.where(all_ids[None, :] == ids[:, None], block_start[None, :], 0), axis=1
        )
        return base[:, None] + (lanes[None, :] >= start[:, None]).astype(jnp.int32)

    same = records(key_ids)[:, :, None, None] == records(query_ids)[None, None, :, :]
    causal = lanes[None, :, None, None] <= lanes[None, None, None, :]
    distance = query_ids[None, :] - key_ids[:, None]
    picked = jnp.zeros(distance.shape, jnp.int32)
    for step in range(flags.shape[1]):
        picked = jnp.where(distance == step + 1, flags[None, :, step], picked)
    earlier = ((picked == 1) & (key_ids[:, None] >= 0))[:, None, :, None]
    own = (distance == 0)[:, None, :, None]
    visible = same & (earlier | (own & causal))
    bias = jnp.where(visible, 0.0, MASKED).astype(jnp.float32)
    return bias.reshape(key_ids.shape[0] * tokens, query_ids.shape[0] * tokens)


def devices_of():
    return math.prod(lax.axis_size(name) for name in ALL)


def send(value, target):
    count = devices_of()
    return lax.ppermute(value, ALL, [(source, target(source) % count) for source in range(count)])


def next_chip(value):
    return send(value, lambda source: source + 2)


def next_chip_crossed(value):
    return send(value, lambda source: (source + 2) ^ 1)


def second_next_chip(value):
    count, ring = devices_of(), lax.axis_size("y")

    def between(source):
        y = source // 2 % ring
        return source + 2 * ((y - 1) % ring - y)

    value = lax.ppermute(value, "y", [(y, (y - 1) % ring) for y in range(ring)])
    return lax.ppermute(
        value, ALL, [(between(source), (source + 4) % count) for source in range(count)]
    )


def to_sibling(value):
    return lax.ppermute(value, "c", [(0, 1), (1, 0)])


def body(q_proj, k_proj, v_proj, block_start, kv_select, pre_gate, post_gate, long_filter):
    channels, tokens = q_proj.shape
    devices = devices_of()
    group = channels // devices
    tables = make_tables(devices, tokens)
    core = lax.axis_index("c")
    first_core = core == 0

    other = pick_heads(1 - core, k_proj, v_proj)
    sibling = to_sibling(other)
    crossed = next_chip_crossed(other)
    k_later, v_later, other = lax.optimization_barrier((k_proj, v_proj, other))
    mine = pick_heads(core, k_later, v_later)
    near = next_chip(mine)
    odd = jnp.where(first_core, sibling, mine)
    far = second_next_chip(odd)
    flags = kv_select.astype(jnp.float32)
    flags = jnp.concatenate([flags, to_sibling(flags)], axis=0).astype(jnp.int32)
    first = 2 * lax.axis_index(ALL[:-1])
    key_ids = jnp.stack(
        [first - 3, first - 2 + core, first - 1 - core, first + core, first + 1 - core]
    )
    query_ids = jnp.stack([first + core, first + 1 - core])
    bias = chip_bias(block_start, flags, key_ids, query_ids, tokens)

    q_later, gate_later, bias, _ = lax.optimization_barrier((q_proj, pre_gate, bias, odd))
    exchanged_half = to_sibling(pick_heads(1 - core, q_later, gate_later))

    def exchanged(source):
        upper, zc, lower, c = source // 64, source // 32 % 2, source // 2 % 16, source % 2
        return upper * 64 + c * 32 + lower * 2 + zc

    taps = long_filter.reshape(group, devices, tokens)
    taps, bias, _ = lax.optimization_barrier((taps, bias, odd))
    taps, far, near = lax.optimization_barrier((taps, far, near))
    moved = [(source, exchanged(source)) for source in range(devices) if exchanged(source) != source]
    swapped = lax.ppermute(taps, ALL, moved)

    out_mine, out_other, gated = attend(
        core, bias, q_proj, pre_gate, exchanged_half, (far, near, crossed, mine, sibling), group
    )
    gated, swapped = lax.optimization_barrier((gated, swapped))
    taps = jnp.where(lax.axis_index("zc") == core, taps, swapped)
    spectrum = transform_filter(taps, tables)
    gathered = lax.all_to_all(gated, CHIPS, split_axis=0, concat_axis=0, tiled=True)
    out_other = to_sibling(out_other)
    attn_out = jnp.stack(
        [
            jnp.where(first_core, out_mine, out_other).reshape(STEPS, -1, tokens),
            jnp.where(first_core, out_other, out_mine).reshape(STEPS, -1, tokens),
        ],
        axis=1,
    ).reshape(channels, tokens)

    signal = gathered.reshape(devices, group, tokens).transpose(1, 0, 2)
    conv_out = convolve(signal, spectrum, tables).transpose(1, 0, 2)
    returned = lax.all_to_all(
        conv_out, OWNERS, split_axis=0, concat_axis=0, tiled=True
    ).reshape(channels, tokens)
    mixed = (post_gate.astype(jnp.float32) * returned.astype(jnp.float32)).astype(jnp.bfloat16)
    return (attn_out, mixed)


def solution(mesh):
    chips = Mesh(mesh.devices.reshape(2, 2, 2, 4, 4, 2), ALL)
    return jax.shard_map(
        body,
        mesh=chips,
        in_specs=(
            P(None, ALL),
            P(None, ALL),
            P(None, ALL),
            P(),
            P(ALL, None),
            P(None, ALL),
            P(None, ALL),
            P(ALL, None),
        ),
        out_specs=(P(None, ALL), P(None, ALL)),
        check_vma=False,
    )
```

time: 205 us -> 181 us (0.88)
  waiting for transfers between devices: 116 us -> 96.9 us
  blocking collectives: 15.5 us -> 0 us
  starting transfers between devices: 22.4 us -> 32.8 us
  Pallas kernels: 33.2 us -> 31.1 us
    all_to_all x2 -> x0, blocking collectives: 13.7 us -> none  [over_cores(): return lax.all_to_all(value, 'c', split_axis=0, concat_axis=0, tiled=True)]
    ppermute x4 -> x9, waiting for transfers between devices: 62.6 us -> 49.6 us  [the longest x1 22.4 us: second_next_chip(): value = lax.ppermute(value, 'y', [(y, (y - 1) % ring) for y in range(ring)])]
    ppermute x4 -> x9, starting transfers between devices: 0.01 us -> 12.9 us  [the longest x4 7.28 us: to_sibling(): return lax.ppermute(value, 'c', [(0, 1), (1, 0)])]
    all_to_all x4 -> x2, waiting for transfers between devices: 53 us -> 47.3 us  [the longest x1 26.2 us: body(): lax.all_to_all(conv_out, OWNERS, split_axis=0, concat_axis=0, tiled=True)]
    squeeze x2 -> x0, local copies, waits for them, and re-layouts: 3.74 us -> none  [the longest x1 1.88 us: body(): v_far = next_chip(v_near[1])]
    unnamed x39 -> x38, local copies, waits for them, and re-layouts: 6.81 us -> 3.61 us
    dynamic_slice x0 -> x5, local copies, waits for them, and re-layouts: none -> 2.65 us  [pick_heads(): lax.dynamic_index_in_dim(pair, which, 1, keepdims=False).reshape(-1, tokens)]
    all_to_all x4 -> x2, starting transfers between devices: 22.4 us -> 19.8 us  [the longest x1 11.9 us: body(): lax.all_to_all(gated, CHIPS, split_axis=0, concat_axis=0, tiled=True)]
  transfers between devices with their start and end apart: 8 -> 11, of which waited for: 7 -> 8; matrix products, arithmetic and copies ran while one was open for 3% -> 5% of each run, Pallas kernels for 4% -> 10%
where the time goes in v1:
time: 181 us
  waiting for transfers between devices  96.9 us (54%)
  starting transfers between devices  32.8 us (18%)
  Pallas kernels  31.1 us (17%)
  local copies, waits for them, and re-layouts  11.9 us (7%)
  other arithmetic  7.22 us (4%)
    all_to_all x1, waiting for transfers between devices, body(): lax.all_to_all(conv_out, OWNERS, split_axis=0, concat_axis=0, tiled=True)  26.2 us
    ppermute x1, waiting for transfers between devices, second_next_chip(): value = lax.ppermute(value, 'y', [(y, (y - 1) % ring) for y in range(ring)])  22.4 us
    all_to_all x1, waiting for transfers between devices, body(): lax.all_to_all(gated, CHIPS, split_axis=0, concat_axis=0, tiled=True)  21.1 us
    ppermute x2, waiting for transfers between devices, send(): lax.ppermute(value, ALL, [(source, target(source) % count) for source in...  18.1 us
    pallas_call x1, Pallas kernels, convolve(): pl.pallas_call(conv_kernel, grid=(channels // step_channels,), in_specs=[...  13.4 us
    all_to_all x1, starting transfers between devices, body(): lax.all_to_all(gated, CHIPS, split_axis=0, concat_axis=0, tiled=True)  11.9 us
    pallas_call x1, Pallas kernels, attend(): pl.pallas_call(attend_kernel, grid_spec=pltpu.PrefetchScalarGridSpec(num_...  11.2 us
    all_to_all x1, starting transfers between devices, body(): lax.all_to_all(conv_out, OWNERS, split_axis=0, concat_axis=0, tiled=True)  7.96 us
  transfers between devices with their start and end apart: 11, of which 8 were waited for; matrix products, arithmetic and copies ran while one was open for 5% of the time, Pallas kernels for 10%

profile of v1, /device:TPU:1, one launch (start us, length us, event | category | flops | bytes accessed | tf_op | source)
XLA Modules:
  0.0 181.0 jit_solution(5786027770410546879)
XLA Ops:
  4.2 3.2 %collective-permute-start.1 = (bf16[2,2048,128]{2,1,0:T(8,128)(2,1)}, bf16[2,2048,128]{2,1,0:T(8,128)(2,1)S(1)}, u32[]{:S(2)}, u32[]{:S(2)}) collective-permute-start(bf16[2,2048,128]{2,1,0:T(8,128)(2,1)} %pad_maximum_fusion), channel_id=1, source_target_pairs={{0,1},{1,0},{2,3},{3,2},{4,5},{5,4},{6,7},{7,6},{8,9},{9,8},{10,11... | collective-permute-start | bytes 3145736 | tf_op jit(solution)/shard_map/ppermute | solution.py:315
  7.9 2.0 %collective-permute-done.1.sibling = bf16[2,2048,128]{2,1,0:T(8,128)(2,1)S(1)} collective-permute-done((bf16[2,2048,128]{2,1,0:T(8,128)(2,1)}, bf16[2,2048,128]{2,1,0:T(8,128)(2,1)S(1)}, u32[]{:S(2)}, u32[]{:S(2)}) %collective-permute-start.1) | collective-permute-done | bytes 1048608 | tf_op jit(solution)/shard_map/ppermute | solution.py:315
  9.9 1.2 pad_maximum_fusion.1
  13.5 22.4 %collective-permute-done.3 = bf16[2,2048,128]{2,1,0:T(8,128)(2,1)} collective-permute-done((bf16[2,2048,128]{2,1,0:T(8,128)(2,1)}, bf16[2,2048,128]{2,1,0:T(8,128)(2,1)}, u32[]{:S(2)}, u32[]{:S(2)}) %collective-permute-start.3) | collective-permute-done | bytes 1048608 | tf_op jit(solution)/shard_map/ppermute | solution.py:308
  35.9 2.2 %collective-permute-start.4 = (bf16[2,2048,128]{2,1,0:T(8,128)(2,1)}, bf16[2,2048,128]{2,1,0:T(8,128)(2,1)}, u32[]{:S(2)}, u32[]{:S(2)}) collective-permute-start(bf16[2,2048,128]{2,1,0:T(8,128)(2,1)} %collective-permute-done.3), channel_id=1, source_target_pairs={{6,4},{7,5},{0,6},{1,7},{2,8},{3,9},{4,10},{5,11},{14,12},{15,13},... | collective-permute-start | bytes 3145736 | tf_op jit(solution)/shard_map/ppermute | solution.py:309
  39.9 1.4 constant_dynamic-slice_fusion
  41.4 1.6 collective-permute-start.2
  44.1 18.1 %collective-permute-done.5.near = bf16[2,2048,128]{2,1,0:T(8,128)(2,1)} collective-permute-done((bf16[2,2048,128]{2,1,0:T(8,128)(2,1)S(1)}, bf16[2,2048,128]{2,1,0:T(8,128)(2,1)}, u32[]{:S(2)}, u32[]{:S(2)}) %collective-permute-start.5) | collective-permute-done | bytes 1048608 | tf_op jit(solution)/shard_map/ppermute | solution.py:290
  62.2 3.4 %collective-permute-done.4.far = bf16[2,2048,128]{2,1,0:T(8,128)(2,1)} collective-permute-done((bf16[2,2048,128]{2,1,0:T(8,128)(2,1)}, bf16[2,2048,128]{2,1,0:T(8,128)(2,1)}, u32[]{:S(2)}, u32[]{:S(2)}) %collective-permute-start.4) | collective-permute-done | bytes 1048608 | tf_op jit(solution)/shard_map/ppermute | solution.py:309
  65.6 1.9 %collective-permute-start.8 = (bf16[16,256,128]{2,1,0:T(8,128)(2,1)}, bf16[16,256,128]{2,1,0:T(8,128)(2,1)}, u32[]{:S(2)}, u32[]{:S(2)}) collective-permute-start(bf16[16,256,128]{2,1,0:T(8,128)(2,1)} %bitcast.44), channel_id=1, source_target_pairs={{1,32},{3,34},{5,36},{7,38},{9,40},{11,42},{13,44},{15,46},{17,48}... | collective-permute-start | bytes 3145736 | tf_op jit(solution)/shard_map/ppermute | solution.py:354
  68.5 11.2 %attend.1 = (bf16[2048,128]{1,0:T(8,128)(2,1)}, bf16[2048,128]{1,0:T(8,128)(2,1)}, bf16[128,2,16,128]{3,2,1,0:T(8,128)(2,1)}) custom-call(s32[1]{0:T(128)} %bitcast.core_ref, f32[640,256]{1,0:T(8,128)} %and_select_fusion.bias_ref, bf16[4096,128]{1,0:T(8,128)(2,1)} %q_mine.1, bf16[4096,128]{1,0:T(8,128)(2,1)} %gate_mine.1, bf16[2,2048,128]{2,1,0:T(8,128)(2,1)} %copy-done.10, ...), custom_call_target="tpu_custom_call" | custom-call | flops 1342177280 | bytes 10092544 | tf_op jit(solution)/shard_map/attend/pallas_call | solution.py:231
  79.7 2.3 %collective-permute-done.8 = bf16[16,256,128]{2,1,0:T(8,128)(2,1)} collective-permute-done((bf16[16,256,128]{2,1,0:T(8,128)(2,1)}, bf16[16,256,128]{2,1,0:T(8,128)(2,1)}, u32[]{:S(2)}, u32[]{:S(2)}) %collective-permute-start.8) | collective-permute-done | bytes 1048608 | tf_op jit(solution)/shard_map/ppermute | solution.py:354
  82.0 11.9 %all-to-all-start = ((bf16[128,2,16,128]{3,2,1,0:T(8,128)(2,1)}), bf16[128,2,16,128]{3,2,1,0:T(8,128)(2,1)}, u32[]{:S(2)}, u32[]{:S(2)}) async-start(bf16[128,2,16,128]{3,2,1,0:T(8,128)(2,1)} %get-tuple-element.30), calls=%async_computation | async-start | bytes 2097152 | tf_op jit(solution)/shard_map/all_to_all | solution.py:362
  93.9 1.4 broadcast_select_fusion.filter_ref
  95.4 6.5 %filter_spectrum.1.spectrum_ref = f32[4096,256]{1,0:T(8,128)} custom-call(bf16[16,256,128]{2,1,0:T(8,128)(2,1)S(1)} %broadcast_select_fusion.filter_ref, bf16[512,512]{1,0:T(8,128)(2,1)S(1)} %copy-done.3, f32[256,128]{1,0:T(8,128)S(1)} %copy-done.7, f32[256,128]{1,0:T(8,128)S(1)} %copy-done.6, bf16[768,256]{1,0:T(8,128)(2,1)S(1)} %copy-done.4), custom_call_target="tpu_custom_call" | custom-call | flops 2720000000 | bytes 6291456 | tf_op jit(solution)/shard_map/filter_spectrum/pallas_call | solution.py:131
  101.9 21.1 %all-to-all-done = bf16[128,2,16,128]{3,2,1,0:T(8,128)(2,1)} async-done(((bf16[128,2,16,128]{3,2,1,0:T(8,128)(2,1)}), bf16[128,2,16,128]{3,2,1,0:T(8,128)(2,1)}, u32[]{:S(2)}, u32[]{:S(2)}) %all-to-all-start) | async-done | bytes 1048608 | tf_op jit(solution)/shard_map/all_to_all | solution.py:362
  123.0 2.2 %copy.53 = bf16[128,2,16,128]{3,1,0,2:T(2,128)(2,1)S(1)} copy(bf16[128,2,16,128]{3,2,1,0:T(8,128)(2,1)} %all-to-all-done) | data formatting | bytes 2097152 | tf_op jit(solution)/shard_map/all_to_all | solution.py:362
  125.3 13.4 %convolve.1 = bf16[16,256,128]{2,1,0:T(8,128)(2,1)S(1)} custom-call(bf16[16,256,128]{2,1,0:T(8,128)(2,1)S(1)} %bitcast.57, f32[4096,256]{1,0:T(8,128)} %filter_spectrum.1.spectrum_ref, bf16[512,512]{1,0:T(8,128)(2,1)S(1)} %copy-done.2, f32[256,128]{1,0:T(8,128)S(1)} %copy-done.7, f32[256,128]{1,0:T(8,128)S(1)} %copy-done.6, bf16[768,256]{1,0:T(8,128)(2,1)S(1)} %copy-done.4, ...), custom_call_target="tpu_custom_call" | custom-call | flops 5920000000 | bytes 8388608 | tf_op jit(solution)/shard_map/convolve/pallas_call | solution.py:151
  138.7 1.6 copy.54
  140.3 8.0 %all-to-all-start.1 = ((bf16[256,16,128]{2,1,0:T(8,128)(2,1)}), bf16[256,16,128]{2,1,0:T(8,128)(2,1)S(1)}, u32[]{:S(2)}, u32[]{:S(2)}) async-start(bf16[256,16,128]{2,1,0:T(8,128)(2,1)} %copy.54), calls=%async_computation.1 | async-start | bytes 2097152 | tf_op jit(solution)/shard_map/all_to_all | solution.py:374
  148.3 2.4 %collective-permute-start.7 = (bf16[2048,128]{1,0:T(8,128)(2,1)S(1)}, bf16[2048,128]{1,0:T(8,128)(2,1)S(1)}, u32[]{:S(2)}, u32[]{:S(2)}) collective-permute-start(bf16[2048,128]{1,0:T(8,128)(2,1)S(1)} %copy-done.16), channel_id=1, source_target_pairs={{0,1},{1,0},{2,3},{3,2},{4,5},{5,4},{6,7},{7,6},{8,9},{9,8},{10,11... | collective-permute-start | bytes 1572872 | tf_op jit(solution)/shard_map/ppermute | solution.py:315
  150.7 1.5 collective-permute-done.7
  153.5 26.2 %all-to-all-done.1 = bf16[256,16,128]{2,1,0:T(8,128)(2,1)S(1)} async-done(((bf16[256,16,128]{2,1,0:T(8,128)(2,1)}), bf16[256,16,128]{2,1,0:T(8,128)(2,1)S(1)}, u32[]{:S(2)}, u32[]{:S(2)}) %all-to-all-start.1) | async-done | bytes 1048608 | tf_op jit(solution)/shard_map/all_to_all | solution.py:374
  179.7 1.3 fusion
  (72 shorter events, 11.6 us)
Async XLA Ops:
  1.9 5.5 %copy-start.17 = (s32[1,3]{1,0:T(1,128)S(1)}, s32[1,3]{1,0:T(1,128)}, u32[]{:S(2)}) copy-start(s32[1,3]{1,0:T(1,128)} %param.19) | copy-start | bytes 40
  1.9 5.8 %copy-start.15 = (s32[256]{0:T(256)S(1)}, s32[256]{0:T(256)}, u32[]{:S(2)}) copy-start(s32[256]{0:T(256)} %param.18) | copy-start | bytes 3076
  1.9 5.9 %copy-start.13 = (bf16[4096,128]{1,0:T(8,128)(2,1)S(1)}, bf16[4096,128]{1,0:T(8,128)(2,1)}, u32[]{:S(2)}) copy-start(bf16[4096,128]{1,0:T(8,128)(2,1)} %param.16) | copy-start | bytes 3145732
  4.2 5.7 %collective-permute-start.1 = (bf16[2,2048,128]{2,1,0:T(8,128)(2,1)}, bf16[2,2048,128]{2,1,0:T(8,128)(2,1)S(1)}, u32[]{:S(2)}, u32[]{:S(2)}) collective-permute-start(bf16[2,2048,128]{2,1,0:T(8,128)(2,1)} %pad_maximum_fusion), channel_id=1, source_target_pairs={{0,1},{1,0},{2,3},{3,2},{4,5},{5,4},{6,7},{7,6},{8,9},{9,8},{10,11... | collective-permute-start | bytes 3145736 | tf_op jit(solution)/shard_map/ppermute | solution.py:315
  7.4 60.1 %collective-permute-start.6 = (bf16[2,2048,128]{2,1,0:T(8,128)(2,1)}, bf16[2,2048,128]{2,1,0:T(8,128)(2,1)}, u32[]{:S(2)}, u32[]{:S(2)}) collective-permute-start(bf16[2,2048,128]{2,1,0:T(8,128)(2,1)} %pad_maximum_fusion), channel_id=1, source_target_pairs={{0,3},{1,2},{2,5},{3,4},{4,7},{5,6},{6,9},{7,8},{8,11},{9,10},{10,... | collective-permute-start | bytes 3145736 | tf_op jit(solution)/shard_map/ppermute | solution.py:290
  7.4 5.3 %collective-permute-start = (f32[1,3]{1,0:T(1,128)S(1)}, f32[1,3]{1,0:T(1,128)S(1)}, u32[]{:S(2)}, u32[]{:S(2)}) collective-permute-start(f32[1,3]{1,0:T(1,128)S(1)} %convert_element_type.39), channel_id=1, source_target_pairs={{0,1},{1,0},{2,3},{3,2},{4,5},{5,4},{6,7},{7,6},{8,9},{9,8},{10,11... | collective-permute-start | bytes 44 | tf_op jit(solution)/shard_map/ppermute | solution.py:315
  11.2 30.1 %copy-start.9 = (bf16[2,2048,128]{2,1,0:T(8,128)(2,1)}, bf16[2,2048,128]{2,1,0:T(8,128)(2,1)S(1)}, u32[]{:S(2)}) copy-start(bf16[2,2048,128]{2,1,0:T(8,128)(2,1)S(1)} %get-tuple-element.41.own) | copy-start | bytes 3145732
  11.2 24.7 %collective-permute-start.3 = (bf16[2,2048,128]{2,1,0:T(8,128)(2,1)}, bf16[2,2048,128]{2,1,0:T(8,128)(2,1)}, u32[]{:S(2)}, u32[]{:S(2)}) collective-permute-start(bf16[2,2048,128]{2,1,0:T(8,128)(2,1)} %get-tuple-element.42), channel_id=1, source_target_pairs={{0,6},{2,0},{4,2},{6,4},{1,7},{3,1},{5,3},{7,5},{8,14},{10,8},{12,... | collective-permute-start | bytes 3145736 | tf_op jit(solution)/shard_map/ppermute | solution.py:308
  13.0 49.2 %collective-permute-start.5 = (bf16[2,2048,128]{2,1,0:T(8,128)(2,1)S(1)}, bf16[2,2048,128]{2,1,0:T(8,128)(2,1)}, u32[]{:S(2)}, u32[]{:S(2)}) collective-permute-start(bf16[2,2048,128]{2,1,0:T(8,128)(2,1)S(1)} %get-tuple-element.41.own), channel_id=1, source_target_pairs={{0,2},{1,3},{2,4},{3,5},{4,6},{5,7},{6,8},{7,9},{8,10},{9,11},{10,... | collective-permute-start | bytes 3145736 | tf_op jit(solution)/shard_map/ppermute | solution.py:290
  35.9 29.6 %collective-permute-start.4 = (bf16[2,2048,128]{2,1,0:T(8,128)(2,1)}, bf16[2,2048,128]{2,1,0:T(8,128)(2,1)}, u32[]{:S(2)}, u32[]{:S(2)}) collective-permute-start(bf16[2,2048,128]{2,1,0:T(8,128)(2,1)} %collective-permute-done.3), channel_id=1, source_target_pairs={{6,4},{7,5},{0,6},{1,7},{2,8},{3,9},{4,10},{5,11},{14,12},{15,13},... | collective-permute-start | bytes 3145736 | tf_op jit(solution)/shard_map/ppermute | solution.py:309
  39.9 3.1 %copy-start.12 = (bf16[16,32768]{1,0:T(8,128)(2,1)S(1)}, bf16[16,32768]{1,0:T(8,128)(2,1)}, u32[]{:S(2)}) copy-start(bf16[16,32768]{1,0:T(8,128)(2,1)} %param.22) | copy-start | bytes 3145732
  41.4 26.1 %collective-permute-start.2 = (bf16[2,2048,128]{2,1,0:T(8,128)(2,1)S(1)}, bf16[2,2048,128]{2,1,0:T(8,128)(2,1)S(1)}, u32[]{:S(2)}, u32[]{:S(2)}) collective-permute-start(bf16[2,2048,128]{2,1,0:T(8,128)(2,1)S(1)} %pad_maximum_fusion.2), channel_id=1, source_target_pairs={{0,1},{1,0},{2,3},{3,2},{4,5},{5,4},{6,7},{7,6},{8,9},{9,8},{10,11... | collective-permute-start | bytes 3145736 | tf_op jit(solution)/shard_map/ppermute | solution.py:315
  65.6 16.4 %collective-permute-start.8 = (bf16[16,256,128]{2,1,0:T(8,128)(2,1)}, bf16[16,256,128]{2,1,0:T(8,128)(2,1)}, u32[]{:S(2)}, u32[]{:S(2)}) collective-permute-start(bf16[16,256,128]{2,1,0:T(8,128)(2,1)} %bitcast.44), channel_id=1, source_target_pairs={{1,32},{3,34},{5,36},{7,38},{9,40},{11,42},{13,44},{15,46},{17,48}... | collective-permute-start | bytes 3145736 | tf_op jit(solution)/shard_map/ppermute | solution.py:354
  82.0 41.1 %all-to-all-start = ((bf16[128,2,16,128]{3,2,1,0:T(8,128)(2,1)}), bf16[128,2,16,128]{3,2,1,0:T(8,128)(2,1)}, u32[]{:S(2)}, u32[]{:S(2)}) async-start(bf16[128,2,16,128]{3,2,1,0:T(8,128)(2,1)} %get-tuple-element.30), calls=%async_computation | async-start | bytes 2097152 | tf_op jit(solution)/shard_map/all_to_all | solution.py:362
  93.8 1.5 copy-start.3
  93.9 1.5 copy-start.7
  101.9 23.4 %copy-start.1 = (bf16[256,1536]{1,0:T(8,128)(2,1)S(1)}, bf16[256,1536]{1,0:T(8,128)(2,1)}, u32[]{:S(2)}) copy-start(bf16[256,1536]{1,0:T(8,128)(2,1)} %constant.91.clone.first_back) | copy-start | bytes 2359300
  101.9 23.4 %copy-start.2 = (bf16[512,512]{1,0:T(8,128)(2,1)S(1)}, bf16[512,512]{1,0:T(8,128)(2,1)}, u32[]{:S(2)}) copy-start(bf16[512,512]{1,0:T(8,128)(2,1)} %constant.89.clone.first) | copy-start | bytes 1572868
  101.9 23.4 %copy-start.5 = (bf16[768,256]{1,0:T(8,128)(2,1)S(1)}, bf16[768,256]{1,0:T(8,128)(2,1)}, u32[]{:S(2)}) copy-start(bf16[768,256]{1,0:T(8,128)(2,1)} %constant.90.clone.second_back) | copy-start | bytes 1179652
  138.7 9.6 %copy-start.16 = (bf16[2048,128]{1,0:T(8,128)(2,1)S(1)}, bf16[2048,128]{1,0:T(8,128)(2,1)}, u32[]{:S(2)}) copy-start(bf16[2048,128]{1,0:T(8,128)(2,1)} %get-tuple-element.27) | copy-start | bytes 1572868
  138.7 13.5 %copy-start.14 = (bf16[2048,128]{1,0:T(8,128)(2,1)S(1)}, bf16[2048,128]{1,0:T(8,128)(2,1)}, u32[]{:S(2)}) copy-start(bf16[2048,128]{1,0:T(8,128)(2,1)} %get-tuple-element.26) | copy-start | bytes 1572868
  140.3 39.3 %all-to-all-start.1 = ((bf16[256,16,128]{2,1,0:T(8,128)(2,1)}), bf16[256,16,128]{2,1,0:T(8,128)(2,1)S(1)}, u32[]{:S(2)}, u32[]{:S(2)}) async-start(bf16[256,16,128]{2,1,0:T(8,128)(2,1)} %copy.54), calls=%async_computation.1 | async-start | bytes 2097152 | tf_op jit(solution)/shard_map/all_to_all | solution.py:374
  148.3 3.9 %collective-permute-start.7 = (bf16[2048,128]{1,0:T(8,128)(2,1)S(1)}, bf16[2048,128]{1,0:T(8,128)(2,1)S(1)}, u32[]{:S(2)}, u32[]{:S(2)}) collective-permute-start(bf16[2048,128]{1,0:T(8,128)(2,1)S(1)} %copy-done.16), channel_id=1, source_target_pairs={{0,1},{1,0},{2,3},{3,2},{4,5},{5,4},{6,7},{7,6},{8,9},{9,8},{10,11... | collective-permute-start | bytes 1572872 | tf_op jit(solution)/shard_map/ppermute | solution.py:315
  152.3 27.3 %copy-start.11 = (bf16[4096,128]{1,0:T(8,128)(2,1)S(1)}, bf16[4096,128]{1,0:T(8,128)(2,1)}, u32[]{:S(2)}) copy-start(bf16[4096,128]{1,0:T(8,128)(2,1)} %param.21) | copy-start | bytes 3145732
  (5 other events, 6.5 us)

commit v2 on v1

--- a/solution.py
+++ b/solution.py
@@ -66,10 +66,20 @@
     return real * cosine - imag * sine, real * sine + imag * cosine
 
 
+def interleaved(tasks, lag=1):
+    waiting, active, turn = list(tasks), [], 0
+    while waiting or active:
+        if waiting and turn % lag == 0:
+            active.append(waiting.pop(0))
+        active = [task for task in active if next(task, None) is not None]
+        turn += 1
+
+
 def forward(signals, first, cosine, sine, second):
     rows, width = signals[0].shape
     signal = jnp.concatenate(signals, axis=1)
     part = dot(first, jnp.concatenate([signal, signal], axis=0))
+    yield part
     turned = []
     for channel in range(2):
         lanes = slice(channel * width, (channel + 1) * width)
@@ -77,47 +87,81 @@
             jnp.concatenate(turned_by(part[:rows, lanes], part[rows:, lanes], cosine, sine), axis=1)
         )
     high, low = split(jnp.concatenate(turned, axis=0))
-    return dot(jnp.concatenate([high, low, high], axis=1), second)
-
-
-def filter_kernel(filter_ref, first, cosine, sine, second, out_ref):
-    for pair in range(filter_ref.shape[0] // 2):
-        signals = [filter_ref[2 * pair], filter_ref[2 * pair + 1]]
-        rows = signals[0].shape[0]
-        out_ref[2 * rows * pair : 2 * rows * (pair + 1)] = forward(
-            signals, first[...], cosine[...], sine[...], second[...]
-        )
-
-
-def conv_kernel(
-    signal_ref, spectrum_ref, first, cosine_ref, sine_ref, second, second_back, first_back, out_ref
+    yield dot(jnp.concatenate([high, low, high], axis=1), second)
+
+
+def filter_task(pair, filter_ref, first, cosine, sine, second, out_ref):
+    signals = [filter_ref[2 * pair], filter_ref[2 * pair + 1]]
+    rows = signals[0].shape[0]
+    for spectrum in forward(signals, first[...], cosine[...], sine[...], second[...]):
+        yield True
+    out_ref[2 * rows * pair : 2 * rows * (pair + 1)] = spectrum
+
+
+def filter_kernel(filter_ref, *rest):
+    pairs = filter_ref.shape[0] // 2
+    interleaved([filter_task(pair, filter_ref, *rest) for pair in range(pairs)])
+
+
+def conv_task(
+    channel, place, rows, load, store, spectrum_ref, first, cosine_ref, sine_ref, second, second_back, first_back
 ):
-    rows, width = signal_ref.shape[1:]
+    width = cosine_ref.shape[1]
     cosine, sine = cosine_ref[...], sine_ref[...]
-    for pair in range(signal_ref.shape[0] // 2):
-        signals = [signal_ref[2 * pair], signal_ref[2 * pair + 1]]
-        spectrum = forward(signals, first[...], cosine, sine, second[...])
-        other = spectrum_ref[2 * rows * pair : 2 * rows * (pair + 1)]
-        product = jnp.concatenate(
-            turned_by(spectrum[:, :width], spectrum[:, width:], other[:, :width], other[:, width:]),
-            axis=1,
-        )
-        high, low = split(product)
-        part = dot(jnp.concatenate([high, low, high], axis=1), second_back[...])
-        reals, imags = [], []
-        for channel in range(2):
-            block = part[channel * rows : (channel + 1) * rows]
-            real, imag = turned_by(block[:, :width], block[:, width:], cosine, -sine)
-            reals.append(real)
-            imags.append(imag)
-        turned = jnp.concatenate(
-            [jnp.concatenate(reals, axis=1), jnp.concatenate(imags, axis=1)], axis=0
-        )
-        high, low = split(turned)
-        result = dot(first_back[...], jnp.concatenate([high, low, high], axis=0))
-        result = result.astype(jnp.bfloat16)
-        out_ref[2 * pair] = result[:, :width]
-        out_ref[2 * pair + 1] = result[:, width:]
+    signals = [load(channel), load(channel + 1)]
+    for spectrum in forward(signals, first[...], cosine, sine, second[...]):
+        yield True
+    other = spectrum_ref[rows * place : rows * (place + 2)]
+    product = jnp.concatenate(
+        turned_by(spectrum[:, :width], spectrum[:, width:], other[:, :width], other[:, width:]),
+        axis=1,
+    )
+    high, low = split(product)
+    part = dot(jnp.concatenate([high, low, high], axis=1), second_back[...])
+    yield True
+    reals, imags = [], []
+    for half in range(2):
+        block = part[half * rows : (half + 1) * rows]
+        real, imag = turned_by(block[:, :width], block[:, width:], cosine, -sine)
+        reals.append(real)
+        imags.append(imag)
+    turned = jnp.concatenate(
+        [jnp.concatenate(reals, axis=1), jnp.concatenate(imags, axis=1)], axis=0
+    )
+    high, low = split(turned)
+    result = dot(first_back[...], jnp.concatenate([high, low, high], axis=0))
+    yield True
+    store(channel, result[:, :width])
+    store(channel + 1, result[:, width:])
+
+
+def conv_kernel(signal_ref, spectrum_ref, *rest):
+    *tables, out_ref, taken, given = rest
+    rows, channels, width = signal_ref.shape
+    here = spectrum_ref.shape[0] // rows
+    step = pl.program_id(0)
+    base = step * here
+
+    @pl.when(step == 0)
+    def _():
+        taken[...] = signal_ref[...].astype(jnp.float32).reshape(taken.shape)
+
+    def load(channel):
+        return taken[pl.ds(base + channel, rows, stride=channels), :].astype(jnp.bfloat16)
+
+    def store(channel, value):
+        given[pl.ds(base + channel, rows, stride=channels), :] = value
+
+    interleaved(
+        [
+            conv_task(channel, channel, rows, load, store, spectrum_ref, *tables)
+            for channel in range(0, here, 2)
+        ]
+    )
+
+    @pl.when(step == pl.num_programs(0) - 1)
+    def _():
+        out_ref[...] = given[...].reshape(out_ref.shape).astype(jnp.bfloat16)
 
 
 def whole(array):
@@ -143,21 +187,21 @@
     )(taps, *constants)
 
 
-def convolve(signal, spectrum, tables, step_channels=4):
+def convolve(signal, spectrum, tables, step_channels=8):
     _, first, twist, second, second_back, first_back = tables
-    channels, rows, width = signal.shape
+    rows, channels, width = signal.shape
     constants = [jnp.asarray(entry) for entry in (first, *twist, second, second_back, first_back)]
-    block = pl.BlockSpec((step_channels, rows, width), lambda step: (step, 0, 0))
     return pl.pallas_call(
         conv_kernel,
         grid=(channels // step_channels,),
         in_specs=[
-            block,
+            whole(signal),
             pl.BlockSpec((step_channels * rows, 2 * width), lambda step: (step, 0)),
         ]
         + [whole(entry) for entry in constants],
-        out_specs=block,
+        out_specs=whole(signal),
         out_shape=jax.ShapeDtypeStruct(signal.shape, jnp.bfloat16),
+        scratch_shapes=[pltpu.VMEM((rows * channels, width), jnp.float32)] * 2,
         compiler_params=pltpu.CompilerParams(vmem_limit_bytes=VMEM_LIMIT),
         cost_estimate=pl.CostEstimate(
             flops=channels * 370_000_000, bytes_accessed=8 * 1024 * 1024, transcendentals=0
@@ -193,35 +237,54 @@
     out_other,
     gated,
 ):
-    heads, tokens = q_mine.shape[0] // HD, q_mine.shape[1]
+    heads, tokens = gate_other.shape[0] // HD, gate_other.shape[1]
     group = gated.shape[2]
     core = core_ref[0]
     pairs = (far, near, crossed, own, sibling)
-    for head in range(heads):
-        rows = slice(head * HD, (head + 1) * HD)
-        queries = jnp.concatenate([q_mine[rows], q_other[rows]], axis=1)
+    part_heads = q_mine.shape[1] // HD
+
+    def rows_of(head):
+        return slice(head * HD, (head + 1) * HD)
+
+    def own_rows(ref, head):
+        return ref[head // part_heads, rows_of(head % part_heads)]
+
+    def task(head):
+        rows = rows_of(head)
+        queries = jnp.concatenate([own_rows(q_mine, head), q_other[rows]], axis=1)
         keys = jnp.concatenate([pair[0, rows] for pair in pairs], axis=1)
         scores = lax.dot_general(
             keys, queries, (((0,), (0,)), ((), ())), preferred_element_type=jnp.float32
         )
+        yield True
         masked = scores * (math.log2(math.e) / math.sqrt(HD)) + bias_ref[...]
         weights = jnp.exp2(masked - jnp.max(masked, axis=0, keepdims=True))
         total = jnp.sum(weights, axis=0, keepdims=True)
+        weights = weights.astype(jnp.bfloat16)
+        yield True
         values = jnp.concatenate([pair[1, rows] for pair in pairs], axis=1)
-        mixed = (dot(values, weights.astype(jnp.bfloat16)) / total).astype(jnp.bfloat16)
-        gates = ((out_mine, gate_mine, core), (out_other, gate_other, 1 - core))
+        mixed = (dot(values, weights) * (1.0 / total)).astype(jnp.bfloat16)
+        gates = (
+            (out_mine, own_rows(gate_mine, head), core),
+            (out_other, gate_other[rows], 1 - core),
+        )
         for place, (out, gate, block) in enumerate(gates):
             part = mixed[:, place * tokens : (place + 1) * tokens]
             out[rows] = part
-            product = (part.astype(jnp.float32) * gate[rows].astype(jnp.float32)).astype(jnp.bfloat16)
+            product = (part.astype(jnp.float32) * gate.astype(jnp.float32)).astype(jnp.bfloat16)
             owners = slice(head * HD // group, (head + 1) * HD // group)
             gated[owners, block] = product.reshape(HD // group, group, tokens)
 
-
-def attend(core, bias, q_proj, gate, exchanged, blocks, group):
+    interleaved([task(head) for head in range(heads)])
+
+
+def attend(core, bias, q_proj, gate, exchanged, blocks, group, steps=2):
     channels, tokens = q_proj.shape[0] // 2, q_proj.shape[1]
-    step_rows = channels // STEPS
-    half = pl.BlockSpec((step_rows, tokens), lambda step, core: (2 * step + core[0], 0))
+    step_rows = channels // steps
+    halves = [value.reshape(STEPS, 2, channels // STEPS, tokens) for value in (q_proj, gate)]
+    half = pl.BlockSpec(
+        (STEPS // steps, None, channels // STEPS, tokens), lambda step, core: (step, core[0], 0, 0)
+    )
     single = pl.BlockSpec((step_rows, tokens), lambda step, core: (step, 0))
     pair = pl.BlockSpec((2, step_rows, tokens), lambda step, core: (0, step, 0))
     pieces = [
@@ -232,7 +295,7 @@
         attend_kernel,
         grid_spec=pltpu.PrefetchScalarGridSpec(
             num_scalar_prefetch=1,
-            grid=(STEPS,),
+            grid=(steps,),
             in_specs=[pl.BlockSpec(bias.shape, lambda step, core: (0, 0)), half, half, *pieces]
             + [pair] * 5,
             out_specs=[
@@ -253,7 +316,7 @@
             transcendentals=(channels // HD) * bias.size,
         ),
         name="attend",
-    )(core.reshape(1), bias, q_proj, gate, exchanged, exchanged, *blocks)
+    )(core.reshape(1), bias, *halves, exchanged, exchanged, *blocks)
 
 
 def chip_bias(block_start, flags, key_ids, query_ids, tokens):
@@ -369,8 +432,7 @@
         axis=1,
     ).reshape(channels, tokens)
 
-    signal = gathered.reshape(devices, group, tokens).transpose(1, 0, 2)
-    conv_out = convolve(signal, spectrum, tables).transpose(1, 0, 2)
+    conv_out = convolve(gathered.reshape(devices, group, tokens), spectrum, tables)
     returned = lax.all_to_all(
         conv_out, OWNERS, split_axis=0, concat_axis=0, tiled=True
     ).reshape(channels, tokens)

time: 181 us -> 179 us (0.989)
  Pallas kernels: 31.1 us -> 25.8 us
  waiting for transfers between devices: 96.9 us -> 101 us
    ppermute x1, waiting for transfers between devices: 2.28 us -> 5.76 us  [body(): swapped = lax.ppermute(taps, ALL, moved)]
    pallas_call x1, Pallas kernels: 11.2 us -> 7.75 us  [attend(): pl.pallas_call(attend_kernel, grid_spec=pltpu.PrefetchScalarGridSpec(num_...]
    unnamed x38 -> x42, local copies, waits for them, and re-layouts: 3.61 us -> 6.55 us
    all_to_all x1 -> x0, local copies, waits for them, and re-layouts: 2.23 us -> none  [body(): lax.all_to_all(gated, CHIPS, split_axis=0, concat_axis=0, tiled=True)]
    pallas_call x1, Pallas kernels: 13.4 us -> 11.5 us  [convolve(): pl.pallas_call(conv_kernel, grid=(channels // step_channels,), in_specs=[...]
  transfers between devices with their start and end apart: 11 -> 11, of which waited for: 8 -> 8; matrix products, arithmetic and copies ran while one was open for 5% -> 5% of each run, Pallas kernels for 10% -> 8%
where the time goes in v2:
time: 179 us; the launch traced here: 178 us
  waiting for transfers between devices  101 us (56%)
  starting transfers between devices  32.4 us (18%)
  Pallas kernels  25.8 us (14%)
  local copies, waits for them, and re-layouts  11 us (6%)
  other arithmetic  7.24 us (4%)
    all_to_all x1, waiting for transfers between devices, body(): lax.all_to_all(conv_out, OWNERS, split_axis=0, concat_axis=0, tiled=True)  26.2 us
    ppermute x1, waiting for transfers between devices, second_next_chip(): value = lax.ppermute(value, 'y', [(y, (y - 1) % ring) for y in range(ring)])  22.4 us
    all_to_all x1, waiting for transfers between devices, body(): lax.all_to_all(gated, CHIPS, split_axis=0, concat_axis=0, tiled=True)  21.5 us
    ppermute x2, waiting for transfers between devices, send(): lax.ppermute(value, ALL, [(source, target(source) % count) for source in...  18.1 us
    pallas_call x1, Pallas kernels, convolve(): pl.pallas_call(conv_kernel, grid=(channels // step_channels,), in_specs=[...  11.5 us
    all_to_all x1, starting transfers between devices, body(): lax.all_to_all(gated, CHIPS, split_axis=0, concat_axis=0, tiled=True)  11.3 us
    all_to_all x1, starting transfers between devices, body(): lax.all_to_all(conv_out, OWNERS, split_axis=0, concat_axis=0, tiled=True)  8.09 us
    pallas_call x1, Pallas kernels, attend(): pl.pallas_call(attend_kernel, grid_spec=pltpu.PrefetchScalarGridSpec(num_...  7.75 us
  transfers between devices with their start and end apart: 11, of which 8 were waited for; matrix products, arithmetic and copies ran while one was open for 5% of the time, Pallas kernels for 8%

profile of v2, /device:TPU:1, one launch (start us, length us, event | category | flops | bytes accessed | tf_op | source)
XLA Modules:
  0.0 178.1 jit_solution(1377921255794509396)
XLA Ops:
  0.7 1.2 copy-done
  4.2 3.2 %collective-permute-start.1 = (bf16[2,2048,128]{2,1,0:T(8,128)(2,1)}, bf16[2,2048,128]{2,1,0:T(8,128)(2,1)S(1)}, u32[]{:S(2)}, u32[]{:S(2)}) collective-permute-start(bf16[2,2048,128]{2,1,0:T(8,128)(2,1)} %pad_maximum_fusion), channel_id=1, source_target_pairs={{0,1},{1,0},{2,3},{3,2},{4,5},{5,4},{6,7},{7,6},{8,9},{9,8},{10,11... | collective-permute-start | bytes 3145736 | tf_op jit(solution)/shard_map/ppermute | solution.py:378
  7.9 2.0 %collective-permute-done.1.sibling = bf16[2,2048,128]{2,1,0:T(8,128)(2,1)S(1)} collective-permute-done((bf16[2,2048,128]{2,1,0:T(8,128)(2,1)}, bf16[2,2048,128]{2,1,0:T(8,128)(2,1)S(1)}, u32[]{:S(2)}, u32[]{:S(2)}) %collective-permute-start.1) | collective-permute-done | bytes 1048608 | tf_op jit(solution)/shard_map/ppermute | solution.py:378
  9.9 1.2 pad_maximum_fusion.1
  13.5 22.4 %collective-permute-done.3 = bf16[2,2048,128]{2,1,0:T(8,128)(2,1)} collective-permute-done((bf16[2,2048,128]{2,1,0:T(8,128)(2,1)}, bf16[2,2048,128]{2,1,0:T(8,128)(2,1)}, u32[]{:S(2)}, u32[]{:S(2)}) %collective-permute-start.3) | collective-permute-done | bytes 1048608 | tf_op jit(solution)/shard_map/ppermute | solution.py:371
  35.9 2.2 %collective-permute-start.4 = (bf16[2,2048,128]{2,1,0:T(8,128)(2,1)}, bf16[2,2048,128]{2,1,0:T(8,128)(2,1)}, u32[]{:S(2)}, u32[]{:S(2)}) collective-permute-start(bf16[2,2048,128]{2,1,0:T(8,128)(2,1)} %collective-permute-done.3), channel_id=1, source_target_pairs={{6,4},{7,5},{0,6},{1,7},{2,8},{3,9},{4,10},{5,11},{14,12},{15,13},... | collective-permute-start | bytes 3145736 | tf_op jit(solution)/shard_map/ppermute | solution.py:372
  39.9 1.4 constant_dynamic-slice_fusion
  41.4 1.6 collective-permute-start.2
  43.0 1.2 copy.46
  44.1 18.1 %collective-permute-done.5.near = bf16[2,2048,128]{2,1,0:T(8,128)(2,1)} collective-permute-done((bf16[2,2048,128]{2,1,0:T(8,128)(2,1)S(1)}, bf16[2,2048,128]{2,1,0:T(8,128)(2,1)}, u32[]{:S(2)}, u32[]{:S(2)}) %collective-permute-start.5) | collective-permute-done | bytes 1048608 | tf_op jit(solution)/shard_map/ppermute | solution.py:353
  62.2 3.4 %collective-permute-done.4.far = bf16[2,2048,128]{2,1,0:T(8,128)(2,1)} collective-permute-done((bf16[2,2048,128]{2,1,0:T(8,128)(2,1)}, bf16[2,2048,128]{2,1,0:T(8,128)(2,1)}, u32[]{:S(2)}, u32[]{:S(2)}) %collective-permute-start.4) | collective-permute-done | bytes 1048608 | tf_op jit(solution)/shard_map/ppermute | solution.py:372
  65.6 1.9 %collective-permute-start.8 = (bf16[16,256,128]{2,1,0:T(8,128)(2,1)}, bf16[16,256,128]{2,1,0:T(8,128)(2,1)}, u32[]{:S(2)}, u32[]{:S(2)}) collective-permute-start(bf16[16,256,128]{2,1,0:T(8,128)(2,1)} %bitcast.43), channel_id=1, source_target_pairs={{1,32},{3,34},{5,36},{7,38},{9,40},{11,42},{13,44},{15,46},{17,48}... | collective-permute-start | bytes 3145736 | tf_op jit(solution)/shard_map/ppermute | solution.py:417
  68.5 7.7 %attend.1 = (bf16[2048,128]{1,0:T(8,128)(2,1)}, bf16[2048,128]{1,0:T(8,128)(2,1)}, bf16[128,2,16,128]{3,2,1,0:T(8,128)(2,1)}) custom-call(s32[1]{0:T(128)} %bitcast.core_ref, f32[640,256]{1,0:T(8,128)} %and_select_fusion.bias_ref, bf16[4,2,512,128]{3,2,1,0:T(8,128)(2,1)} %bitcast.58, bf16[4,2,512,128]{3,2,1,0:T(8,128)(2,1)} %bitcast.60, ...), custom_call_target="tpu_custom_call" | custom-call | flops 1342177280 | bytes 10092544 | tf_op jit(solution)/shard_map/attend/pallas_call | solution.py:294
  76.2 5.8 %collective-permute-done.8 = bf16[16,256,128]{2,1,0:T(8,128)(2,1)} collective-permute-done((bf16[16,256,128]{2,1,0:T(8,128)(2,1)}, bf16[16,256,128]{2,1,0:T(8,128)(2,1)}, u32[]{:S(2)}, u32[]{:S(2)}) %collective-permute-start.8) | collective-permute-done | bytes 1048608 | tf_op jit(solution)/shard_map/ppermute | solution.py:417
  82.0 11.3 %all-to-all-start = ((bf16[128,2,16,128]{3,2,1,0:T(8,128)(2,1)}), bf16[128,2,16,128]{3,2,1,0:T(8,128)(2,1)S(1)}, u32[]{:S(2)}, u32[]{:S(2)}) async-start(bf16[128,2,16,128]{3,2,1,0:T(8,128)(2,1)} %get-tuple-element.30), calls=%async_computation | async-start | bytes 2097152 | tf_op jit(solution)/shard_map/all_to_all | solution.py:425
  93.4 1.4 broadcast_select_fusion.filter_ref
  94.9 6.5 %filter_spectrum.1.spectrum_ref = f32[4096,256]{1,0:T(8,128)} custom-call(bf16[16,256,128]{2,1,0:T(8,128)(2,1)S(1)} %broadcast_select_fusion.filter_ref, bf16[512,512]{1,0:T(8,128)(2,1)S(1)} %copy-done.3, f32[256,128]{1,0:T(8,128)S(1)} %copy-done.8, f32[256,128]{1,0:T(8,128)S(1)} %copy-done.7, bf16[768,256]{1,0:T(8,128)(2,1)S(1)} %copy-done.4), custom_call_target="tpu_custom_call" | custom-call | flops 2720000000 | bytes 6291456 | tf_op jit(solution)/shard_map/filter_spectrum/pallas_call | solution.py:175
  101.4 21.5 %all-to-all-done = bf16[128,2,16,128]{3,2,1,0:T(8,128)(2,1)S(1)} async-done(((bf16[128,2,16,128]{3,2,1,0:T(8,128)(2,1)}), bf16[128,2,16,128]{3,2,1,0:T(8,128)(2,1)S(1)}, u32[]{:S(2)}, u32[]{:S(2)}) %all-to-all-start) | async-done | bytes 1048608 | tf_op jit(solution)/shard_map/all_to_all | solution.py:425
  125.8 11.5 %convolve.1 = bf16[256,16,128]{2,1,0:T(8,128)(2,1)} custom-call(bf16[256,16,128]{2,1,0:T(8,128)(2,1)S(1)} %bitcast.56, f32[4096,256]{1,0:T(8,128)} %filter_spectrum.1.spectrum_ref, bf16[512,512]{1,0:T(8,128)(2,1)S(1)} %copy-done.2, f32[256,128]{1,0:T(8,128)S(1)} %copy-done.9, f32[256,128]{1,0:T(8,128)S(1)} %copy-done.7, bf16[768,256]{1,0:T(8,128)(2,1)S(1)} %copy-done.5, ...), custom_call_target="tpu_custom_call" | custom-call | flops 5920000000 | bytes 8388608 | tf_op jit(solution)/shard_map/convolve/pallas_call | solution.py:194
  137.4 8.1 %all-to-all-start.1 = ((bf16[256,16,128]{2,1,0:T(8,128)(2,1)}), bf16[256,16,128]{2,1,0:T(8,128)(2,1)S(1)}, u32[]{:S(2)}, u32[]{:S(2)}) async-start(bf16[256,16,128]{2,1,0:T(8,128)(2,1)} %convolve.1), calls=%async_computation.1 | async-start | bytes 2097152 | tf_op jit(solution)/shard_map/all_to_all | solution.py:436
  145.5 2.4 %collective-permute-start.7 = (bf16[2048,128]{1,0:T(8,128)(2,1)S(1)}, bf16[2048,128]{1,0:T(8,128)(2,1)S(1)}, u32[]{:S(2)}, u32[]{:S(2)}) collective-permute-start(bf16[2048,128]{1,0:T(8,128)(2,1)S(1)} %copy-done.18), channel_id=1, source_target_pairs={{0,1},{1,0},{2,3},{3,2},{4,5},{5,4},{6,7},{7,6},{8,9},{9,8},{10,11... | collective-permute-start | bytes 1572872 | tf_op jit(solution)/shard_map/ppermute | solution.py:378
  147.8 1.5 collective-permute-done.7
  150.6 26.2 %all-to-all-done.1 = bf16[256,16,128]{2,1,0:T(8,128)(2,1)S(1)} async-done(((bf16[256,16,128]{2,1,0:T(8,128)(2,1)}), bf16[256,16,128]{2,1,0:T(8,128)(2,1)S(1)}, u32[]{:S(2)}, u32[]{:S(2)}) %all-to-all-start.1) | async-done | bytes 1048608 | tf_op jit(solution)/shard_map/all_to_all | solution.py:436
  176.8 1.3 fusion
  (74 shorter events, 12.2 us)
Async XLA Ops:
  1.9 5.5 %copy-start.19 = (s32[1,3]{1,0:T(1,128)S(1)}, s32[1,3]{1,0:T(1,128)}, u32[]{:S(2)}) copy-start(s32[1,3]{1,0:T(1,128)} %param.19) | copy-start | bytes 40
  1.9 5.8 %copy-start.17 = (s32[256]{0:T(256)S(1)}, s32[256]{0:T(256)}, u32[]{:S(2)}) copy-start(s32[256]{0:T(256)} %param.18) | copy-start | bytes 3076
  1.9 5.9 %copy-start.15 = (bf16[4096,128]{1,0:T(8,128)(2,1)S(1)}, bf16[4096,128]{1,0:T(8,128)(2,1)}, u32[]{:S(2)}) copy-start(bf16[4096,128]{1,0:T(8,128)(2,1)} %param.16) | copy-start | bytes 3145732
  4.2 5.7 %collective-permute-start.1 = (bf16[2,2048,128]{2,1,0:T(8,128)(2,1)}, bf16[2,2048,128]{2,1,0:T(8,128)(2,1)S(1)}, u32[]{:S(2)}, u32[]{:S(2)}) collective-permute-start(bf16[2,2048,128]{2,1,0:T(8,128)(2,1)} %pad_maximum_fusion), channel_id=1, source_target_pairs={{0,1},{1,0},{2,3},{3,2},{4,5},{5,4},{6,7},{7,6},{8,9},{9,8},{10,11... | collective-permute-start | bytes 3145736 | tf_op jit(solution)/shard_map/ppermute | solution.py:378
  7.4 60.1 %collective-permute-start.6 = (bf16[2,2048,128]{2,1,0:T(8,128)(2,1)}, bf16[2,2048,128]{2,1,0:T(8,128)(2,1)}, u32[]{:S(2)}, u32[]{:S(2)}) collective-permute-start(bf16[2,2048,128]{2,1,0:T(8,128)(2,1)} %pad_maximum_fusion), channel_id=1, source_target_pairs={{0,3},{1,2},{2,5},{3,4},{4,7},{5,6},{6,9},{7,8},{8,11},{9,10},{10,... | collective-permute-start | bytes 3145736 | tf_op jit(solution)/shard_map/ppermute | solution.py:353
  7.4 5.3 %collective-permute-start = (f32[1,3]{1,0:T(1,128)S(1)}, f32[1,3]{1,0:T(1,128)S(1)}, u32[]{:S(2)}, u32[]{:S(2)}) collective-permute-start(f32[1,3]{1,0:T(1,128)S(1)} %convert_element_type.39), channel_id=1, source_target_pairs={{0,1},{1,0},{2,3},{3,2},{4,5},{5,4},{6,7},{7,6},{8,9},{9,8},{10,11... | collective-permute-start | bytes 44 | tf_op jit(solution)/shard_map/ppermute | solution.py:378
  11.2 30.2 %copy-start.11 = (bf16[2,2048,128]{2,1,0:T(8,128)(2,1)}, bf16[2,2048,128]{2,1,0:T(8,128)(2,1)S(1)}, u32[]{:S(2)}) copy-start(bf16[2,2048,128]{2,1,0:T(8,128)(2,1)S(1)} %get-tuple-element.41.own) | copy-start | bytes 3145732
  11.2 24.7 %collective-permute-start.3 = (bf16[2,2048,128]{2,1,0:T(8,128)(2,1)}, bf16[2,2048,128]{2,1,0:T(8,128)(2,1)}, u32[]{:S(2)}, u32[]{:S(2)}) collective-permute-start(bf16[2,2048,128]{2,1,0:T(8,128)(2,1)} %get-tuple-element.42), channel_id=1, source_target_pairs={{0,6},{2,0},{4,2},{6,4},{1,7},{3,1},{5,3},{7,5},{8,14},{10,8},{12,... | collective-permute-start | bytes 3145736 | tf_op jit(solution)/shard_map/ppermute | solution.py:371
  13.0 49.2 %collective-permute-start.5 = (bf16[2,2048,128]{2,1,0:T(8,128)(2,1)S(1)}, bf16[2,2048,128]{2,1,0:T(8,128)(2,1)}, u32[]{:S(2)}, u32[]{:S(2)}) collective-permute-start(bf16[2,2048,128]{2,1,0:T(8,128)(2,1)S(1)} %get-tuple-element.41.own), channel_id=1, source_target_pairs={{0,2},{1,3},{2,4},{3,5},{4,6},{5,7},{6,8},{7,9},{8,10},{9,11},{10,... | collective-permute-start | bytes 3145736 | tf_op jit(solution)/shard_map/ppermute | solution.py:353
  35.9 29.6 %collective-permute-start.4 = (bf16[2,2048,128]{2,1,0:T(8,128)(2,1)}, bf16[2,2048,128]{2,1,0:T(8,128)(2,1)}, u32[]{:S(2)}, u32[]{:S(2)}) collective-permute-start(bf16[2,2048,128]{2,1,0:T(8,128)(2,1)} %collective-permute-done.3), channel_id=1, source_target_pairs={{6,4},{7,5},{0,6},{1,7},{2,8},{3,9},{4,10},{5,11},{14,12},{15,13},... | collective-permute-start | bytes 3145736 | tf_op jit(solution)/shard_map/ppermute | solution.py:372
  39.9 3.1 %copy-start.14 = (bf16[16,32768]{1,0:T(8,128)(2,1)S(1)}, bf16[16,32768]{1,0:T(8,128)(2,1)}, u32[]{:S(2)}) copy-start(bf16[16,32768]{1,0:T(8,128)(2,1)} %param.22) | copy-start | bytes 3145732
  41.4 26.1 %collective-permute-start.2 = (bf16[2,2048,128]{2,1,0:T(8,128)(2,1)S(1)}, bf16[2,2048,128]{2,1,0:T(8,128)(2,1)S(1)}, u32[]{:S(2)}, u32[]{:S(2)}) collective-permute-start(bf16[2,2048,128]{2,1,0:T(8,128)(2,1)S(1)} %pad_maximum_fusion.2), channel_id=1, source_target_pairs={{0,1},{1,0},{2,3},{3,2},{4,5},{5,4},{6,7},{7,6},{8,9},{9,8},{10,11... | collective-permute-start | bytes 3145736 | tf_op jit(solution)/shard_map/ppermute | solution.py:378
  65.6 16.4 %collective-permute-start.8 = (bf16[16,256,128]{2,1,0:T(8,128)(2,1)}, bf16[16,256,128]{2,1,0:T(8,128)(2,1)}, u32[]{:S(2)}, u32[]{:S(2)}) collective-permute-start(bf16[16,256,128]{2,1,0:T(8,128)(2,1)} %bitcast.43), channel_id=1, source_target_pairs={{1,32},{3,34},{5,36},{7,38},{9,40},{11,42},{13,44},{15,46},{17,48}... | collective-permute-start | bytes 3145736 | tf_op jit(solution)/shard_map/ppermute | solution.py:417
  82.0 41.0 %all-to-all-start = ((bf16[128,2,16,128]{3,2,1,0:T(8,128)(2,1)}), bf16[128,2,16,128]{3,2,1,0:T(8,128)(2,1)S(1)}, u32[]{:S(2)}, u32[]{:S(2)}) async-start(bf16[128,2,16,128]{3,2,1,0:T(8,128)(2,1)} %get-tuple-element.30), calls=%async_computation | async-start | bytes 2097152 | tf_op jit(solution)/shard_map/all_to_all | solution.py:425
  93.3 1.5 copy-start.7
  93.3 1.5 copy-start.4
  93.4 1.5 copy-start.8
  94.9 28.1 %copy-start.1 = (bf16[256,1536]{1,0:T(8,128)(2,1)S(1)}, bf16[256,1536]{1,0:T(8,128)(2,1)}, u32[]{:S(2)}) copy-start(bf16[256,1536]{1,0:T(8,128)(2,1)} %constant.91.clone.rest_5_) | copy-start | bytes 2359300
  94.9 28.1 %copy-start.2 = (bf16[512,512]{1,0:T(8,128)(2,1)S(1)}, bf16[512,512]{1,0:T(8,128)(2,1)}, u32[]{:S(2)}) copy-start(bf16[512,512]{1,0:T(8,128)(2,1)} %constant.89.clone.rest_0_) | copy-start | bytes 1572868
  137.4 8.1 %copy-start.18 = (bf16[2048,128]{1,0:T(8,128)(2,1)S(1)}, bf16[2048,128]{1,0:T(8,128)(2,1)}, u32[]{:S(2)}) copy-start(bf16[2048,128]{1,0:T(8,128)(2,1)} %get-tuple-element.27) | copy-start | bytes 1572868
  137.4 12.0 %copy-start.16 = (bf16[2048,128]{1,0:T(8,128)(2,1)S(1)}, bf16[2048,128]{1,0:T(8,128)(2,1)}, u32[]{:S(2)}) copy-start(bf16[2048,128]{1,0:T(8,128)(2,1)} %get-tuple-element.26) | copy-start | bytes 1572868
  137.4 39.4 %all-to-all-start.1 = ((bf16[256,16,128]{2,1,0:T(8,128)(2,1)}), bf16[256,16,128]{2,1,0:T(8,128)(2,1)S(1)}, u32[]{:S(2)}, u32[]{:S(2)}) async-start(bf16[256,16,128]{2,1,0:T(8,128)(2,1)} %convolve.1), calls=%async_computation.1 | async-start | bytes 2097152 | tf_op jit(solution)/shard_map/all_to_all | solution.py:436
  145.5 3.9 %collective-permute-start.7 = (bf16[2048,128]{1,0:T(8,128)(2,1)S(1)}, bf16[2048,128]{1,0:T(8,128)(2,1)S(1)}, u32[]{:S(2)}, u32[]{:S(2)}) collective-permute-start(bf16[2048,128]{1,0:T(8,128)(2,1)S(1)} %copy-done.18), channel_id=1, source_target_pairs={{0,1},{1,0},{2,3},{3,2},{4,5},{5,4},{6,7},{7,6},{8,9},{9,8},{10,11... | collective-permute-start | bytes 1572872 | tf_op jit(solution)/shard_map/ppermute | solution.py:378
  149.5 27.3 %copy-start.13 = (bf16[4096,128]{1,0:T(8,128)(2,1)S(1)}, bf16[4096,128]{1,0:T(8,128)(2,1)}, u32[]{:S(2)}) copy-start(bf16[4096,128]{1,0:T(8,128)(2,1)} %param.21) | copy-start | bytes 3145732
  (7 other events, 7.9 us)

commit v3 on v2

--- a/solution.py
+++ b/solution.py
@@ -179,7 +179,7 @@
         + [whole(entry) for entry in constants],
         out_specs=pl.BlockSpec((step_channels * rows, 2 * width), lambda step: (step, 0)),
         out_shape=jax.ShapeDtypeStruct((channels * rows, 2 * width), jnp.float32),
-        compiler_params=pltpu.CompilerParams(vmem_limit_bytes=VMEM_LIMIT),
+        compiler_params=pltpu.CompilerParams(vmem_limit_bytes=HBM_ONLY),
         cost_estimate=pl.CostEstimate(
             flops=channels * 170_000_000, bytes_accessed=6 * 1024 * 1024, transcendentals=0
         ),
@@ -202,7 +202,7 @@
         out_specs=whole(signal),
         out_shape=jax.ShapeDtypeStruct(signal.shape, jnp.bfloat16),
         scratch_shapes=[pltpu.VMEM((rows * channels, width), jnp.float32)] * 2,
-        compiler_params=pltpu.CompilerParams(vmem_limit_bytes=VMEM_LIMIT),
+        compiler_params=pltpu.CompilerParams(vmem_limit_bytes=HBM_ONLY),
         cost_estimate=pl.CostEstimate(
             flops=channels * 370_000_000, bytes_accessed=8 * 1024 * 1024, transcendentals=0
         ),
@@ -412,7 +412,7 @@
 
     taps = long_filter.reshape(group, devices, tokens)
     taps, bias, _ = lax.optimization_barrier((taps, bias, odd))
-    taps, far, near = lax.optimization_barrier((taps, far, near))
+    taps, near, crossed = lax.optimization_barrier((taps, near, crossed))
     moved = [(source, exchanged(source)) for source in range(devices) if exchanged(source) != source]
     swapped = lax.ppermute(taps, ALL, moved)
 

time: 179 us -> 171 us (0.955)
  waiting for transfers between devices: 101 us -> 92.2 us
  local copies, waits for them, and re-layouts: 11 us -> 7.76 us
  Pallas kernels: 25.8 us -> 28.2 us
    unnamed x42 -> x24, local copies, waits for them, and re-layouts: 6.55 us -> 2.53 us
    ppermute x1, waiting for transfers between devices: 5.76 us -> 1.78 us  [body(): swapped = lax.ppermute(taps, ALL, moved)]
    ppermute x1, waiting for transfers between devices: 22.4 us -> 18.6 us  [second_next_chip(): value = lax.ppermute(value, 'y', [(y, (y - 1) % ring) for y in range(ring)])]
    all_to_all x1, waiting for transfers between devices: 21.5 us -> 19.2 us  [body(): lax.all_to_all(gated, CHIPS, split_axis=0, concat_axis=0, tiled=True)]
  transfers between devices with their start and end apart: 11 -> 11, of which waited for: 8 -> 9; matrix products, arithmetic and copies ran while one was open for 5% -> 6% of each run, Pallas kernels for 8% -> 9%
where the time goes in v3:
time: 171 us
  waiting for transfers between devices  92.2 us (54%)
  starting transfers between devices  33.9 us (20%)
  Pallas kernels  28.2 us (16%)
  other arithmetic  8.15 us (5%)
  local copies, waits for them, and re-layouts  7.76 us (5%)
    all_to_all x1, waiting for transfers between devices, body(): lax.all_to_all(conv_out, OWNERS, split_axis=0, concat_axis=0, tiled=True)  26.2 us
    ppermute x2, waiting for transfers between devices, send(): lax.ppermute(value, ALL, [(source, target(source) % count) for source in...  19.6 us
    all_to_all x1, waiting for transfers between devices, body(): lax.all_to_all(gated, CHIPS, split_axis=0, concat_axis=0, tiled=True)  19.2 us
    ppermute x1, waiting for transfers between devices, second_next_chip(): value = lax.ppermute(value, 'y', [(y, (y - 1) % ring) for y in range(ring)])  18.6 us
    pallas_call x1, Pallas kernels, convolve(): pl.pallas_call(conv_kernel, grid=(channels // step_channels,), in_specs=[...  12.4 us
    all_to_all x1, starting transfers between devices, body(): lax.all_to_all(gated, CHIPS, split_axis=0, concat_axis=0, tiled=True)  10.1 us
    all_to_all x1, starting transfers between devices, body(): lax.all_to_all(conv_out, OWNERS, split_axis=0, concat_axis=0, tiled=True)  9.03 us
    pallas_call x1, Pallas kernels, transform_filter(): pl.pallas_call(filter_kernel, grid=(channels // step_channels,), in_specs...  7.98 us
  transfers between devices with their start and end apart: 11, of which 9 were waited for; matrix products, arithmetic and copies ran while one was open for 6% of the time, Pallas kernels for 9%

profile of v3, /device:TPU:1, one launch (start us, length us, event | category | flops | bytes accessed | tf_op | source)
XLA Modules:
  0.0 171.0 jit_solution(14943634908923124797)
XLA Ops:
  0.7 1.2 copy-done
  1.9 1.2 constant_dynamic-slice_fusion.4
  4.2 3.2 %collective-permute-start.1 = (bf16[2,2048,128]{2,1,0:T(8,128)(2,1)}, bf16[2,2048,128]{2,1,0:T(8,128)(2,1)S(1)}, u32[]{:S(2)}, u32[]{:S(2)}) collective-permute-start(bf16[2,2048,128]{2,1,0:T(8,128)(2,1)} %pad_maximum_fusion), channel_id=1, source_target_pairs={{0,1},{1,0},{2,3},{3,2},{4,5},{5,4},{6,7},{7,6},{8,9},{9,8},{10,11... | collective-permute-start | bytes 3145736 | tf_op jit(solution)/shard_map/ppermute | solution.py:378
  9.9 2.5 %pad_maximum_fusion.1 = (bf16[2,2048,128]{2,1,0:T(8,128)(2,1)S(1)}, bf16[2,2048,128]{2,1,0:T(8,128)(2,1)}) fusion(bf16[1,2048,128]{2,1,0:T(8,128)(2,1)S(1)} %bitcast.61, bf16[1,2048,128]{2,1,0:T(8,128)(2,1)} %bitcast.60, bf16[2,2048,128]{2,1,0:T(8,128)(2,1)S(1)} %collective-permute-done.1.sibling, pred[]{:T(512)S(6)} %eq.73), kind=kLoop, calls=%fused_computation.3 | loop fusion | flops 1048576 | bytes 4194305 | tf_op jit(solution)/shard_map/stack | solution.py:216
  13.1 2.3 %collective-permute-start.3 = (bf16[2,2048,128]{2,1,0:T(8,128)(2,1)}, bf16[2,2048,128]{2,1,0:T(8,128)(2,1)}, u32[]{:S(2)}, u32[]{:S(2)}) collective-permute-start(bf16[2,2048,128]{2,1,0:T(8,128)(2,1)} %get-tuple-element.42), channel_id=1, source_target_pairs={{0,6},{2,0},{4,2},{6,4},{1,7},{3,1},{5,3},{7,5},{8,14},{10,8},{12,... | collective-permute-start | bytes 3145736 | tf_op jit(solution)/shard_map/ppermute | solution.py:371
  17.2 1.4 constant_dynamic-slice_fusion
  19.4 18.6 %collective-permute-done.3 = bf16[2,2048,128]{2,1,0:T(8,128)(2,1)} collective-permute-done((bf16[2,2048,128]{2,1,0:T(8,128)(2,1)}, bf16[2,2048,128]{2,1,0:T(8,128)(2,1)}, u32[]{:S(2)}, u32[]{:S(2)}) %collective-permute-start.3) | collective-permute-done | bytes 1048608 | tf_op jit(solution)/shard_map/ppermute | solution.py:371
  38.0 3.4 %collective-permute-start.4 = (bf16[2,2048,128]{2,1,0:T(8,128)(2,1)}, bf16[2,2048,128]{2,1,0:T(8,128)(2,1)}, u32[]{:S(2)}, u32[]{:S(2)}) collective-permute-start(bf16[2,2048,128]{2,1,0:T(8,128)(2,1)} %collective-permute-done.3), channel_id=1, source_target_pairs={{6,4},{7,5},{0,6},{1,7},{2,8},{3,9},{4,10},{5,11},{14,12},{15,13},... | collective-permute-start | bytes 3145736 | tf_op jit(solution)/shard_map/ppermute | solution.py:372
  41.4 1.2 copy.46
  42.6 19.6 %collective-permute-done.5.near = bf16[2,2048,128]{2,1,0:T(8,128)(2,1)} collective-permute-done((bf16[2,2048,128]{2,1,0:T(8,128)(2,1)S(1)}, bf16[2,2048,128]{2,1,0:T(8,128)(2,1)}, u32[]{:S(2)}, u32[]{:S(2)}) %collective-permute-start.5) | collective-permute-done | bytes 1048608 | tf_op jit(solution)/shard_map/ppermute | solution.py:353
  62.2 1.9 %collective-permute-start.8 = (bf16[16,256,128]{2,1,0:T(8,128)(2,1)}, bf16[16,256,128]{2,1,0:T(8,128)(2,1)S(1)}, u32[]{:S(2)}, u32[]{:S(2)}) collective-permute-start(bf16[16,256,128]{2,1,0:T(8,128)(2,1)} %bitcast.43), channel_id=1, source_target_pairs={{1,32},{3,34},{5,36},{7,38},{9,40},{11,42},{13,44},{15,46},{17,48}... | collective-permute-start | bytes 3145736 | tf_op jit(solution)/shard_map/ppermute | solution.py:417
  64.1 4.9 %collective-permute-done.4.far = bf16[2,2048,128]{2,1,0:T(8,128)(2,1)} collective-permute-done((bf16[2,2048,128]{2,1,0:T(8,128)(2,1)}, bf16[2,2048,128]{2,1,0:T(8,128)(2,1)}, u32[]{:S(2)}, u32[]{:S(2)}) %collective-permute-start.4) | collective-permute-done | bytes 1048608 | tf_op jit(solution)/shard_map/ppermute | solution.py:372
  69.0 7.7 %attend.1 = (bf16[2048,128]{1,0:T(8,128)(2,1)}, bf16[2048,128]{1,0:T(8,128)(2,1)}, bf16[128,2,16,128]{3,2,1,0:T(8,128)(2,1)}) custom-call(s32[1]{0:T(128)} %bitcast.core_ref, f32[640,256]{1,0:T(8,128)} %and_select_fusion.bias_ref, bf16[4,2,512,128]{3,2,1,0:T(8,128)(2,1)} %bitcast.57, bf16[4,2,512,128]{3,2,1,0:T(8,128)(2,1)} %bitcast.59, ...), custom_call_target="tpu_custom_call" | custom-call | flops 1342177280 | bytes 10092544 | tf_op jit(solution)/shard_map/attend/pallas_call | solution.py:294
  76.7 1.8 %collective-permute-done.8 = bf16[16,256,128]{2,1,0:T(8,128)(2,1)S(1)} collective-permute-done((bf16[16,256,128]{2,1,0:T(8,128)(2,1)}, bf16[16,256,128]{2,1,0:T(8,128)(2,1)S(1)}, u32[]{:S(2)}, u32[]{:S(2)}) %collective-permute-start.8) | collective-permute-done | bytes 1048608 | tf_op jit(solution)/shard_map/ppermute | solution.py:417
  78.5 10.1 %all-to-all-start = ((bf16[128,2,16,128]{3,2,1,0:T(8,128)(2,1)}), bf16[128,2,16,128]{3,2,1,0:T(8,128)(2,1)}, u32[]{:S(2)}, u32[]{:S(2)}) async-start(bf16[128,2,16,128]{3,2,1,0:T(8,128)(2,1)} %get-tuple-element.30), calls=%async_computation | async-start | bytes 2097152 | tf_op jit(solution)/shard_map/all_to_all | solution.py:425
  88.6 1.1 broadcast_select_fusion.filter_ref
  89.7 8.0 %filter_spectrum.1.spectrum_ref = f32[4096,256]{1,0:T(8,128)} custom-call(bf16[16,256,128]{2,1,0:T(8,128)(2,1)} %broadcast_select_fusion.filter_ref, bf16[512,512]{1,0:T(8,128)(2,1)} %constant.85.clone.rest_0_, f32[256,128]{1,0:T(8,128)} %constant.86.clone.rest_1_, f32[256,128]{1,0:T(8,128)} %constant.87.clone.rest_2_, bf16[768,256]{1,0:T(8,128)(2,1)} %constant.88.clone.rest_3_), custom_call_target="tpu_custom_call" | custom-call | flops 2720000000 | bytes 6291456 | tf_op jit(solution)/shard_map/filter_spectrum/pallas_call | solution.py:175
  97.7 19.2 %all-to-all-done = bf16[128,2,16,128]{3,2,1,0:T(8,128)(2,1)} async-done(((bf16[128,2,16,128]{3,2,1,0:T(8,128)(2,1)}), bf16[128,2,16,128]{3,2,1,0:T(8,128)(2,1)}, u32[]{:S(2)}, u32[]{:S(2)}) %all-to-all-start) | async-done | bytes 1048608 | tf_op jit(solution)/shard_map/all_to_all | solution.py:425
  116.9 12.4 %convolve.1 = bf16[256,16,128]{2,1,0:T(8,128)(2,1)} custom-call(bf16[256,16,128]{2,1,0:T(8,128)(2,1)} %bitcast.27.signal_ref, f32[4096,256]{1,0:T(8,128)} %filter_spectrum.1.spectrum_ref, bf16[512,512]{1,0:T(8,128)(2,1)} %constant.89.clone.rest_0_, f32[256,128]{1,0:T(8,128)} %constant.86.clone.rest_1_, f32[256,128]{1,0:T(8,128)} %constant.87.clone.rest_2_, ...), custom_call_target="tpu_custom_call" | custom-call | flops 5920000000 | bytes 8388608 | tf_op jit(solution)/shard_map/convolve/pallas_call | solution.py:194
  129.3 9.0 %all-to-all-start.1 = ((bf16[256,16,128]{2,1,0:T(8,128)(2,1)}), bf16[256,16,128]{2,1,0:T(8,128)(2,1)S(1)}, u32[]{:S(2)}, u32[]{:S(2)}) async-start(bf16[256,16,128]{2,1,0:T(8,128)(2,1)} %convolve.1), calls=%async_computation.1 | async-start | bytes 2097152 | tf_op jit(solution)/shard_map/all_to_all | solution.py:436
  138.4 2.4 %collective-permute-start.7 = (bf16[2048,128]{1,0:T(8,128)(2,1)S(1)}, bf16[2048,128]{1,0:T(8,128)(2,1)S(1)}, u32[]{:S(2)}, u32[]{:S(2)}) collective-permute-start(bf16[2048,128]{1,0:T(8,128)(2,1)S(1)} %copy-done.9), channel_id=1, source_target_pairs={{0,1},{1,0},{2,3},{3,2},{4,5},{5,4},{6,7},{7,6},{8,9},{9,8},{10,11... | collective-permute-start | bytes 1572872 | tf_op jit(solution)/shard_map/ppermute | solution.py:378
  140.7 1.5 collective-permute-done.7
  143.5 26.2 %all-to-all-done.1 = bf16[256,16,128]{2,1,0:T(8,128)(2,1)S(1)} async-done(((bf16[256,16,128]{2,1,0:T(8,128)(2,1)}), bf16[256,16,128]{2,1,0:T(8,128)(2,1)S(1)}, u32[]{:S(2)}, u32[]{:S(2)}) %all-to-all-start.1) | async-done | bytes 1048608 | tf_op jit(solution)/shard_map/all_to_all | solution.py:436
  169.7 1.3 fusion
  (56 shorter events, 8.0 us)
Async XLA Ops:
  0.6 1.2 copy-start
  1.9 5.5 %copy-start.10 = (s32[1,3]{1,0:T(1,128)S(1)}, s32[1,3]{1,0:T(1,128)}, u32[]{:S(2)}) copy-start(s32[1,3]{1,0:T(1,128)} %param.19) | copy-start | bytes 40
  1.9 5.7 %copy-start.8 = (s32[256]{0:T(256)S(1)}, s32[256]{0:T(256)}, u32[]{:S(2)}) copy-start(s32[256]{0:T(256)} %param.18) | copy-start | bytes 3076
  1.9 7.1 %copy-start.6 = (bf16[4096,128]{1,0:T(8,128)(2,1)S(1)}, bf16[4096,128]{1,0:T(8,128)(2,1)}, u32[]{:S(2)}) copy-start(bf16[4096,128]{1,0:T(8,128)(2,1)} %param.17) | copy-start | bytes 3145732
  4.2 5.7 %collective-permute-start.1 = (bf16[2,2048,128]{2,1,0:T(8,128)(2,1)}, bf16[2,2048,128]{2,1,0:T(8,128)(2,1)S(1)}, u32[]{:S(2)}, u32[]{:S(2)}) collective-permute-start(bf16[2,2048,128]{2,1,0:T(8,128)(2,1)} %pad_maximum_fusion), channel_id=1, source_target_pairs={{0,1},{1,0},{2,3},{3,2},{4,5},{5,4},{6,7},{7,6},{8,9},{9,8},{10,11... | collective-permute-start | bytes 3145736 | tf_op jit(solution)/shard_map/ppermute | solution.py:378
  7.4 35.2 %collective-permute-start.6 = (bf16[2,2048,128]{2,1,0:T(8,128)(2,1)}, bf16[2,2048,128]{2,1,0:T(8,128)(2,1)}, u32[]{:S(2)}, u32[]{:S(2)}) collective-permute-start(bf16[2,2048,128]{2,1,0:T(8,128)(2,1)} %pad_maximum_fusion), channel_id=1, source_target_pairs={{0,3},{1,2},{2,5},{3,4},{4,7},{5,6},{6,9},{7,8},{8,11},{9,10},{10,... | collective-permute-start | bytes 3145736 | tf_op jit(solution)/shard_map/ppermute | solution.py:353
  7.4 2.1 %collective-permute-start = (f32[1,3]{1,0:T(1,128)S(1)}, f32[1,3]{1,0:T(1,128)S(1)}, u32[]{:S(2)}, u32[]{:S(2)}) collective-permute-start(f32[1,3]{1,0:T(1,128)S(1)} %convert_element_type.39), channel_id=1, source_target_pairs={{0,1},{1,0},{2,3},{3,2},{4,5},{5,4},{6,7},{7,6},{8,9},{9,8},{10,11... | collective-permute-start | bytes 44 | tf_op jit(solution)/shard_map/ppermute | solution.py:378
  9.9 2.5 %copy-start.1 = (bf16[2,2048,128]{2,1,0:T(8,128)(2,1)}, bf16[2,2048,128]{2,1,0:T(8,128)(2,1)S(1)}, u32[]{:S(2)}) copy-start(bf16[2,2048,128]{2,1,0:T(8,128)(2,1)S(1)} %collective-permute-done.1.sibling) | copy-start | bytes 3145732
  12.4 6.3 %copy-start.2 = (bf16[2,2048,128]{2,1,0:T(8,128)(2,1)}, bf16[2,2048,128]{2,1,0:T(8,128)(2,1)S(1)}, u32[]{:S(2)}) copy-start(bf16[2,2048,128]{2,1,0:T(8,128)(2,1)S(1)} %get-tuple-element.41.own) | copy-start | bytes 3145732
  12.4 49.8 %collective-permute-start.5 = (bf16[2,2048,128]{2,1,0:T(8,128)(2,1)S(1)}, bf16[2,2048,128]{2,1,0:T(8,128)(2,1)}, u32[]{:S(2)}, u32[]{:S(2)}) collective-permute-start(bf16[2,2048,128]{2,1,0:T(8,128)(2,1)S(1)} %get-tuple-element.41.own), channel_id=1, source_target_pairs={{0,2},{1,3},{2,4},{3,5},{4,6},{5,7},{6,8},{7,9},{8,10},{9,11},{10,... | collective-permute-start | bytes 3145736 | tf_op jit(solution)/shard_map/ppermute | solution.py:353
  13.1 24.8 %collective-permute-start.3 = (bf16[2,2048,128]{2,1,0:T(8,128)(2,1)}, bf16[2,2048,128]{2,1,0:T(8,128)(2,1)}, u32[]{:S(2)}, u32[]{:S(2)}) collective-permute-start(bf16[2,2048,128]{2,1,0:T(8,128)(2,1)} %get-tuple-element.42), channel_id=1, source_target_pairs={{0,6},{2,0},{4,2},{6,4},{1,7},{3,1},{5,3},{7,5},{8,14},{10,8},{12,... | collective-permute-start | bytes 3145736 | tf_op jit(solution)/shard_map/ppermute | solution.py:371
  17.2 24.2 %copy-start.5 = (bf16[16,32768]{1,0:T(8,128)(2,1)S(1)}, bf16[16,32768]{1,0:T(8,128)(2,1)}, u32[]{:S(2)}) copy-start(bf16[16,32768]{1,0:T(8,128)(2,1)} %param.22) | copy-start | bytes 3145732
  18.7 45.4 %collective-permute-start.2 = (bf16[2,2048,128]{2,1,0:T(8,128)(2,1)S(1)}, bf16[2,2048,128]{2,1,0:T(8,128)(2,1)S(1)}, u32[]{:S(2)}, u32[]{:S(2)}) collective-permute-start(bf16[2,2048,128]{2,1,0:T(8,128)(2,1)S(1)} %pad_maximum_fusion.2), channel_id=1, source_target_pairs={{0,1},{1,0},{2,3},{3,2},{4,5},{5,4},{6,7},{7,6},{8,9},{9,8},{10,11... | collective-permute-start | bytes 3145736 | tf_op jit(solution)/shard_map/ppermute | solution.py:378
  38.0 31.0 %collective-permute-start.4 = (bf16[2,2048,128]{2,1,0:T(8,128)(2,1)}, bf16[2,2048,128]{2,1,0:T(8,128)(2,1)}, u32[]{:S(2)}, u32[]{:S(2)}) collective-permute-start(bf16[2,2048,128]{2,1,0:T(8,128)(2,1)} %collective-permute-done.3), channel_id=1, source_target_pairs={{6,4},{7,5},{0,6},{1,7},{2,8},{3,9},{4,10},{5,11},{14,12},{15,13},... | collective-permute-start | bytes 3145736 | tf_op jit(solution)/shard_map/ppermute | solution.py:372
  62.2 16.3 %collective-permute-start.8 = (bf16[16,256,128]{2,1,0:T(8,128)(2,1)}, bf16[16,256,128]{2,1,0:T(8,128)(2,1)S(1)}, u32[]{:S(2)}, u32[]{:S(2)}) collective-permute-start(bf16[16,256,128]{2,1,0:T(8,128)(2,1)} %bitcast.43), channel_id=1, source_target_pairs={{1,32},{3,34},{5,36},{7,38},{9,40},{11,42},{13,44},{15,46},{17,48}... | collective-permute-start | bytes 3145736 | tf_op jit(solution)/shard_map/ppermute | solution.py:417
  64.1 4.9 %copy-start.3 = (bf16[2,2048,128]{2,1,0:T(8,128)(2,1)}, bf16[2,2048,128]{2,1,0:T(8,128)(2,1)S(1)}, u32[]{:S(2)}) copy-start(bf16[2,2048,128]{2,1,0:T(8,128)(2,1)S(1)} %collective-permute-done.2.q_other.gate_other) | copy-start | bytes 3145732
  78.5 38.3 %all-to-all-start = ((bf16[128,2,16,128]{3,2,1,0:T(8,128)(2,1)}), bf16[128,2,16,128]{3,2,1,0:T(8,128)(2,1)}, u32[]{:S(2)}, u32[]{:S(2)}) async-start(bf16[128,2,16,128]{3,2,1,0:T(8,128)(2,1)} %get-tuple-element.30), calls=%async_computation | async-start | bytes 2097152 | tf_op jit(solution)/shard_map/all_to_all | solution.py:425
  129.3 9.0 %copy-start.9 = (bf16[2048,128]{1,0:T(8,128)(2,1)S(1)}, bf16[2048,128]{1,0:T(8,128)(2,1)}, u32[]{:S(2)}) copy-start(bf16[2048,128]{1,0:T(8,128)(2,1)} %get-tuple-element.27) | copy-start | bytes 1572868
  129.3 13.0 %copy-start.7 = (bf16[2048,128]{1,0:T(8,128)(2,1)S(1)}, bf16[2048,128]{1,0:T(8,128)(2,1)}, u32[]{:S(2)}) copy-start(bf16[2048,128]{1,0:T(8,128)(2,1)} %get-tuple-element.26) | copy-start | bytes 1572868
  129.3 40.4 %all-to-all-start.1 = ((bf16[256,16,128]{2,1,0:T(8,128)(2,1)}), bf16[256,16,128]{2,1,0:T(8,128)(2,1)S(1)}, u32[]{:S(2)}, u32[]{:S(2)}) async-start(bf16[256,16,128]{2,1,0:T(8,128)(2,1)} %convolve.1), calls=%async_computation.1 | async-start | bytes 2097152 | tf_op jit(solution)/shard_map/all_to_all | solution.py:436
  138.4 3.9 %collective-permute-start.7 = (bf16[2048,128]{1,0:T(8,128)(2,1)S(1)}, bf16[2048,128]{1,0:T(8,128)(2,1)S(1)}, u32[]{:S(2)}, u32[]{:S(2)}) collective-permute-start(bf16[2048,128]{1,0:T(8,128)(2,1)S(1)} %copy-done.9), channel_id=1, source_target_pairs={{0,1},{1,0},{2,3},{3,2},{4,5},{5,4},{6,7},{7,6},{8,9},{9,8},{10,11... | collective-permute-start | bytes 1572872 | tf_op jit(solution)/shard_map/ppermute | solution.py:378
  142.3 27.3 %copy-start.4 = (bf16[4096,128]{1,0:T(8,128)(2,1)S(1)}, bf16[4096,128]{1,0:T(8,128)(2,1)}, u32[]{:S(2)}) copy-start(bf16[4096,128]{1,0:T(8,128)(2,1)} %param.21) | copy-start | bytes 3145732

commit v4 on v3

--- a/solution.py
+++ b/solution.py
@@ -1,3 +1,4 @@
+import functools
 import math
 
 import jax
@@ -222,39 +223,35 @@
 
 
 def attend_kernel(
-    core_ref,
-    bias_ref,
-    q_mine,
-    gate_mine,
-    q_other,
-    gate_other,
-    far,
-    near,
-    crossed,
-    own,
-    sibling,
-    out_mine,
-    out_other,
-    gated,
+    parity, core_ref, bias_ref, q_mine, gate_mine, q_other, gate_other, near, crossed, own, sibling, *rest
 ):
+    out_ref, gated = rest[-2:]
     heads, tokens = gate_other.shape[0] // HD, gate_other.shape[1]
-    group = gated.shape[2]
-    core = core_ref[0]
-    pairs = (far, near, crossed, own, sibling)
+    group = gated.shape[1]
+    is_mine = core_ref[0] == parity
     part_heads = q_mine.shape[1] // HD
 
     def rows_of(head):
         return slice(head * HD, (head + 1) * HD)
 
-    def own_rows(ref, head):
-        return ref[head // part_heads, rows_of(head % part_heads)]
+    def chosen(mine_ref, other_ref, head):
+        mine = mine_ref[head // part_heads, rows_of(head % part_heads)]
+        return jnp.where(is_mine, mine, other_ref[rows_of(head)])
+
+    def window(kind, rows):
+        shared = [near[kind, rows], crossed[kind, rows]]
+        if parity == 1:
+            return jnp.concatenate(shared + [own[kind, rows], sibling[kind, rows]], axis=1)
+        itself = jnp.where(is_mine, own[kind, rows], sibling[kind, rows])
+        return jnp.concatenate(shared + [rest[0][kind, rows], itself], axis=1)
 
     def task(head):
         rows = rows_of(head)
-        queries = jnp.concatenate([own_rows(q_mine, head), q_other[rows]], axis=1)
-        keys = jnp.concatenate([pair[0, rows] for pair in pairs], axis=1)
         scores = lax.dot_general(
-            keys, queries, (((0,), (0,)), ((), ())), preferred_element_type=jnp.float32
+            window(0, rows),
+            chosen(q_mine, q_other, head),
+            (((0,), (0,)), ((), ())),
+            preferred_element_type=jnp.float32,
         )
         yield True
         masked = scores * (math.log2(math.e) / math.sqrt(HD)) + bias_ref[...]
@@ -262,61 +259,62 @@
         total = jnp.sum(weights, axis=0, keepdims=True)
         weights = weights.astype(jnp.bfloat16)
         yield True
-        values = jnp.concatenate([pair[1, rows] for pair in pairs], axis=1)
-        mixed = (dot(values, weights) * (1.0 / total)).astype(jnp.bfloat16)
-        gates = (
-            (out_mine, own_rows(gate_mine, head), core),
-            (out_other, gate_other[rows], 1 - core),
-        )
-        for place, (out, gate, block) in enumerate(gates):
-            part = mixed[:, place * tokens : (place + 1) * tokens]
-            out[rows] = part
-            product = (part.astype(jnp.float32) * gate.astype(jnp.float32)).astype(jnp.bfloat16)
-            owners = slice(head * HD // group, (head + 1) * HD // group)
-            gated[owners, block] = product.reshape(HD // group, group, tokens)
+        mixed = (dot(window(1, rows), weights) * (1.0 / total)).astype(jnp.bfloat16)
+        out_ref[rows] = mixed
+        gate = chosen(gate_mine, gate_other, head)
+        product = (mixed.astype(jnp.float32) * gate.astype(jnp.float32)).astype(jnp.bfloat16)
+        owners = slice(head * HD // group, (head + 1) * HD // group)
+        gated[owners] = product.reshape(HD // group, group, tokens)
 
     interleaved([task(head) for head in range(heads)])
 
 
-def attend(core, bias, q_proj, gate, exchanged, blocks, group, steps=2):
+def attend(parity, core, bias, q_proj, gate, exchanged, blocks, group, gated=None, steps=2):
     channels, tokens = q_proj.shape[0] // 2, q_proj.shape[1]
     step_rows = channels // steps
     halves = [value.reshape(STEPS, 2, channels // STEPS, tokens) for value in (q_proj, gate)]
     half = pl.BlockSpec(
         (STEPS // steps, None, channels // STEPS, tokens), lambda step, core: (step, core[0], 0, 0)
     )
-    single = pl.BlockSpec((step_rows, tokens), lambda step, core: (step, 0))
     pair = pl.BlockSpec((2, step_rows, tokens), lambda step, core: (0, step, 0))
     pieces = [
         pl.BlockSpec((None, step_rows, tokens), lambda step, core, which=which: (which, step, 0))
         for which in range(2)
     ]
+    operands = [core.reshape(1), bias, *halves, exchanged, exchanged, *blocks]
+    in_specs = [pl.BlockSpec(bias.shape, lambda step, core: (0, 0)), half, half, *pieces]
+    in_specs += [pair] * len(blocks)
+    aliases = {}
+    if gated is not None:
+        aliases = {len(operands): 1}
+        operands.append(gated)
+        in_specs.append(pl.BlockSpec(memory_space=pl.ANY))
     return pl.pallas_call(
-        attend_kernel,
+        functools.partial(attend_kernel, parity),
         grid_spec=pltpu.PrefetchScalarGridSpec(
             num_scalar_prefetch=1,
             grid=(steps,),
-            in_specs=[pl.BlockSpec(bias.shape, lambda step, core: (0, 0)), half, half, *pieces]
-            + [pair] * 5,
+            in_specs=in_specs,
             out_specs=[
-                single,
-                single,
-                pl.BlockSpec((step_rows // group, 2, group, tokens), lambda step, core: (step, 0, 0, 0)),
+                pl.BlockSpec((step_rows, tokens), lambda step, core: (step, 0)),
+                pl.BlockSpec(
+                    (step_rows // group, None, group, tokens), lambda step, core: (step, parity, 0, 0)
+                ),
             ],
         ),
         out_shape=[
             jax.ShapeDtypeStruct((channels, tokens), jnp.bfloat16),
-            jax.ShapeDtypeStruct((channels, tokens), jnp.bfloat16),
             jax.ShapeDtypeStruct((channels // group, 2, group, tokens), jnp.bfloat16),
         ],
+        input_output_aliases=aliases,
         compiler_params=pltpu.CompilerParams(vmem_limit_bytes=HBM_ONLY),
         cost_estimate=pl.CostEstimate(
             flops=(channels // HD) * 4 * HD * bias.size,
-            bytes_accessed=18 * 2 * channels * tokens + 4 * bias.size,
+            bytes_accessed=16 * 2 * channels * tokens + 4 * bias.size,
             transcendentals=(channels // HD) * bias.size,
         ),
-        name="attend",
-    )(core.reshape(1), bias, *halves, exchanged, exchanged, *blocks)
+        name=("attend_first", "attend_second")[parity],
+    )(*operands)
 
 
 def chip_bias(block_start, flags, key_ids, query_ids, tokens):
@@ -397,13 +395,20 @@
     flags = kv_select.astype(jnp.float32)
     flags = jnp.concatenate([flags, to_sibling(flags)], axis=0).astype(jnp.int32)
     first = 2 * lax.axis_index(ALL[:-1])
-    key_ids = jnp.stack(
-        [first - 3, first - 2 + core, first - 1 - core, first + core, first + 1 - core]
-    )
-    query_ids = jnp.stack([first + core, first + 1 - core])
-    bias = chip_bias(block_start, flags, key_ids, query_ids, tokens)
-
-    q_later, gate_later, bias, _ = lax.optimization_barrier((q_proj, pre_gate, bias, odd))
+    near_ids = [first - 2 + core, first - 1 - core]
+    windows = [[first - 3, first], [first + core, first + 1 - core]]
+    biases = [
+        chip_bias(
+            block_start,
+            jnp.where(core == parity, flags[:1], flags[1:]),
+            jnp.stack(near_ids + windows[parity]),
+            jnp.stack([first + parity]),
+            tokens,
+        )
+        for parity in range(2)
+    ]
+
+    q_later, gate_later, biases, _ = lax.optimization_barrier((q_proj, pre_gate, biases, odd))
     exchanged_half = to_sibling(pick_heads(1 - core, q_later, gate_later))
 
     def exchanged(source):
@@ -411,19 +416,22 @@
         return upper * 64 + c * 32 + lower * 2 + zc
 
     taps = long_filter.reshape(group, devices, tokens)
-    taps, bias, _ = lax.optimization_barrier((taps, bias, odd))
+    taps, biases, _ = lax.optimization_barrier((taps, biases, odd))
     taps, near, crossed = lax.optimization_barrier((taps, near, crossed))
     moved = [(source, exchanged(source)) for source in range(devices) if exchanged(source) != source]
     swapped = lax.ppermute(taps, ALL, moved)
 
-    out_mine, out_other, gated = attend(
-        core, bias, q_proj, pre_gate, exchanged_half, (far, near, crossed, mine, sibling), group
+    near_blocks = (near, crossed, mine, sibling)
+    out_second, gated = attend(1, core, biases[1], q_proj, pre_gate, exchanged_half, near_blocks, group)
+    out_first, gated = attend(
+        0, core, biases[0], q_proj, pre_gate, exchanged_half, (*near_blocks, far), group, gated
     )
     gated, swapped = lax.optimization_barrier((gated, swapped))
     taps = jnp.where(lax.axis_index("zc") == core, taps, swapped)
     spectrum = transform_filter(taps, tables)
     gathered = lax.all_to_all(gated, CHIPS, split_axis=0, concat_axis=0, tiled=True)
-    out_other = to_sibling(out_other)
+    out_mine = jnp.where(first_core, out_first, out_second)
+    out_other = to_sibling(jnp.where(first_core, out_second, out_first))
     attn_out = jnp.stack(
         [
             jnp.where(first_core, out_mine, out_other).reshape(STEPS, -1, tokens),

time: 171 us -> 176 us (1.029)
  other arithmetic: 8.15 us -> 12.9 us
  waiting for transfers between devices: 92.2 us -> 87.6 us
  Pallas kernels: 28.2 us -> 31 us
  starting transfers between devices: 33.9 us -> 35.9 us
    and x1 -> x2, other arithmetic: 0.08 us -> 3.98 us  [chip_bias(): earlier = ((picked == 1) & (key_ids[:, None] >= 0))[:, None, :, None]]
    ppermute x2, waiting for transfers between devices: 19.6 us -> 16 us  [send(): lax.ppermute(value, ALL, [(source, target(source) % count) for source in...]
    all_to_all x1, starting transfers between devices: 10.1 us -> 13.2 us  [body(): lax.all_to_all(gated, CHIPS, split_axis=0, concat_axis=0, tiled=True)]
    pallas_call x1 -> x2, Pallas kernels: 7.74 us -> 10.6 us  [attend(): pl.pallas_call(functools.partial(attend_kernel, parity), grid_spec=pltpu....]
    add x2 -> x3, other arithmetic: 0.08 us -> 2.7 us  [records(): return base[:, None] + (lanes[None, :] >= start[:, None]).astype(jnp.int32)]
    another operation x3, other arithmetic: 3.67 us -> 1.3 us  [pick_heads(): jnp.stack([lax.dynamic_index_in_dim(pair, which, 1, keepdims=False).resha...]
    dynamic_slice x5, local copies, waits for them, and re-layouts: 3.44 us -> 1.53 us  [pick_heads(): lax.dynamic_index_in_dim(pair, which, 1, keepdims=False).reshape(-1, tokens)]
    ppermute x1, waiting for transfers between devices: 18.6 us -> 20.4 us  [second_next_chip(): value = lax.ppermute(value, 'y', [(y, (y - 1) % ring) for y in range(ring)])]
  transfers between devices with their start and end apart: 11 -> 11, of which waited for: 9 -> 6; matrix products, arithmetic and copies ran while one was open for 6% -> 8% of each run, Pallas kernels for 9% -> 11%
where the time goes in v4:
time: 176 us
  waiting for transfers between devices  87.6 us (50%)
  starting transfers between devices  35.9 us (20%)
  Pallas kernels  31 us (18%)
  other arithmetic  12.9 us (7%)
  local copies, waits for them, and re-layouts  7.14 us (4%)
    all_to_all x1, waiting for transfers between devices, body(): lax.all_to_all(conv_out, OWNERS, split_axis=0, concat_axis=0, tiled=True)  26.1 us
    ppermute x1, waiting for transfers between devices, second_next_chip(): value = lax.ppermute(value, 'y', [(y, (y - 1) % ring) for y in range(ring)])  20.4 us
    all_to_all x1, waiting for transfers between devices, body(): lax.all_to_all(gated, CHIPS, split_axis=0, concat_axis=0, tiled=True)  19.6 us
    ppermute x2, waiting for transfers between devices, send(): lax.ppermute(value, ALL, [(source, target(source) % count) for source in...  16 us
    all_to_all x1, starting transfers between devices, body(): lax.all_to_all(gated, CHIPS, split_axis=0, concat_axis=0, tiled=True)  13.2 us
    pallas_call x1, Pallas kernels, convolve(): pl.pallas_call(conv_kernel, grid=(channels // step_channels,), in_specs=[...  12.4 us
    pallas_call x2, Pallas kernels, attend(): pl.pallas_call(functools.partial(attend_kernel, parity), grid_spec=pltpu....  10.6 us
    all_to_all x1, starting transfers between devices, body(): lax.all_to_all(conv_out, OWNERS, split_axis=0, concat_axis=0, tiled=True)  9.05 us
  transfers between devices with their start and end apart: 11, of which 6 were waited for; matrix products, arithmetic and copies ran while one was open for 8% of the time, Pallas kernels for 11%

profile of v4, /device:TPU:1, one launch (start us, length us, event | category | flops | bytes accessed | tf_op | source)
XLA Modules:
  0.0 175.6 jit_solution(9848862217663694335)
XLA Ops:
  0.7 1.4 constant_dynamic-slice_fusion.4
  3.1 3.2 %collective-permute-start.1 = (bf16[2,2048,128]{2,1,0:T(8,128)(2,1)}, bf16[2,2048,128]{2,1,0:T(8,128)(2,1)S(1)}, u32[]{:S(2)}, u32[]{:S(2)}) collective-permute-start(bf16[2,2048,128]{2,1,0:T(8,128)(2,1)} %pad_maximum_fusion), channel_id=1, source_target_pairs={{0,1},{1,0},{2,3},{3,2},{4,5},{5,4},{6,7},{7,6},{8,9},{9,8},{10,11... | collective-permute-start | bytes 3145736 | tf_op jit(solution)/shard_map/ppermute | solution.py:376
  7.4 2.6 %fusion.11 = (s32[128]{0:T(128)S(1)}, s32[128]{0:T(128)S(1)}) fusion(s32[]{:T(128)} %get-tuple-element.46, s32[]{:T(128)} %get-tuple-element.45, s32[]{:T(128)} %get-tuple-element.47, s32[]{:T(128)} %get-tuple-element.44), kind=kLoop, calls=%fused_computation.65 | loop fusion | flops 768 | bytes 1040 | tf_op jit(solution)/shard_map/add | solution.py:330
  11.3 2.0 %compare_and_fusion.1 = (pred[4]{0:T(512)(128)(4,1)S(1)}, s32[4]{0:T(128)S(1)}) fusion(s32[]{:T(128)} %bitcast.8, s32[]{:T(128)} %bitcast.7, s32[]{:T(128)} %bitcast.6, s32[]{:T(128)} %mul.22, s32[1]{0:T(128)} %bitcast.4, s32[1]{0:T(128)} %bitcast.3, s32[1]{0:T(128)} %bitcast.2, s32[1]{0:T(128)} %bitcast.1), kind=kLoop, calls=%fused_computation.40 | loop fusion | flops 52 | bytes 52 | tf_op jit(solution)/shard_map/and | solution.py:338
  13.2 2.0 %compare_and_fusion = (pred[4]{0:T(512)(128)(4,1)S(1)}, s32[4]{0:T(128)S(1)}, pred[4]{0:T(512)(128)(4,1)S(1)}) fusion(s32[]{:T(128)} %bitcast.17, s32[]{:T(128)} %bitcast.16, s32[]{:T(128)} %bitcast.15, s32[]{:T(128)S(6)} %add.106, s32[1]{0:T(128)} %bitcast.13, s32[1]{0:T(128)} %bitcast.12, s32[1]{0:T(128)} %bitcast.2, s32[1]{0:T(128)} %bitcast.1, ...), kind=kLoop, calls=%fused_computation.33 | loop fusion | flops 60 | bytes 76 | tf_op jit(solution)/shard_map/and | solution.py:338
  16.7 2.1 %collective-permute-start.5 = (bf16[2,2048,128]{2,1,0:T(8,128)(2,1)S(1)}, bf16[2,2048,128]{2,1,0:T(8,128)(2,1)}, u32[]{:S(2)}, u32[]{:S(2)}) collective-permute-start(bf16[2,2048,128]{2,1,0:T(8,128)(2,1)S(1)} %get-tuple-element.55), channel_id=1, source_target_pairs={{0,6},{2,0},{4,2},{6,4},{1,7},{3,1},{5,3},{7,5},{8,14},{10,8},{12,... | collective-permute-start | bytes 3145736 | tf_op jit(solution)/shard_map/ppermute | solution.py:369
  19.1 1.3 fusion.6
  21.0 20.4 %collective-permute-done.5 = bf16[2,2048,128]{2,1,0:T(8,128)(2,1)} collective-permute-done((bf16[2,2048,128]{2,1,0:T(8,128)(2,1)S(1)}, bf16[2,2048,128]{2,1,0:T(8,128)(2,1)}, u32[]{:S(2)}, u32[]{:S(2)}) %collective-permute-start.5) | collective-permute-done | bytes 1048608 | tf_op jit(solution)/shard_map/ppermute | solution.py:369
  41.4 3.5 %collective-permute-start.6 = (bf16[2,2048,128]{2,1,0:T(8,128)(2,1)}, bf16[2,2048,128]{2,1,0:T(8,128)(2,1)}, u32[]{:S(2)}, u32[]{:S(2)}) collective-permute-start(bf16[2,2048,128]{2,1,0:T(8,128)(2,1)} %collective-permute-done.5), channel_id=1, source_target_pairs={{6,4},{7,5},{0,6},{1,7},{2,8},{3,9},{4,10},{5,11},{14,12},{15,13},... | collective-permute-start | bytes 3145736 | tf_op jit(solution)/shard_map/ppermute | solution.py:370
  45.1 16.0 %collective-permute-done.3.near = bf16[2,2048,128]{2,1,0:T(8,128)(2,1)S(1)} collective-permute-done((bf16[2,2048,128]{2,1,0:T(8,128)(2,1)S(1)}, bf16[2,2048,128]{2,1,0:T(8,128)(2,1)S(1)}, u32[]{:S(2)}, u32[]{:S(2)}) %collective-permute-start.3) | collective-permute-done | bytes 1048608 | tf_op jit(solution)/shard_map/ppermute | solution.py:351
  61.1 1.9 %collective-permute-start.8 = (bf16[16,256,128]{2,1,0:T(8,128)(2,1)S(1)}, bf16[16,256,128]{2,1,0:T(8,128)(2,1)S(1)}, u32[]{:S(2)}, u32[]{:S(2)}) collective-permute-start(bf16[16,256,128]{2,1,0:T(8,128)(2,1)S(1)} %bitcast.81), channel_id=1, source_target_pairs={{1,32},{3,34},{5,36},{7,38},{9,40},{11,42},{13,44},{15,46},{17,48}... | collective-permute-start | bytes 3145736 | tf_op jit(solution)/shard_map/ppermute | solution.py:422
  64.0 5.2 %attend_second.1 = (bf16[2048,128]{1,0:T(8,128)(2,1)}, bf16[128,2,16,128]{3,2,1,0:T(8,128)(2,1)}) custom-call(s32[1]{0:T(128)} %bitcast.core_ref, f32[512,128]{1,0:T(8,128)} %get-tuple-element.30.bias_ref, bf16[4,2,512,128]{3,2,1,0:T(8,128)(2,1)} %bitcast.75, bf16[4,2,512,128]{3,2,1,0:T(8,128)(2,1)} %bitcast.78, bf16[2,2048,128]{2,1,0:T(8,128)(2,1)} %copy-done, ...), custom_call_target="tpu_custom_call" | custom-call | flops 536870912 | bytes 8650752 | tf_op jit(solution)/shard_map/attend_second/pallas_call | solution.py:292
  69.2 4.0 %collective-permute-done.6.rest_0_ = bf16[2,2048,128]{2,1,0:T(8,128)(2,1)} collective-permute-done((bf16[2,2048,128]{2,1,0:T(8,128)(2,1)}, bf16[2,2048,128]{2,1,0:T(8,128)(2,1)}, u32[]{:S(2)}, u32[]{:S(2)}) %collective-permute-start.6) | collective-permute-done | bytes 1048608 | tf_op jit(solution)/shard_map/ppermute | solution.py:370
  73.2 5.4 %attend_first.1 = (bf16[2048,128]{1,0:T(8,128)(2,1)}, bf16[128,2,16,128]{3,2,1,0:T(8,128)(2,1)}) custom-call(s32[1]{0:T(128)} %bitcast.core_ref, f32[512,128]{1,0:T(8,128)} %get-tuple-element.24.bias_ref, bf16[4,2,512,128]{3,2,1,0:T(8,128)(2,1)} %bitcast.76, bf16[4,2,512,128]{3,2,1,0:T(8,128)(2,1)} %bitcast.79, ...), custom_call_target="tpu_custom_call", output_to_operand_aliasing={{1}: (11, {})} | custom-call | flops 536870912 | bytes 8650752 | tf_op jit(solution)/shard_map/attend_first/pallas_call | solution.py:292
  78.6 13.2 %all-to-all-start = ((bf16[128,2,16,128]{3,2,1,0:T(8,128)(2,1)}), bf16[128,2,16,128]{3,2,1,0:T(8,128)(2,1)S(1)}, u32[]{:S(2)}, u32[]{:S(2)}) async-start(bf16[128,2,16,128]{3,2,1,0:T(8,128)(2,1)} %get-tuple-element.36), calls=%async_computation | async-start | bytes 2097152 | tf_op jit(solution)/shard_map/all_to_all | solution.py:432
  91.8 1.1 broadcast_select_fusion.filter_ref
  92.9 8.0 %filter_spectrum.1.spectrum_ref = f32[4096,256]{1,0:T(8,128)} custom-call(bf16[16,256,128]{2,1,0:T(8,128)(2,1)} %broadcast_select_fusion.filter_ref, bf16[512,512]{1,0:T(8,128)(2,1)} %constant.84.clone.rest_0_, f32[256,128]{1,0:T(8,128)} %constant.85.clone.rest_1_, f32[256,128]{1,0:T(8,128)} %constant.86.clone.rest_2_, bf16[768,256]{1,0:T(8,128)(2,1)} %constant.87.clone.rest_3_), custom_call_target="tpu_custom_call" | custom-call | flops 2720000000 | bytes 6291456 | tf_op jit(solution)/shard_map/filter_spectrum/pallas_call | solution.py:176
  100.8 19.6 %all-to-all-done = bf16[128,2,16,128]{3,2,1,0:T(8,128)(2,1)S(1)} async-done(((bf16[128,2,16,128]{3,2,1,0:T(8,128)(2,1)}), bf16[128,2,16,128]{3,2,1,0:T(8,128)(2,1)S(1)}, u32[]{:S(2)}, u32[]{:S(2)}) %all-to-all-start) | async-done | bytes 1048608 | tf_op jit(solution)/shard_map/all_to_all | solution.py:432
  121.4 12.4 %convolve.1 = bf16[256,16,128]{2,1,0:T(8,128)(2,1)} custom-call(bf16[256,16,128]{2,1,0:T(8,128)(2,1)} %bitcast.96, f32[4096,256]{1,0:T(8,128)} %filter_spectrum.1.spectrum_ref, bf16[512,512]{1,0:T(8,128)(2,1)} %constant.88.clone.rest_0_, f32[256,128]{1,0:T(8,128)} %constant.85.clone.rest_1_, f32[256,128]{1,0:T(8,128)} %constant.86.clone.rest_2_, ...), custom_call_target="tpu_custom_call" | custom-call | flops 5920000000 | bytes 8388608 | tf_op jit(solution)/shard_map/convolve/pallas_call | solution.py:195
  133.8 9.1 %all-to-all-start.1 = ((bf16[256,16,128]{2,1,0:T(8,128)(2,1)}), bf16[256,16,128]{2,1,0:T(8,128)(2,1)S(1)}, u32[]{:S(2)}, u32[]{:S(2)}) async-start(bf16[256,16,128]{2,1,0:T(8,128)(2,1)} %convolve.1), calls=%async_computation.1 | async-start | bytes 2097152 | tf_op jit(solution)/shard_map/all_to_all | solution.py:444
  143.0 2.4 %collective-permute-start.7 = (bf16[2048,128]{1,0:T(8,128)(2,1)S(1)}, bf16[2048,128]{1,0:T(8,128)(2,1)S(1)}, u32[]{:S(2)}, u32[]{:S(2)}) collective-permute-start(bf16[2048,128]{1,0:T(8,128)(2,1)S(1)} %broadcast_select_fusion.4), channel_id=1, source_target_pairs={{0,1},{1,0},{2,3},{3,2},{4,5},{5,4},{6,7},{7,6},{8,9},{9,8},{10,11... | collective-permute-start | bytes 1572872 | tf_op jit(solution)/shard_map/ppermute | solution.py:376
  145.4 1.5 collective-permute-done.7
  148.2 26.1 %all-to-all-done.1 = bf16[256,16,128]{2,1,0:T(8,128)(2,1)S(1)} async-done(((bf16[256,16,128]{2,1,0:T(8,128)(2,1)}), bf16[256,16,128]{2,1,0:T(8,128)(2,1)S(1)}, u32[]{:S(2)}, u32[]{:S(2)}) %all-to-all-start.1) | async-done | bytes 1048608 | tf_op jit(solution)/shard_map/all_to_all | solution.py:444
  174.3 1.3 fusion
  (67 shorter events, 9.0 us)
Async XLA Ops:
  0.6 5.7 %copy-start.14 = (s32[1,3]{1,0:T(1,128)S(1)}, s32[1,3]{1,0:T(1,128)}, u32[]{:S(2)}) copy-start(s32[1,3]{1,0:T(1,128)} %param.19) | copy-start | bytes 40
  0.6 5.8 %copy-start.13 = (s32[256]{0:T(256)S(1)}, s32[256]{0:T(256)}, u32[]{:S(2)}) copy-start(s32[256]{0:T(256)} %param.18) | copy-start | bytes 3076
  0.7 6.6 %copy-start.9 = (bf16[4096,128]{1,0:T(8,128)(2,1)S(1)}, bf16[4096,128]{1,0:T(8,128)(2,1)}, u32[]{:S(2)}) copy-start(bf16[4096,128]{1,0:T(8,128)(2,1)} %param.17) | copy-start | bytes 3145732
  2.0 5.3 %copy-start.10 = (bf16[4096,128]{1,0:T(8,128)(2,1)S(1)}, bf16[4096,128]{1,0:T(8,128)(2,1)}, u32[]{:S(2)}) copy-start(bf16[4096,128]{1,0:T(8,128)(2,1)} %param.16) | copy-start | bytes 3145732
  3.1 12.6 %collective-permute-start.1 = (bf16[2,2048,128]{2,1,0:T(8,128)(2,1)}, bf16[2,2048,128]{2,1,0:T(8,128)(2,1)S(1)}, u32[]{:S(2)}, u32[]{:S(2)}) collective-permute-start(bf16[2,2048,128]{2,1,0:T(8,128)(2,1)} %pad_maximum_fusion), channel_id=1, source_target_pairs={{0,1},{1,0},{2,3},{3,2},{4,5},{5,4},{6,7},{7,6},{8,9},{9,8},{10,11... | collective-permute-start | bytes 3145736 | tf_op jit(solution)/shard_map/ppermute | solution.py:376
  6.4 38.7 %collective-permute-start.4 = (bf16[2,2048,128]{2,1,0:T(8,128)(2,1)}, bf16[2,2048,128]{2,1,0:T(8,128)(2,1)}, u32[]{:S(2)}, u32[]{:S(2)}) collective-permute-start(bf16[2,2048,128]{2,1,0:T(8,128)(2,1)} %pad_maximum_fusion), channel_id=1, source_target_pairs={{0,3},{1,2},{2,5},{3,4},{4,7},{5,6},{6,9},{7,8},{8,11},{9,10},{10,... | collective-permute-start | bytes 3145736 | tf_op jit(solution)/shard_map/ppermute | solution.py:351
  6.4 3.6 %collective-permute-start = (f32[1,3]{1,0:T(1,128)S(1)}, f32[1,3]{1,0:T(1,128)S(1)}, u32[]{:S(2)}, u32[]{:S(2)}) collective-permute-start(f32[1,3]{1,0:T(1,128)S(1)} %convert_element_type.59), channel_id=1, source_target_pairs={{0,1},{1,0},{2,3},{3,2},{4,5},{5,4},{6,7},{7,6},{8,9},{9,8},{10,11... | collective-permute-start | bytes 44 | tf_op jit(solution)/shard_map/ppermute | solution.py:376
  15.7 1.0 copy-start.1
  15.7 4.6 %copy-start.4 = (bf16[4096,128]{1,0:T(8,128)(2,1)S(1)}, bf16[4096,128]{1,0:T(8,128)(2,1)}, u32[]{:S(2)}) copy-start(bf16[4096,128]{1,0:T(8,128)(2,1)} %param.20) | copy-start | bytes 3145732
  15.7 4.7 %copy-start.3 = (bf16[4096,128]{1,0:T(8,128)(2,1)S(1)}, bf16[4096,128]{1,0:T(8,128)(2,1)}, u32[]{:S(2)}) copy-start(bf16[4096,128]{1,0:T(8,128)(2,1)} %param.15) | copy-start | bytes 3145732
  16.7 3.9 %copy-start.2 = (bf16[2,2048,128]{2,1,0:T(8,128)(2,1)}, bf16[2,2048,128]{2,1,0:T(8,128)(2,1)S(1)}, u32[]{:S(2)}) copy-start(bf16[2,2048,128]{2,1,0:T(8,128)(2,1)S(1)} %get-tuple-element.54.own) | copy-start | bytes 3145732
  16.7 24.7 %collective-permute-start.5 = (bf16[2,2048,128]{2,1,0:T(8,128)(2,1)S(1)}, bf16[2,2048,128]{2,1,0:T(8,128)(2,1)}, u32[]{:S(2)}, u32[]{:S(2)}) collective-permute-start(bf16[2,2048,128]{2,1,0:T(8,128)(2,1)S(1)} %get-tuple-element.55), channel_id=1, source_target_pairs={{0,6},{2,0},{4,2},{6,4},{1,7},{3,1},{5,3},{7,5},{8,14},{10,8},{12,... | collective-permute-start | bytes 3145736 | tf_op jit(solution)/shard_map/ppermute | solution.py:369
  18.9 42.2 %collective-permute-start.3 = (bf16[2,2048,128]{2,1,0:T(8,128)(2,1)S(1)}, bf16[2,2048,128]{2,1,0:T(8,128)(2,1)S(1)}, u32[]{:S(2)}, u32[]{:S(2)}) collective-permute-start(bf16[2,2048,128]{2,1,0:T(8,128)(2,1)S(1)} %get-tuple-element.54.own), channel_id=1, source_target_pairs={{0,2},{1,3},{2,4},{3,5},{4,6},{5,7},{6,8},{7,9},{8,10},{9,11},{10,... | collective-permute-start | bytes 3145736 | tf_op jit(solution)/shard_map/ppermute | solution.py:351
  20.4 24.5 %copy-start.11 = (bf16[16,32768]{1,0:T(8,128)(2,1)S(1)}, bf16[16,32768]{1,0:T(8,128)(2,1)}, u32[]{:S(2)}) copy-start(bf16[16,32768]{1,0:T(8,128)(2,1)} %param.22) | copy-start | bytes 3145732
  20.6 42.4 %collective-permute-start.2 = (bf16[2,2048,128]{2,1,0:T(8,128)(2,1)S(1)}, bf16[2,2048,128]{2,1,0:T(8,128)(2,1)S(1)}, u32[]{:S(2)}, u32[]{:S(2)}) collective-permute-start(bf16[2,2048,128]{2,1,0:T(8,128)(2,1)S(1)} %pad_maximum_fusion.2), channel_id=1, source_target_pairs={{0,1},{1,0},{2,3},{3,2},{4,5},{5,4},{6,7},{7,6},{8,9},{9,8},{10,11... | collective-permute-start | bytes 3145736 | tf_op jit(solution)/shard_map/ppermute | solution.py:376
  41.4 31.8 %collective-permute-start.6 = (bf16[2,2048,128]{2,1,0:T(8,128)(2,1)}, bf16[2,2048,128]{2,1,0:T(8,128)(2,1)}, u32[]{:S(2)}, u32[]{:S(2)}) collective-permute-start(bf16[2,2048,128]{2,1,0:T(8,128)(2,1)} %collective-permute-done.5), channel_id=1, source_target_pairs={{6,4},{7,5},{0,6},{1,7},{2,8},{3,9},{4,10},{5,11},{14,12},{15,13},... | collective-permute-start | bytes 3145736 | tf_op jit(solution)/shard_map/ppermute | solution.py:370
  61.1 1.9 %copy-start.5 = (bf16[2,2048,128]{2,1,0:T(8,128)(2,1)}, bf16[2,2048,128]{2,1,0:T(8,128)(2,1)S(1)}, u32[]{:S(2)}) copy-start(bf16[2,2048,128]{2,1,0:T(8,128)(2,1)S(1)} %collective-permute-done.3.near) | copy-start | bytes 3145732
  61.1 17.5 %collective-permute-start.8 = (bf16[16,256,128]{2,1,0:T(8,128)(2,1)S(1)}, bf16[16,256,128]{2,1,0:T(8,128)(2,1)S(1)}, u32[]{:S(2)}, u32[]{:S(2)}) collective-permute-start(bf16[16,256,128]{2,1,0:T(8,128)(2,1)S(1)} %bitcast.81), channel_id=1, source_target_pairs={{1,32},{3,34},{5,36},{7,38},{9,40},{11,42},{13,44},{15,46},{17,48}... | collective-permute-start | bytes 3145736 | tf_op jit(solution)/shard_map/ppermute | solution.py:422
  78.6 41.8 %all-to-all-start = ((bf16[128,2,16,128]{3,2,1,0:T(8,128)(2,1)}), bf16[128,2,16,128]{3,2,1,0:T(8,128)(2,1)S(1)}, u32[]{:S(2)}, u32[]{:S(2)}) async-start(bf16[128,2,16,128]{3,2,1,0:T(8,128)(2,1)} %get-tuple-element.36), calls=%async_computation | async-start | bytes 2097152 | tf_op jit(solution)/shard_map/all_to_all | solution.py:432
  133.8 9.1 %copy-start.6 = (bf16[2048,128]{1,0:T(8,128)(2,1)S(1)}, bf16[2048,128]{1,0:T(8,128)(2,1)}, u32[]{:S(2)}) copy-start(bf16[2048,128]{1,0:T(8,128)(2,1)} %get-tuple-element.33) | copy-start | bytes 1572868
  133.8 9.1 %copy-start.7 = (bf16[2048,128]{1,0:T(8,128)(2,1)S(1)}, bf16[2048,128]{1,0:T(8,128)(2,1)}, u32[]{:S(2)}) copy-start(bf16[2048,128]{1,0:T(8,128)(2,1)} %get-tuple-element.32) | copy-start | bytes 1572868
  133.8 40.4 %all-to-all-start.1 = ((bf16[256,16,128]{2,1,0:T(8,128)(2,1)}), bf16[256,16,128]{2,1,0:T(8,128)(2,1)S(1)}, u32[]{:S(2)}, u32[]{:S(2)}) async-start(bf16[256,16,128]{2,1,0:T(8,128)(2,1)} %convolve.1), calls=%async_computation.1 | async-start | bytes 2097152 | tf_op jit(solution)/shard_map/all_to_all | solution.py:444
  143.0 3.9 %collective-permute-start.7 = (bf16[2048,128]{1,0:T(8,128)(2,1)S(1)}, bf16[2048,128]{1,0:T(8,128)(2,1)S(1)}, u32[]{:S(2)}, u32[]{:S(2)}) collective-permute-start(bf16[2048,128]{1,0:T(8,128)(2,1)S(1)} %broadcast_select_fusion.4), channel_id=1, source_target_pairs={{0,1},{1,0},{2,3},{3,2},{4,5},{5,4},{6,7},{7,6},{8,9},{9,8},{10,11... | collective-permute-start | bytes 1572872 | tf_op jit(solution)/shard_map/ppermute | solution.py:376
  147.0 27.3 %copy-start.8 = (bf16[4096,128]{1,0:T(8,128)(2,1)S(1)}, bf16[4096,128]{1,0:T(8,128)(2,1)}, u32[]{:S(2)}) copy-start(bf16[4096,128]{1,0:T(8,128)(2,1)} %param.21) | copy-start | bytes 3145732
  (2 other events, 1.9 us)

commit v5 on v4

--- a/solution.py
+++ b/solution.py
@@ -391,15 +391,16 @@
     mine = pick_heads(core, k_later, v_later)
     near = next_chip(mine)
     odd = jnp.where(first_core, sibling, mine)
+    starts, picked, odd = lax.optimization_barrier((block_start, kv_select, odd))
     far = second_next_chip(odd)
-    flags = kv_select.astype(jnp.float32)
+    flags = picked.astype(jnp.float32)
     flags = jnp.concatenate([flags, to_sibling(flags)], axis=0).astype(jnp.int32)
     first = 2 * lax.axis_index(ALL[:-1])
     near_ids = [first - 2 + core, first - 1 - core]
     windows = [[first - 3, first], [first + core, first + 1 - core]]
     biases = [
         chip_bias(
-            block_start,
+            starts,
             jnp.where(core == parity, flags[:1], flags[1:]),
             jnp.stack(near_ids + windows[parity]),
             jnp.stack([first + parity]),

time: 176 us -> 171 us (0.972)
  starting transfers between devices: 35.9 us -> 30.7 us
  waiting for transfers between devices: 87.6 us -> 85.3 us
    ppermute x1, waiting for transfers between devices: 20.4 us -> 11.9 us  [second_next_chip(): value = lax.ppermute(value, 'y', [(y, (y - 1) % ring) for y in range(ring)])]
    ppermute x2, waiting for transfers between devices: 16 us -> 22.3 us  [send(): lax.ppermute(value, ALL, [(source, target(source) % count) for source in...]
    all_to_all x1, starting transfers between devices: 13.2 us -> 8.11 us  [body(): lax.all_to_all(gated, CHIPS, split_axis=0, concat_axis=0, tiled=True)]
    ppermute x1, waiting for transfers between devices: 4.03 us -> 0.01 us  [second_next_chip(): lax.ppermute(value, ALL, [(between(source), (source + 4) % count) for sou...]
    ppermute x1, waiting for transfers between devices: 0.01 us -> 2.8 us  [body(): swapped = lax.ppermute(taps, ALL, moved)]
    ppermute x4, waiting for transfers between devices: 1.54 us -> 3.91 us  [to_sibling(): return lax.ppermute(value, 'c', [(0, 1), (1, 0)])]
  transfers between devices with their start and end apart: 11 -> 11, of which waited for: 6 -> 8; matrix products, arithmetic and copies ran while one was open for 8% -> 9% of each run, Pallas kernels for 11% -> 11%
where the time goes in v5:
time: 171 us; the launch traced here: 170 us
  waiting for transfers between devices  85.3 us (50%)
  Pallas kernels  30.9 us (18%)
  starting transfers between devices  30.7 us (18%)
  other arithmetic  14.2 us (8%)
  local copies, waits for them, and re-layouts  8.2 us (5%)
    all_to_all x1, waiting for transfers between devices, body(): lax.all_to_all(conv_out, OWNERS, split_axis=0, concat_axis=0, tiled=True)  26.1 us
    ppermute x2, waiting for transfers between devices, send(): lax.ppermute(value, ALL, [(source, target(source) % count) for source in...  22.3 us
    all_to_all x1, waiting for transfers between devices, body(): lax.all_to_all(gated, CHIPS, split_axis=0, concat_axis=0, tiled=True)  18.3 us
    pallas_call x1, Pallas kernels, convolve(): pl.pallas_call(conv_kernel, grid=(channels // step_channels,), in_specs=[...  12.5 us
    ppermute x1, waiting for transfers between devices, second_next_chip(): value = lax.ppermute(value, 'y', [(y, (y - 1) % ring) for y in range(ring)])  11.9 us
    pallas_call x2, Pallas kernels, attend(): pl.pallas_call(functools.partial(attend_kernel, parity), grid_spec=pltpu....  10.5 us
    all_to_all x1, starting transfers between devices, body(): lax.all_to_all(conv_out, OWNERS, split_axis=0, concat_axis=0, tiled=True)  9.13 us
    all_to_all x1, starting transfers between devices, body(): lax.all_to_all(gated, CHIPS, split_axis=0, concat_axis=0, tiled=True)  8.11 us
  transfers between devices with their start and end apart: 11, of which 8 were waited for; matrix products, arithmetic and copies ran while one was open for 9% of the time, Pallas kernels for 11%

profile of v5, /device:TPU:1, one launch (start us, length us, event | category | flops | bytes accessed | tf_op | source)
XLA Modules:
  0.0 170.2 jit_solution(2439762055140478671)
XLA Ops:
  4.2 3.2 %collective-permute-start = (bf16[2,2048,128]{2,1,0:T(8,128)(2,1)}, bf16[2,2048,128]{2,1,0:T(8,128)(2,1)S(1)}, u32[]{:S(2)}, u32[]{:S(2)}) collective-permute-start(bf16[2,2048,128]{2,1,0:T(8,128)(2,1)} %pad_maximum_fusion), channel_id=1, source_target_pairs={{0,1},{1,0},{2,3},{3,2},{4,5},{5,4},{6,7},{7,6},{8,9},{9,8},{10,11... | collective-permute-start | bytes 3145736 | tf_op jit(solution)/shard_map/ppermute | solution.py:376
  7.5 2.4 %collective-permute-done.sibling = bf16[2,2048,128]{2,1,0:T(8,128)(2,1)S(1)} collective-permute-done((bf16[2,2048,128]{2,1,0:T(8,128)(2,1)}, bf16[2,2048,128]{2,1,0:T(8,128)(2,1)S(1)}, u32[]{:S(2)}, u32[]{:S(2)}) %collective-permute-start) | collective-permute-done | bytes 1048608 | tf_op jit(solution)/shard_map/ppermute | solution.py:376
  12.1 1.9 %collective-permute-start.5 = (bf16[2,2048,128]{2,1,0:T(8,128)(2,1)S(1)}, bf16[2,2048,128]{2,1,0:T(8,128)(2,1)}, u32[]{:S(2)}, u32[]{:S(2)}) collective-permute-start(bf16[2,2048,128]{2,1,0:T(8,128)(2,1)S(1)} %get-tuple-element.27), channel_id=1, source_target_pairs={{0,6},{2,0},{4,2},{6,4},{1,7},{3,1},{5,3},{7,5},{8,14},{10,8},{12,... | collective-permute-start | bytes 3145736 | tf_op jit(solution)/shard_map/ppermute | solution.py:369
  13.9 2.5 %fusion.11 = (s32[128]{0:T(128)S(1)}, s32[128]{0:T(128)S(1)}) fusion(s32[]{:T(128)} %get-tuple-element.52, s32[]{:T(128)} %get-tuple-element.51, s32[]{:T(128)} %get-tuple-element.53, s32[]{:T(128)} %get-tuple-element.50), kind=kLoop, calls=%fused_computation.65 | loop fusion | flops 768 | bytes 1040 | tf_op jit(solution)/shard_map/add | solution.py:330
  17.8 2.0 %compare_and_fusion.1 = (pred[4]{0:T(512)(128)(4,1)S(1)}, s32[4]{0:T(128)S(1)}) fusion(s32[]{:T(128)} %bitcast.16, s32[]{:T(128)} %bitcast.15, s32[]{:T(128)} %bitcast.14, s32[]{:T(128)} %mul.22, s32[1]{0:T(128)} %bitcast.4, s32[1]{0:T(128)} %bitcast.3, s32[1]{0:T(128)} %bitcast.2, s32[1]{0:T(128)} %bitcast.1), kind=kLoop, calls=%fused_computation.40 | loop fusion | flops 52 | bytes 52 | tf_op jit(solution)/shard_map/and | solution.py:338
  19.8 2.0 %compare_and_fusion = (pred[4]{0:T(512)(128)(4,1)S(1)}, s32[4]{0:T(128)S(1)}, pred[4]{0:T(512)(128)(4,1)S(1)}) fusion(s32[]{:T(128)} %bitcast.25, s32[]{:T(128)} %bitcast.24, s32[]{:T(128)} %bitcast.23, s32[]{:T(128)S(6)} %add.108, s32[1]{0:T(128)} %bitcast.21, s32[1]{0:T(128)} %bitcast.20, s32[1]{0:T(128)} %bitcast.2, s32[1]{0:T(128)} %bitcast.1, ...), kind=kLoop, calls=%fused_computation.33 | loop fusion | flops 60 | bytes 76 | tf_op jit(solution)/shard_map/and | solution.py:338
  22.5 1.3 fusion.6
  24.8 11.9 %collective-permute-done.5 = bf16[2,2048,128]{2,1,0:T(8,128)(2,1)} collective-permute-done((bf16[2,2048,128]{2,1,0:T(8,128)(2,1)S(1)}, bf16[2,2048,128]{2,1,0:T(8,128)(2,1)}, u32[]{:S(2)}, u32[]{:S(2)}) %collective-permute-start.5) | collective-permute-done | bytes 1048608 | tf_op jit(solution)/shard_map/ppermute | solution.py:369
  36.8 2.8 %collective-permute-start.6 = (bf16[2,2048,128]{2,1,0:T(8,128)(2,1)}, bf16[2,2048,128]{2,1,0:T(8,128)(2,1)}, u32[]{:S(2)}, u32[]{:S(2)}) collective-permute-start(bf16[2,2048,128]{2,1,0:T(8,128)(2,1)} %collective-permute-done.5), channel_id=1, source_target_pairs={{6,4},{7,5},{0,6},{1,7},{2,8},{3,9},{4,10},{5,11},{14,12},{15,13},... | collective-permute-start | bytes 3145736 | tf_op jit(solution)/shard_map/ppermute | solution.py:370
  39.8 22.3 %collective-permute-done.3.near = bf16[2,2048,128]{2,1,0:T(8,128)(2,1)S(1)} collective-permute-done((bf16[2,2048,128]{2,1,0:T(8,128)(2,1)S(1)}, bf16[2,2048,128]{2,1,0:T(8,128)(2,1)S(1)}, u32[]{:S(2)}, u32[]{:S(2)}) %collective-permute-start.3) | collective-permute-done | bytes 1048608 | tf_op jit(solution)/shard_map/ppermute | solution.py:351
  62.1 1.9 %collective-permute-start.8 = (bf16[16,256,128]{2,1,0:T(8,128)(2,1)S(1)}, bf16[16,256,128]{2,1,0:T(8,128)(2,1)}, u32[]{:S(2)}, u32[]{:S(2)}) collective-permute-start(bf16[16,256,128]{2,1,0:T(8,128)(2,1)S(1)} %bitcast.83), channel_id=1, source_target_pairs={{1,32},{3,34},{5,36},{7,38},{9,40},{11,42},{13,44},{15,46},{17,48}... | collective-permute-start | bytes 3145736 | tf_op jit(solution)/shard_map/ppermute | solution.py:423
  65.0 5.1 %attend_second.1 = (bf16[2048,128]{1,0:T(8,128)(2,1)}, bf16[128,2,16,128]{3,2,1,0:T(8,128)(2,1)}) custom-call(s32[1]{0:T(128)} %bitcast.core_ref, f32[512,128]{1,0:T(8,128)} %get-tuple-element.36.bias_ref, bf16[4,2,512,128]{3,2,1,0:T(8,128)(2,1)} %bitcast.77, bf16[4,2,512,128]{3,2,1,0:T(8,128)(2,1)} %bitcast.80, bf16[2,2048,128]{2,1,0:T(8,128)(2,1)} %copy-done.1, ...), custom_call_target="tpu_custom_call" | custom-call | flops 536870912 | bytes 8650752 | tf_op jit(solution)/shard_map/attend_second/pallas_call | solution.py:292
  70.1 5.4 %attend_first.1 = (bf16[2048,128]{1,0:T(8,128)(2,1)}, bf16[128,2,16,128]{3,2,1,0:T(8,128)(2,1)}) custom-call(s32[1]{0:T(128)} %bitcast.core_ref, f32[512,128]{1,0:T(8,128)} %get-tuple-element.30.bias_ref, bf16[4,2,512,128]{3,2,1,0:T(8,128)(2,1)} %bitcast.78, bf16[4,2,512,128]{3,2,1,0:T(8,128)(2,1)} %bitcast.81, ...), custom_call_target="tpu_custom_call", output_to_operand_aliasing={{1}: (11, {})} | custom-call | flops 536870912 | bytes 8650752 | tf_op jit(solution)/shard_map/attend_first/pallas_call | solution.py:292
  75.5 2.8 %collective-permute-done.8 = bf16[16,256,128]{2,1,0:T(8,128)(2,1)} collective-permute-done((bf16[16,256,128]{2,1,0:T(8,128)(2,1)S(1)}, bf16[16,256,128]{2,1,0:T(8,128)(2,1)}, u32[]{:S(2)}, u32[]{:S(2)}) %collective-permute-start.8) | collective-permute-done | bytes 1048608 | tf_op jit(solution)/shard_map/ppermute | solution.py:423
  78.3 8.1 %all-to-all-start = ((bf16[128,2,16,128]{3,2,1,0:T(8,128)(2,1)}), bf16[128,2,16,128]{3,2,1,0:T(8,128)(2,1)S(1)}, u32[]{:S(2)}, u32[]{:S(2)}) async-start(bf16[128,2,16,128]{3,2,1,0:T(8,128)(2,1)} %get-tuple-element.42), calls=%async_computation | async-start | bytes 2097152 | tf_op jit(solution)/shard_map/all_to_all | solution.py:433
  86.4 2.3 %broadcast_select_fusion.filter_ref = bf16[16,256,128]{2,1,0:T(8,128)(2,1)} fusion(bf16[16,256,128]{2,1,0:T(8,128)(2,1)S(1)} %bitcast.84, bf16[16,256,128]{2,1,0:T(8,128)(2,1)} %collective-permute-done.8, pred[]{:T(512)S(6)} %eq.186), kind=kLoop, calls=%fused_computation.6 | loop fusion | flops 524288 | bytes 3145729 | tf_op jit(solution)/shard_map/jit(_where)/select_n | solution.py:431
  88.7 8.0 %filter_spectrum.1.spectrum_ref = f32[4096,256]{1,0:T(8,128)} custom-call(bf16[16,256,128]{2,1,0:T(8,128)(2,1)} %broadcast_select_fusion.filter_ref, bf16[512,512]{1,0:T(8,128)(2,1)} %constant.84.clone.rest_0_, f32[256,128]{1,0:T(8,128)} %constant.85.clone.rest_1_, f32[256,128]{1,0:T(8,128)} %constant.86.clone.rest_2_, bf16[768,256]{1,0:T(8,128)(2,1)} %constant.87.clone.rest_3_), custom_call_target="tpu_custom_call" | custom-call | flops 2720000000 | bytes 6291456 | tf_op jit(solution)/shard_map/filter_spectrum/pallas_call | solution.py:176
  96.7 18.3 %all-to-all-done = bf16[128,2,16,128]{3,2,1,0:T(8,128)(2,1)S(1)} async-done(((bf16[128,2,16,128]{3,2,1,0:T(8,128)(2,1)}), bf16[128,2,16,128]{3,2,1,0:T(8,128)(2,1)S(1)}, u32[]{:S(2)}, u32[]{:S(2)}) %all-to-all-start) | async-done | bytes 1048608 | tf_op jit(solution)/shard_map/all_to_all | solution.py:433
  116.0 12.5 %convolve.1 = bf16[256,16,128]{2,1,0:T(8,128)(2,1)} custom-call(bf16[256,16,128]{2,1,0:T(8,128)(2,1)} %bitcast.94, f32[4096,256]{1,0:T(8,128)} %filter_spectrum.1.spectrum_ref, bf16[512,512]{1,0:T(8,128)(2,1)} %constant.88.clone.rest_0_, f32[256,128]{1,0:T(8,128)} %constant.85.clone.rest_1_, f32[256,128]{1,0:T(8,128)} %constant.86.clone.rest_2_, ...), custom_call_target="tpu_custom_call" | custom-call | flops 5920000000 | bytes 8388608 | tf_op jit(solution)/shard_map/convolve/pallas_call | solution.py:195
  128.4 9.1 %all-to-all-start.1 = ((bf16[256,16,128]{2,1,0:T(8,128)(2,1)}), bf16[256,16,128]{2,1,0:T(8,128)(2,1)S(1)}, u32[]{:S(2)}, u32[]{:S(2)}) async-start(bf16[256,16,128]{2,1,0:T(8,128)(2,1)} %convolve.1), calls=%async_computation.1 | async-start | bytes 2097152 | tf_op jit(solution)/shard_map/all_to_all | solution.py:445
  137.7 2.4 %collective-permute-start.7 = (bf16[2048,128]{1,0:T(8,128)(2,1)S(1)}, bf16[2048,128]{1,0:T(8,128)(2,1)S(1)}, u32[]{:S(2)}, u32[]{:S(2)}) collective-permute-start(bf16[2048,128]{1,0:T(8,128)(2,1)S(1)} %broadcast_select_fusion.4), channel_id=1, source_target_pairs={{0,1},{1,0},{2,3},{3,2},{4,5},{5,4},{6,7},{7,6},{8,9},{9,8},{10,11... | collective-permute-start | bytes 1572872 | tf_op jit(solution)/shard_map/ppermute | solution.py:376
  140.0 1.5 collective-permute-done.7
  142.8 26.1 %all-to-all-done.1 = bf16[256,16,128]{2,1,0:T(8,128)(2,1)S(1)} async-done(((bf16[256,16,128]{2,1,0:T(8,128)(2,1)}), bf16[256,16,128]{2,1,0:T(8,128)(2,1)S(1)}, u32[]{:S(2)}, u32[]{:S(2)}) %all-to-all-start.1) | async-done | bytes 1048608 | tf_op jit(solution)/shard_map/all_to_all | solution.py:445
  168.9 1.3 fusion
  (68 shorter events, 12.2 us)
Async XLA Ops:
  0.6 1.2 copy-start
  1.9 5.6 %copy-start.12 = (bf16[4096,128]{1,0:T(8,128)(2,1)S(1)}, bf16[4096,128]{1,0:T(8,128)(2,1)}, u32[]{:S(2)}) copy-start(bf16[4096,128]{1,0:T(8,128)(2,1)} %param.16) | copy-start | bytes 3145732
  4.2 5.7 %collective-permute-start = (bf16[2,2048,128]{2,1,0:T(8,128)(2,1)}, bf16[2,2048,128]{2,1,0:T(8,128)(2,1)S(1)}, u32[]{:S(2)}, u32[]{:S(2)}) collective-permute-start(bf16[2,2048,128]{2,1,0:T(8,128)(2,1)} %pad_maximum_fusion), channel_id=1, source_target_pairs={{0,1},{1,0},{2,3},{3,2},{4,5},{5,4},{6,7},{7,6},{8,9},{9,8},{10,11... | collective-permute-start | bytes 3145736 | tf_op jit(solution)/shard_map/ppermute | solution.py:376
  7.4 32.4 %collective-permute-start.4 = (bf16[2,2048,128]{2,1,0:T(8,128)(2,1)}, bf16[2,2048,128]{2,1,0:T(8,128)(2,1)}, u32[]{:S(2)}, u32[]{:S(2)}) collective-permute-start(bf16[2,2048,128]{2,1,0:T(8,128)(2,1)} %pad_maximum_fusion), channel_id=1, source_target_pairs={{0,3},{1,2},{2,5},{3,4},{4,7},{5,6},{6,9},{7,8},{8,11},{9,10},{10,... | collective-permute-start | bytes 3145736 | tf_op jit(solution)/shard_map/ppermute | solution.py:351
  9.9 1.7 copy-start.14
  9.9 13.9 %copy-start.5 = (bf16[4096,128]{1,0:T(8,128)(2,1)S(1)}, bf16[4096,128]{1,0:T(8,128)(2,1)}, u32[]{:S(2)}) copy-start(bf16[4096,128]{1,0:T(8,128)(2,1)} %param.20) | copy-start | bytes 3145732
  9.9 14.0 %copy-start.4 = (bf16[4096,128]{1,0:T(8,128)(2,1)S(1)}, bf16[4096,128]{1,0:T(8,128)(2,1)}, u32[]{:S(2)}) copy-start(bf16[4096,128]{1,0:T(8,128)(2,1)} %param.15) | copy-start | bytes 3145732
  10.9 13.2 %copy-start.3 = (bf16[2,2048,128]{2,1,0:T(8,128)(2,1)}, bf16[2,2048,128]{2,1,0:T(8,128)(2,1)S(1)}, u32[]{:S(2)}) copy-start(bf16[2,2048,128]{2,1,0:T(8,128)(2,1)S(1)} %get-tuple-element.60.own) | copy-start | bytes 3145732
  11.6 4.9 %collective-permute-start.1 = (f32[1,3]{1,0:T(1,128)S(1)}, f32[1,3]{1,0:T(1,128)S(1)}, u32[]{:S(2)}, u32[]{:S(2)}) collective-permute-start(f32[1,3]{1,0:T(1,128)S(1)} %convert_element_type.59), channel_id=1, source_target_pairs={{0,1},{1,0},{2,3},{3,2},{4,5},{5,4},{6,7},{7,6},{8,9},{9,8},{10,11... | collective-permute-start | bytes 44 | tf_op jit(solution)/shard_map/ppermute | solution.py:376
  12.1 50.0 %collective-permute-start.3 = (bf16[2,2048,128]{2,1,0:T(8,128)(2,1)S(1)}, bf16[2,2048,128]{2,1,0:T(8,128)(2,1)S(1)}, u32[]{:S(2)}, u32[]{:S(2)}) collective-permute-start(bf16[2,2048,128]{2,1,0:T(8,128)(2,1)S(1)} %get-tuple-element.60.own), channel_id=1, source_target_pairs={{0,2},{1,3},{2,4},{3,5},{4,6},{5,7},{6,8},{7,9},{8,10},{9,11},{10,... | collective-permute-start | bytes 3145736 | tf_op jit(solution)/shard_map/ppermute | solution.py:351
  12.1 24.7 %collective-permute-start.5 = (bf16[2,2048,128]{2,1,0:T(8,128)(2,1)S(1)}, bf16[2,2048,128]{2,1,0:T(8,128)(2,1)}, u32[]{:S(2)}, u32[]{:S(2)}) collective-permute-start(bf16[2,2048,128]{2,1,0:T(8,128)(2,1)S(1)} %get-tuple-element.27), channel_id=1, source_target_pairs={{0,6},{2,0},{4,2},{6,4},{1,7},{3,1},{5,3},{7,5},{8,14},{10,8},{12,... | collective-permute-start | bytes 3145736 | tf_op jit(solution)/shard_map/ppermute | solution.py:369
  23.8 15.7 %copy-start.10 = (bf16[16,32768]{1,0:T(8,128)(2,1)S(1)}, bf16[16,32768]{1,0:T(8,128)(2,1)}, u32[]{:S(2)}) copy-start(bf16[16,32768]{1,0:T(8,128)(2,1)} %param.22) | copy-start | bytes 3145732
  24.0 40.0 %collective-permute-start.2 = (bf16[2,2048,128]{2,1,0:T(8,128)(2,1)S(1)}, bf16[2,2048,128]{2,1,0:T(8,128)(2,1)S(1)}, u32[]{:S(2)}, u32[]{:S(2)}) collective-permute-start(bf16[2,2048,128]{2,1,0:T(8,128)(2,1)S(1)} %pad_maximum_fusion.2), channel_id=1, source_target_pairs={{0,1},{1,0},{2,3},{3,2},{4,5},{5,4},{6,7},{7,6},{8,9},{9,8},{10,11... | collective-permute-start | bytes 3145736 | tf_op jit(solution)/shard_map/ppermute | solution.py:376
  36.8 33.4 %collective-permute-start.6 = (bf16[2,2048,128]{2,1,0:T(8,128)(2,1)}, bf16[2,2048,128]{2,1,0:T(8,128)(2,1)}, u32[]{:S(2)}, u32[]{:S(2)}) collective-permute-start(bf16[2,2048,128]{2,1,0:T(8,128)(2,1)} %collective-permute-done.5), channel_id=1, source_target_pairs={{6,4},{7,5},{0,6},{1,7},{2,8},{3,9},{4,10},{5,11},{14,12},{15,13},... | collective-permute-start | bytes 3145736 | tf_op jit(solution)/shard_map/ppermute | solution.py:370
  62.1 1.9 %copy-start.6 = (bf16[2,2048,128]{2,1,0:T(8,128)(2,1)}, bf16[2,2048,128]{2,1,0:T(8,128)(2,1)S(1)}, u32[]{:S(2)}) copy-start(bf16[2,2048,128]{2,1,0:T(8,128)(2,1)S(1)} %collective-permute-done.3.near) | copy-start | bytes 3145732
  62.1 16.2 %collective-permute-start.8 = (bf16[16,256,128]{2,1,0:T(8,128)(2,1)S(1)}, bf16[16,256,128]{2,1,0:T(8,128)(2,1)}, u32[]{:S(2)}, u32[]{:S(2)}) collective-permute-start(bf16[16,256,128]{2,1,0:T(8,128)(2,1)S(1)} %bitcast.83), channel_id=1, source_target_pairs={{1,32},{3,34},{5,36},{7,38},{9,40},{11,42},{13,44},{15,46},{17,48}... | collective-permute-start | bytes 3145736 | tf_op jit(solution)/shard_map/ppermute | solution.py:423
  64.0 1.0 copy-start.1
  78.3 36.7 %all-to-all-start = ((bf16[128,2,16,128]{3,2,1,0:T(8,128)(2,1)}), bf16[128,2,16,128]{3,2,1,0:T(8,128)(2,1)S(1)}, u32[]{:S(2)}, u32[]{:S(2)}) async-start(bf16[128,2,16,128]{3,2,1,0:T(8,128)(2,1)} %get-tuple-element.42), calls=%async_computation | async-start | bytes 2097152 | tf_op jit(solution)/shard_map/all_to_all | solution.py:433
  115.0 1.0 copy-start.11
  128.4 9.1 %copy-start.7 = (bf16[2048,128]{1,0:T(8,128)(2,1)S(1)}, bf16[2048,128]{1,0:T(8,128)(2,1)}, u32[]{:S(2)}) copy-start(bf16[2048,128]{1,0:T(8,128)(2,1)} %get-tuple-element.39) | copy-start | bytes 1572868
  128.4 9.2 %copy-start.8 = (bf16[2048,128]{1,0:T(8,128)(2,1)S(1)}, bf16[2048,128]{1,0:T(8,128)(2,1)}, u32[]{:S(2)}) copy-start(bf16[2048,128]{1,0:T(8,128)(2,1)} %get-tuple-element.38) | copy-start | bytes 1572868
  128.4 40.5 %all-to-all-start.1 = ((bf16[256,16,128]{2,1,0:T(8,128)(2,1)}), bf16[256,16,128]{2,1,0:T(8,128)(2,1)S(1)}, u32[]{:S(2)}, u32[]{:S(2)}) async-start(bf16[256,16,128]{2,1,0:T(8,128)(2,1)} %convolve.1), calls=%async_computation.1 | async-start | bytes 2097152 | tf_op jit(solution)/shard_map/all_to_all | solution.py:445
  137.7 3.9 %collective-permute-start.7 = (bf16[2048,128]{1,0:T(8,128)(2,1)S(1)}, bf16[2048,128]{1,0:T(8,128)(2,1)S(1)}, u32[]{:S(2)}, u32[]{:S(2)}) collective-permute-start(bf16[2048,128]{1,0:T(8,128)(2,1)S(1)} %broadcast_select_fusion.4), channel_id=1, source_target_pairs={{0,1},{1,0},{2,3},{3,2},{4,5},{5,4},{6,7},{7,6},{8,9},{9,8},{10,11... | collective-permute-start | bytes 1572872 | tf_op jit(solution)/shard_map/ppermute | solution.py:376
  141.7 27.3 %copy-start.9 = (bf16[4096,128]{1,0:T(8,128)(2,1)S(1)}, bf16[4096,128]{1,0:T(8,128)(2,1)}, u32[]{:S(2)}) copy-start(bf16[4096,128]{1,0:T(8,128)(2,1)} %param.21) | copy-start | bytes 3145732
  (2 other events, 1.9 us)

commit v6 on v5

--- a/solution.py
+++ b/solution.py
@@ -18,7 +18,7 @@
 STEPS = 4
 MASKED = -1e30
 VMEM_LIMIT = 48 * 1024 * 1024
-HBM_ONLY = 60 * 1024 * 1024
+HBM_ONLY = 63 * 1024 * 1024
 
 
 def hi_lo(table):

time: 171 us -> 170 us (level)
  waiting for transfers between devices: 85.3 us -> 80.9 us
  starting transfers between devices: 30.7 us -> 34.2 us
    dynamic_slice x6, local copies, waits for them, and re-layouts: 1.37 us -> 4.42 us  [pick_heads(): lax.dynamic_index_in_dim(pair, which, 1, keepdims=False).reshape(-1, tokens)]
    ppermute x2, waiting for transfers between devices: 22.3 us -> 19.9 us  [send(): lax.ppermute(value, ALL, [(source, target(source) % count) for source in...]
    ppermute x4, waiting for transfers between devices: 3.91 us -> 1.63 us  [to_sibling(): return lax.ppermute(value, 'c', [(0, 1), (1, 0)])]
    unnamed x31 -> x25, local copies, waits for them, and re-layouts: 4.18 us -> 2.06 us
  transfers between devices with their start and end apart: 11 -> 11, of which waited for: 8 -> 7; matrix products, arithmetic and copies ran while one was open for 9% -> 11% of each run, Pallas kernels for 11% -> 11%
where the time goes in v6:
time: 170 us; the launch traced here: 169 us
  waiting for transfers between devices  80.9 us (48%)
  starting transfers between devices  34.2 us (20%)
  Pallas kernels  31 us (18%)
  other arithmetic  13.1 us (8%)
  local copies, waits for them, and re-layouts  9.07 us (5%)
    all_to_all x1, waiting for transfers between devices, body(): lax.all_to_all(conv_out, OWNERS, split_axis=0, concat_axis=0, tiled=True)  26.1 us
    ppermute x2, waiting for transfers between devices, send(): lax.ppermute(value, ALL, [(source, target(source) % count) for source in...  19.9 us
    all_to_all x1, waiting for transfers between devices, body(): lax.all_to_all(gated, CHIPS, split_axis=0, concat_axis=0, tiled=True)  17.9 us
    pallas_call x1, Pallas kernels, convolve(): pl.pallas_call(conv_kernel, grid=(channels // step_channels,), in_specs=[...  12.4 us
    ppermute x1, waiting for transfers between devices, second_next_chip(): value = lax.ppermute(value, 'y', [(y, (y - 1) % ring) for y in range(ring)])  11.5 us
    pallas_call x2, Pallas kernels, attend(): pl.pallas_call(functools.partial(attend_kernel, parity), grid_spec=pltpu....  10.5 us
    all_to_all x1, starting transfers between devices, body(): lax.all_to_all(gated, CHIPS, split_axis=0, concat_axis=0, tiled=True)  9.72 us
    all_to_all x1, starting transfers between devices, body(): lax.all_to_all(conv_out, OWNERS, split_axis=0, concat_axis=0, tiled=True)  9.07 us
  transfers between devices with their start and end apart: 11, of which 7 were waited for; matrix products, arithmetic and copies ran while one was open for 11% of the time, Pallas kernels for 11%

profile of v6, /device:TPU:1, one launch (start us, length us, event | category | flops | bytes accessed | tf_op | source)
XLA Modules:
  0.0 169.2 jit_solution(13635590933771823763)
XLA Ops:
  2.9 3.3 %collective-permute-start = (bf16[2,2048,128]{2,1,0:T(8,128)(2,1)S(1)}, bf16[2,2048,128]{2,1,0:T(8,128)(2,1)S(1)}, u32[]{:S(2)}, u32[]{:S(2)}) collective-permute-start(bf16[2,2048,128]{2,1,0:T(8,128)(2,1)S(1)} %pad_maximum_fusion), channel_id=1, source_target_pairs={{0,1},{1,0},{2,3},{3,2},{4,5},{5,4},{6,7},{7,6},{8,9},{9,8},{10,11... | collective-permute-start | bytes 3145736 | tf_op jit(solution)/shard_map/ppermute | solution.py:376
  11.6 2.3 %collective-permute-start.5 = (bf16[2,2048,128]{2,1,0:T(8,128)(2,1)S(1)}, bf16[2,2048,128]{2,1,0:T(8,128)(2,1)}, u32[]{:S(2)}, u32[]{:S(2)}) collective-permute-start(bf16[2,2048,128]{2,1,0:T(8,128)(2,1)S(1)} %get-tuple-element.27), channel_id=1, source_target_pairs={{0,6},{2,0},{4,2},{6,4},{1,7},{3,1},{5,3},{7,5},{8,14},{10,8},{12,... | collective-permute-start | bytes 3145736 | tf_op jit(solution)/shard_map/ppermute | solution.py:369
  13.9 2.6 %fusion.11 = (s32[128]{0:T(128)S(1)}, s32[128]{0:T(128)S(1)}) fusion(s32[]{:T(128)} %get-tuple-element.52, s32[]{:T(128)} %get-tuple-element.51, s32[]{:T(128)} %get-tuple-element.53, s32[]{:T(128)} %get-tuple-element.50), kind=kLoop, calls=%fused_computation.65 | loop fusion | flops 768 | bytes 1040 | tf_op jit(solution)/shard_map/add | solution.py:330
  17.8 1.8 %compare_and_fusion.1 = (pred[4]{0:T(512)(128)(4,1)S(1)}, s32[4]{0:T(128)S(1)}) fusion(s32[]{:T(128)} %bitcast.16, s32[]{:T(128)} %bitcast.15, s32[]{:T(128)} %bitcast.14, s32[]{:T(128)} %mul.22, s32[1]{0:T(128)} %bitcast.4, s32[1]{0:T(128)} %bitcast.3, s32[1]{0:T(128)} %bitcast.2, s32[1]{0:T(128)} %bitcast.1), kind=kLoop, calls=%fused_computation.40 | loop fusion | flops 52 | bytes 52 | tf_op jit(solution)/shard_map/and | solution.py:338
  19.6 2.1 %compare_and_fusion = (pred[4]{0:T(512)(128)(4,1)S(1)}, s32[4]{0:T(128)S(1)}, pred[4]{0:T(512)(128)(4,1)S(1)}) fusion(s32[]{:T(128)} %bitcast.25, s32[]{:T(128)} %bitcast.24, s32[]{:T(128)} %bitcast.23, s32[]{:T(128)S(6)} %add.108, s32[1]{0:T(128)} %bitcast.21, s32[1]{0:T(128)} %bitcast.20, s32[1]{0:T(128)} %bitcast.2, s32[1]{0:T(128)} %bitcast.1, ...), kind=kLoop, calls=%fused_computation.33 | loop fusion | flops 60 | bytes 76 | tf_op jit(solution)/shard_map/and | solution.py:338
  22.3 1.3 fusion.6
  24.6 11.5 %collective-permute-done.5 = bf16[2,2048,128]{2,1,0:T(8,128)(2,1)} collective-permute-done((bf16[2,2048,128]{2,1,0:T(8,128)(2,1)S(1)}, bf16[2,2048,128]{2,1,0:T(8,128)(2,1)}, u32[]{:S(2)}, u32[]{:S(2)}) %collective-permute-start.5) | collective-permute-done | bytes 1048608 | tf_op jit(solution)/shard_map/ppermute | solution.py:369
  36.1 3.5 %collective-permute-start.6 = (bf16[2,2048,128]{2,1,0:T(8,128)(2,1)}, bf16[2,2048,128]{2,1,0:T(8,128)(2,1)}, u32[]{:S(2)}, u32[]{:S(2)}) collective-permute-start(bf16[2,2048,128]{2,1,0:T(8,128)(2,1)} %collective-permute-done.5), channel_id=1, source_target_pairs={{6,4},{7,5},{0,6},{1,7},{2,8},{3,9},{4,10},{5,11},{14,12},{15,13},... | collective-permute-start | bytes 3145736 | tf_op jit(solution)/shard_map/ppermute | solution.py:370
  39.6 1.2 copy.38
  40.8 19.9 %collective-permute-done.3.near = bf16[2,2048,128]{2,1,0:T(8,128)(2,1)S(1)} collective-permute-done((bf16[2,2048,128]{2,1,0:T(8,128)(2,1)S(1)}, bf16[2,2048,128]{2,1,0:T(8,128)(2,1)S(1)}, u32[]{:S(2)}, u32[]{:S(2)}) %collective-permute-start.3) | collective-permute-done | bytes 1048608 | tf_op jit(solution)/shard_map/ppermute | solution.py:351
  60.7 1.9 %collective-permute-start.8 = (bf16[16,256,128]{2,1,0:T(8,128)(2,1)}, bf16[16,256,128]{2,1,0:T(8,128)(2,1)}, u32[]{:S(2)}, u32[]{:S(2)}) collective-permute-start(bf16[16,256,128]{2,1,0:T(8,128)(2,1)} %bitcast.53), channel_id=1, source_target_pairs={{1,32},{3,34},{5,36},{7,38},{9,40},{11,42},{13,44},{15,46},{17,48}... | collective-permute-start | bytes 3145736 | tf_op jit(solution)/shard_map/ppermute | solution.py:423
  62.6 5.2 %attend_second.1 = (bf16[2048,128]{1,0:T(8,128)(2,1)}, bf16[128,2,16,128]{3,2,1,0:T(8,128)(2,1)}) custom-call(s32[1]{0:T(128)} %bitcast.core_ref, f32[512,128]{1,0:T(8,128)} %get-tuple-element.36.bias_ref, bf16[4,2,512,128]{3,2,1,0:T(8,128)(2,1)} %bitcast.75, bf16[4,2,512,128]{3,2,1,0:T(8,128)(2,1)} %bitcast.78, ...), custom_call_target="tpu_custom_call" | custom-call | flops 536870912 | bytes 8650752 | tf_op jit(solution)/shard_map/attend_second/pallas_call | solution.py:292
  67.8 5.4 %attend_first.1 = (bf16[2048,128]{1,0:T(8,128)(2,1)}, bf16[128,2,16,128]{3,2,1,0:T(8,128)(2,1)}) custom-call(s32[1]{0:T(128)} %bitcast.core_ref, f32[512,128]{1,0:T(8,128)} %get-tuple-element.30.bias_ref, bf16[4,2,512,128]{3,2,1,0:T(8,128)(2,1)} %bitcast.76, bf16[4,2,512,128]{3,2,1,0:T(8,128)(2,1)} %bitcast.79, ...), custom_call_target="tpu_custom_call", output_to_operand_aliasing={{1}: (11, {})} | custom-call | flops 536870912 | bytes 8650752 | tf_op jit(solution)/shard_map/attend_first/pallas_call | solution.py:292
  73.1 4.0 %collective-permute-done.8 = bf16[16,256,128]{2,1,0:T(8,128)(2,1)} collective-permute-done((bf16[16,256,128]{2,1,0:T(8,128)(2,1)}, bf16[16,256,128]{2,1,0:T(8,128)(2,1)}, u32[]{:S(2)}, u32[]{:S(2)}) %collective-permute-start.8) | collective-permute-done | bytes 1048608 | tf_op jit(solution)/shard_map/ppermute | solution.py:423
  77.1 9.7 %all-to-all-start = ((bf16[128,2,16,128]{3,2,1,0:T(8,128)(2,1)}), bf16[128,2,16,128]{3,2,1,0:T(8,128)(2,1)}, u32[]{:S(2)}, u32[]{:S(2)}) async-start(bf16[128,2,16,128]{3,2,1,0:T(8,128)(2,1)} %get-tuple-element.42), calls=%async_computation | async-start | bytes 2097152 | tf_op jit(solution)/shard_map/all_to_all | solution.py:433
  86.8 2.3 %broadcast_select_fusion.filter_ref = bf16[16,256,128]{2,1,0:T(8,128)(2,1)} fusion(bf16[16,256,128]{2,1,0:T(8,128)(2,1)} %bitcast.53, bf16[16,256,128]{2,1,0:T(8,128)(2,1)} %collective-permute-done.8, pred[]{:T(512)S(6)} %eq.186), kind=kLoop, calls=%fused_computation.6 | loop fusion | flops 524288 | bytes 3145729 | tf_op jit(solution)/shard_map/jit(_where)/select_n | solution.py:431
  89.1 8.0 %filter_spectrum.1.spectrum_ref = f32[4096,256]{1,0:T(8,128)} custom-call(bf16[16,256,128]{2,1,0:T(8,128)(2,1)} %broadcast_select_fusion.filter_ref, bf16[512,512]{1,0:T(8,128)(2,1)} %constant.84.clone.rest_0_, f32[256,128]{1,0:T(8,128)} %constant.85.clone.rest_1_, f32[256,128]{1,0:T(8,128)} %constant.86.clone.rest_2_, bf16[768,256]{1,0:T(8,128)(2,1)} %constant.87.clone.rest_3_), custom_call_target="tpu_custom_call" | custom-call | flops 2720000000 | bytes 6291456 | tf_op jit(solution)/shard_map/filter_spectrum/pallas_call | solution.py:176
  97.2 17.9 %all-to-all-done = bf16[128,2,16,128]{3,2,1,0:T(8,128)(2,1)} async-done(((bf16[128,2,16,128]{3,2,1,0:T(8,128)(2,1)}), bf16[128,2,16,128]{3,2,1,0:T(8,128)(2,1)}, u32[]{:S(2)}, u32[]{:S(2)}) %all-to-all-start) | async-done | bytes 1048608 | tf_op jit(solution)/shard_map/all_to_all | solution.py:433
  115.0 12.4 %convolve.1 = bf16[256,16,128]{2,1,0:T(8,128)(2,1)} custom-call(bf16[256,16,128]{2,1,0:T(8,128)(2,1)} %bitcast.37.signal_ref, f32[4096,256]{1,0:T(8,128)} %filter_spectrum.1.spectrum_ref, bf16[512,512]{1,0:T(8,128)(2,1)} %constant.88.clone.rest_0_, f32[256,128]{1,0:T(8,128)} %constant.85.clone.rest_1_, f32[256,128]{1,0:T(8,128)} %constant.86.clone.rest_2_, ...), custom_call_target="tpu_custom_call" | custom-call | flops 5920000000 | bytes 8388608 | tf_op jit(solution)/shard_map/convolve/pallas_call | solution.py:195
  127.5 9.1 %all-to-all-start.1 = ((bf16[256,16,128]{2,1,0:T(8,128)(2,1)}), bf16[256,16,128]{2,1,0:T(8,128)(2,1)S(1)}, u32[]{:S(2)}, u32[]{:S(2)}) async-start(bf16[256,16,128]{2,1,0:T(8,128)(2,1)} %convolve.1), calls=%async_computation.1 | async-start | bytes 2097152 | tf_op jit(solution)/shard_map/all_to_all | solution.py:445
  136.6 2.4 %collective-permute-start.7 = (bf16[2048,128]{1,0:T(8,128)(2,1)S(1)}, bf16[2048,128]{1,0:T(8,128)(2,1)S(1)}, u32[]{:S(2)}, u32[]{:S(2)}) collective-permute-start(bf16[2048,128]{1,0:T(8,128)(2,1)S(1)} %broadcast_select_fusion.4), channel_id=1, source_target_pairs={{0,1},{1,0},{2,3},{3,2},{4,5},{5,4},{6,7},{7,6},{8,9},{9,8},{10,11... | collective-permute-start | bytes 1572872 | tf_op jit(solution)/shard_map/ppermute | solution.py:376
  139.0 1.5 collective-permute-done.7
  141.8 26.1 %all-to-all-done.1 = bf16[256,16,128]{2,1,0:T(8,128)(2,1)S(1)} async-done(((bf16[256,16,128]{2,1,0:T(8,128)(2,1)}), bf16[256,16,128]{2,1,0:T(8,128)(2,1)S(1)}, u32[]{:S(2)}, u32[]{:S(2)}) %all-to-all-start.1) | async-done | bytes 1048608 | tf_op jit(solution)/shard_map/all_to_all | solution.py:445
  167.9 1.3 fusion
  (62 shorter events, 11.7 us)
Async XLA Ops:
  2.9 5.6 %collective-permute-start = (bf16[2,2048,128]{2,1,0:T(8,128)(2,1)S(1)}, bf16[2,2048,128]{2,1,0:T(8,128)(2,1)S(1)}, u32[]{:S(2)}, u32[]{:S(2)}) collective-permute-start(bf16[2,2048,128]{2,1,0:T(8,128)(2,1)S(1)} %pad_maximum_fusion), channel_id=1, source_target_pairs={{0,1},{1,0},{2,3},{3,2},{4,5},{5,4},{6,7},{7,6},{8,9},{9,8},{10,11... | collective-permute-start | bytes 3145736 | tf_op jit(solution)/shard_map/ppermute | solution.py:376
  6.3 34.5 %collective-permute-start.4 = (bf16[2,2048,128]{2,1,0:T(8,128)(2,1)S(1)}, bf16[2,2048,128]{2,1,0:T(8,128)(2,1)S(1)}, u32[]{:S(2)}, u32[]{:S(2)}) collective-permute-start(bf16[2,2048,128]{2,1,0:T(8,128)(2,1)S(1)} %pad_maximum_fusion), channel_id=1, source_target_pairs={{0,3},{1,2},{2,5},{3,4},{4,7},{5,6},{6,9},{7,8},{8,11},{9,10},{10,... | collective-permute-start | bytes 3145736 | tf_op jit(solution)/shard_map/ppermute | solution.py:351
  8.5 1.0 copy-start
  8.5 1.0 copy-start.10
  8.5 1.7 %copy-start.11 = (s32[1,3]{1,0:T(1,128)S(1)}, s32[1,3]{1,0:T(1,128)}, u32[]{:S(2)}) copy-start(s32[1,3]{1,0:T(1,128)} %param.19) | copy-start | bytes 40
  8.5 15.1 %copy-start.3 = (bf16[4096,128]{1,0:T(8,128)(2,1)S(1)}, bf16[4096,128]{1,0:T(8,128)(2,1)}, u32[]{:S(2)}) copy-start(bf16[4096,128]{1,0:T(8,128)(2,1)} %param.20) | copy-start | bytes 3145732
  8.6 15.1 %copy-start.2 = (bf16[4096,128]{1,0:T(8,128)(2,1)S(1)}, bf16[4096,128]{1,0:T(8,128)(2,1)}, u32[]{:S(2)}) copy-start(bf16[4096,128]{1,0:T(8,128)(2,1)} %param.15) | copy-start | bytes 3145732
  9.5 14.3 %copy-start.1 = (bf16[2,2048,128]{2,1,0:T(8,128)(2,1)}, bf16[2,2048,128]{2,1,0:T(8,128)(2,1)S(1)}, u32[]{:S(2)}) copy-start(bf16[2,2048,128]{2,1,0:T(8,128)(2,1)S(1)} %get-tuple-element.60.own) | copy-start | bytes 3145732
  10.3 6.2 %collective-permute-start.1 = (f32[1,3]{1,0:T(1,128)S(1)}, f32[1,3]{1,0:T(1,128)S(1)}, u32[]{:S(2)}, u32[]{:S(2)}) collective-permute-start(f32[1,3]{1,0:T(1,128)S(1)} %convert_element_type.59), channel_id=1, source_target_pairs={{0,1},{1,0},{2,3},{3,2},{4,5},{5,4},{6,7},{7,6},{8,9},{9,8},{10,11... | collective-permute-start | bytes 44 | tf_op jit(solution)/shard_map/ppermute | solution.py:376
  10.7 49.9 %collective-permute-start.3 = (bf16[2,2048,128]{2,1,0:T(8,128)(2,1)S(1)}, bf16[2,2048,128]{2,1,0:T(8,128)(2,1)S(1)}, u32[]{:S(2)}, u32[]{:S(2)}) collective-permute-start(bf16[2,2048,128]{2,1,0:T(8,128)(2,1)S(1)} %get-tuple-element.60.own), channel_id=1, source_target_pairs={{0,2},{1,3},{2,4},{3,5},{4,6},{5,7},{6,8},{7,9},{8,10},{9,11},{10,... | collective-permute-start | bytes 3145736 | tf_op jit(solution)/shard_map/ppermute | solution.py:351
  11.6 24.5 %collective-permute-start.5 = (bf16[2,2048,128]{2,1,0:T(8,128)(2,1)S(1)}, bf16[2,2048,128]{2,1,0:T(8,128)(2,1)}, u32[]{:S(2)}, u32[]{:S(2)}) collective-permute-start(bf16[2,2048,128]{2,1,0:T(8,128)(2,1)S(1)} %get-tuple-element.27), channel_id=1, source_target_pairs={{0,6},{2,0},{4,2},{6,4},{1,7},{3,1},{5,3},{7,5},{8,14},{10,8},{12,... | collective-permute-start | bytes 3145736 | tf_op jit(solution)/shard_map/ppermute | solution.py:369
  23.6 15.9 %copy-start.9 = (bf16[16,32768]{1,0:T(8,128)(2,1)S(1)}, bf16[16,32768]{1,0:T(8,128)(2,1)}, u32[]{:S(2)}) copy-start(bf16[16,32768]{1,0:T(8,128)(2,1)} %param.22) | copy-start | bytes 3145732
  23.9 38.7 %collective-permute-start.2 = (bf16[2,2048,128]{2,1,0:T(8,128)(2,1)S(1)}, bf16[2,2048,128]{2,1,0:T(8,128)(2,1)}, u32[]{:S(2)}, u32[]{:S(2)}) collective-permute-start(bf16[2,2048,128]{2,1,0:T(8,128)(2,1)S(1)} %pad_maximum_fusion.2), channel_id=1, source_target_pairs={{0,1},{1,0},{2,3},{3,2},{4,5},{5,4},{6,7},{7,6},{8,9},{9,8},{10,11... | collective-permute-start | bytes 3145736 | tf_op jit(solution)/shard_map/ppermute | solution.py:376
  36.1 31.7 %collective-permute-start.6 = (bf16[2,2048,128]{2,1,0:T(8,128)(2,1)}, bf16[2,2048,128]{2,1,0:T(8,128)(2,1)}, u32[]{:S(2)}, u32[]{:S(2)}) collective-permute-start(bf16[2,2048,128]{2,1,0:T(8,128)(2,1)} %collective-permute-done.5), channel_id=1, source_target_pairs={{6,4},{7,5},{0,6},{1,7},{2,8},{3,9},{4,10},{5,11},{14,12},{15,13},... | collective-permute-start | bytes 3145736 | tf_op jit(solution)/shard_map/ppermute | solution.py:370
  40.8 19.9 %copy-start.4 = (bf16[2,2048,128]{2,1,0:T(8,128)(2,1)}, bf16[2,2048,128]{2,1,0:T(8,128)(2,1)S(1)}, u32[]{:S(2)}) copy-start(bf16[2,2048,128]{2,1,0:T(8,128)(2,1)S(1)} %collective-permute-done.4.crossed) | copy-start | bytes 3145732
  60.7 1.9 %copy-start.5 = (bf16[2,2048,128]{2,1,0:T(8,128)(2,1)}, bf16[2,2048,128]{2,1,0:T(8,128)(2,1)S(1)}, u32[]{:S(2)}) copy-start(bf16[2,2048,128]{2,1,0:T(8,128)(2,1)S(1)} %collective-permute-done.3.near) | copy-start | bytes 3145732
  60.7 16.4 %collective-permute-start.8 = (bf16[16,256,128]{2,1,0:T(8,128)(2,1)}, bf16[16,256,128]{2,1,0:T(8,128)(2,1)}, u32[]{:S(2)}, u32[]{:S(2)}) collective-permute-start(bf16[16,256,128]{2,1,0:T(8,128)(2,1)} %bitcast.53), channel_id=1, source_target_pairs={{1,32},{3,34},{5,36},{7,38},{9,40},{11,42},{13,44},{15,46},{17,48}... | collective-permute-start | bytes 3145736 | tf_op jit(solution)/shard_map/ppermute | solution.py:423
  77.1 38.0 %all-to-all-start = ((bf16[128,2,16,128]{3,2,1,0:T(8,128)(2,1)}), bf16[128,2,16,128]{3,2,1,0:T(8,128)(2,1)}, u32[]{:S(2)}, u32[]{:S(2)}) async-start(bf16[128,2,16,128]{3,2,1,0:T(8,128)(2,1)} %get-tuple-element.42), calls=%async_computation | async-start | bytes 2097152 | tf_op jit(solution)/shard_map/all_to_all | solution.py:433
  127.5 9.1 %copy-start.6 = (bf16[2048,128]{1,0:T(8,128)(2,1)S(1)}, bf16[2048,128]{1,0:T(8,128)(2,1)}, u32[]{:S(2)}) copy-start(bf16[2048,128]{1,0:T(8,128)(2,1)} %get-tuple-element.39) | copy-start | bytes 1572868
  127.5 9.1 %copy-start.7 = (bf16[2048,128]{1,0:T(8,128)(2,1)S(1)}, bf16[2048,128]{1,0:T(8,128)(2,1)}, u32[]{:S(2)}) copy-start(bf16[2048,128]{1,0:T(8,128)(2,1)} %get-tuple-element.38) | copy-start | bytes 1572868
  127.5 40.4 %all-to-all-start.1 = ((bf16[256,16,128]{2,1,0:T(8,128)(2,1)}), bf16[256,16,128]{2,1,0:T(8,128)(2,1)S(1)}, u32[]{:S(2)}, u32[]{:S(2)}) async-start(bf16[256,16,128]{2,1,0:T(8,128)(2,1)} %convolve.1), calls=%async_computation.1 | async-start | bytes 2097152 | tf_op jit(solution)/shard_map/all_to_all | solution.py:445
  136.6 3.9 %collective-permute-start.7 = (bf16[2048,128]{1,0:T(8,128)(2,1)S(1)}, bf16[2048,128]{1,0:T(8,128)(2,1)S(1)}, u32[]{:S(2)}, u32[]{:S(2)}) collective-permute-start(bf16[2048,128]{1,0:T(8,128)(2,1)S(1)} %broadcast_select_fusion.4), channel_id=1, source_target_pairs={{0,1},{1,0},{2,3},{3,2},{4,5},{5,4},{6,7},{7,6},{8,9},{9,8},{10,11... | collective-permute-start | bytes 1572872 | tf_op jit(solution)/shard_map/ppermute | solution.py:376
  140.7 27.3 %copy-start.8 = (bf16[4096,128]{1,0:T(8,128)(2,1)S(1)}, bf16[4096,128]{1,0:T(8,128)(2,1)}, u32[]{:S(2)}) copy-start(bf16[4096,128]{1,0:T(8,128)(2,1)} %param.21) | copy-start | bytes 3145732
